TPU v7x, 512 devices: a whole 4x4x16 slice. The times are simulated.
512 devices in a mesh: tm: 64 (over z, x), sta: 8 (over y, core).
Axes of the slice: x: 4, y: 4, z: 16, core: 2. Of those that a mesh axis runs over, the one named last changes fastest.
Arguments:
- record: bfloat16 [3, 32, 65536], P(None, 'sta', 'tm'), may hold values from -36 to 36
- templates: bfloat16 [512, 3, 4, 1536], P(('tm', 'sta')), may hold values from -18 to 18
- template_groups: int32 [512, 3], replicated, may hold values from 0 to 7, all different within a row; in each aligned block of 8 rows (0 to 7, 8 to 15, ...) at most 4 rows name the same one
Outputs:
- detection: float32 [512, 65536], P('sta', 'tm')
Inputs may be any that keep to these rules, and one draw needn't show every extreme that they name: `template_groups`: each row names 3 different station groups. Among the 8 templates of one index of tm (rows m * 8 to m * 8 + 7) no group is named by more than 4 rows, a bound that some block reaches.
All inputs are finite; a program needn't handle non-finite values.
Results may differ from a plain program's by a relative error of at most 0.0003.
Values may be sent and summed in bfloat16 or wider, within the bound.
No kernel may reach another device: no remote copies, remote signals or barrier semaphores. Data moves between devices by JAX's collectives and lax.ppermute only.
A program may use at most 64 MiB of HBM per device.

v0:
```python
import math

import jax
import jax.numpy as jnp
from jax import lax
from jax.sharding import PartitionSpec as P

L = 512


epsilon = 1e-06


def shifted(value, axis, steps):
    count = lax.axis_size(axis)
    first, last = (max(0, -steps), min(count, count - steps))
    return lax.ppermute(value, axis, [(source, source + steps) for source in range(first, last)])


def hankel_rows(series, columns):
    length = series.shape[-1]
    leading = series.shape[:-1]
    tiled = jnp.broadcast_to(series[..., None, :], leading + (L + 1, length))
    tiled = tiled.reshape(leading + ((L + 1) * length,))
    tiled = tiled[..., : L * (length + 1)].reshape(leading + (L, length + 1))
    return tiled[..., :columns]


def on_device(record, templates, template_groups):
    channels = record.shape[0]
    stations = record.shape[1]
    samples = record.shape[2]
    n_time = lax.axis_size("tm")
    n_group = lax.axis_size("sta")
    my_group = lax.axis_index("sta")
    my_row = lax.axis_index("tm")
    spread = template_groups.shape[1]
    first_samples = record[:, :, : L - 1]
    following = shifted(first_samples, "tm", -1)
    extended = jnp.concatenate([record, following], axis=2)
    squares = jnp.sum(jnp.square(extended.astype(jnp.float32)), axis=0)
    running = jnp.concatenate(
        [jnp.zeros((stations, 1), jnp.float32), jnp.cumsum(squares, axis=1)], axis=1
    )
    energy = running[:, L : L + samples] - running[:, :samples]
    data_scale = 1.0 / jnp.sqrt(energy + epsilon)
    own_index = my_row * n_group + my_group
    own_groups = lax.dynamic_index_in_dim(template_groups, own_index, 0, keepdims=False)
    target = (own_groups[:, None] == jnp.arange(n_group)[None, :]).astype(jnp.bfloat16)
    outgoing = jnp.einsum(
        "ig,isd->sgd", target, templates[0], preferred_element_type=jnp.float32
    ).astype(jnp.bfloat16)
    arriving = lax.all_to_all(outgoing, "sta", split_axis=1, concat_axis=1, tiled=True)

    def station_term(station, summed):
        block_rows = lax.dynamic_index_in_dim(arriving, station, 0, keepdims=False)
        series = lax.dynamic_index_in_dim(extended, station, 1, keepdims=False)
        windows = hankel_rows(series, samples).reshape(channels * L, samples)
        pieces = lax.all_gather(block_rows, "tm", axis=0, tiled=True)
        product = jnp.dot(pieces, windows, preferred_element_type=jnp.float32)
        weight = jnp.sum(jnp.square(pieces.astype(jnp.float32)), axis=1)
        numerator = product * (1.0 / jnp.sqrt(weight + epsilon))[:, None]
        scale_row = lax.dynamic_index_in_dim(data_scale, station, 0, keepdims=False)
        return summed + numerator * scale_row[None, :]

    rows_total = arriving.shape[1] * n_time
    summed = lax.fori_loop(0, stations, station_term, jnp.zeros((rows_total, samples), jnp.float32))
    stacked = lax.psum_scatter(summed, "sta", scatter_dimension=0, tiled=True)
    factor = math.sqrt(channels * L / (spread * stations))
    return stacked * factor


def solution(mesh):
    return jax.shard_map(
        on_device,
        mesh=mesh,
        in_specs=(P(None, "sta", "tm"), P(("tm", "sta"), None, None, None), P()),
        out_specs=P("sta", "tm"),
        check_vma=False,
    )
```

profile of v0, /device:TPU:1, one launch (start us, length us, event | category | flops | bytes accessed | tf_op | source)
XLA Modules:
  0.0 668.8 jit_solution(17506866715736663334)
XLA Ops:
  7.4 0.9 dynamic-slice_reduce_fusion
  8.2 0.3 fusion.1
  8.5 0.7 copy.9
  9.2 10.1 %all-to-all-start = ((bf16[4,8,1536]{2,0,1:T(4,128)(2,1)}), bf16[4,8,1536]{2,0,1:T(4,128)(2,1)S(1)}, u32[]{:S(2)}, u32[]{:S(2)}) async-start(bf16[4,8,1536]{2,0,1:T(4,128)(2,1)} %copy.9), calls=%async_computation | async-start | bytes 196608 | tf_op jit(solution)/shard_map/all_to_all | solution.py:53
  19.4 0.7 slice.43
  20.1 1.3 collective-permute-start
  21.4 0.8 constant_dynamic-update-slice_fusion.1
  22.2 2.6 collective-permute-done
  24.8 0.1 multiply_reduce_fusion.1
  24.9 1.2 reduce-window.6
  26.1 0.2 slice_reduce_fusion
  26.2 0.2 reduce-window.9
  26.4 0.1 add_bitcast_fusion
  26.5 0.1 fusion.5
  26.6 0.0 all-to-all-done
  26.7 585.5 %while.14 = (s32[]{:T(128)}, f32[512,1024]{1,0:T(8,128)}, bf16[4,8,1536]{2,1,0:T(8,128)(2,1)S(1)}, bf16[3,4,1535]{2,0,1:T(4,128)(2,1)S(1)}, f32[4,1024]{1,0:T(4,128)S(1)}, /*index=5*/s32[]{:T(128)}, s32[]{:T(128)}) while((s32[]{:T(128)}, f32[512,1024]{1,0:T(8,128)}, bf16[4,8,1536]{2,1,0:T(8,128)(2,1)S(1)}, ...), condition=%wide.region_5.6_spmd.clone, body=%wide.region_3.5_spmd.clone.sunk | while | flops 1615069184 | bytes 72029304 | solution.py:67
  26.7 0.0 all-gather.6.cloned.1.call-start
  26.7 0.6 constant_dynamic-slice_fusion.4
  27.4 0.1 all-gather.6.cloned.1.call-update
  27.4 2.5 broadcast_in_dim.31
  29.9 13.2 %reshape.53 = bf16[2362365]{0:T(1024)(128)(2,1)} reshape(bf16[3,513,1535]{2,1,0:T(8,128)(2,1)} %broadcast_in_dim.31) | data formatting | bytes 9449460 | tf_op jit(solution)/shard_map/while
  43.1 7.9 %reshape.54 = bf16[3,787455]{1,0:T(4,128)(2,1)} reshape(bf16[2362365]{0:T(1024)(128)(2,1)} %reshape.53) | data formatting | bytes 9449460 | tf_op jit(solution)/shard_map/while/body/eval_jaxpr/reshape | solution.py:24
  51.0 2.8 slice-done
  53.7 1.1 copy.24
  54.9 0.5 slice.59
  55.4 109.1 %all-gather.6.cloned.1.call-done = bf16[1,512,1536]{2,1,0:T(8,128)(2,1)} async-done(((bf16[1,8,1536]{2,1,0:T(8,128)(2,1)}), bf16[1,512,1536]{2,1,0:T(8,128)(2,1)}) %all-gather.6.cloned.1.call-update) | async-done | bytes 1572880 | tf_op jit(solution)/shard_map/while/body/eval_jaxpr/all_gather | solution.py:59
  164.5 1.8 multiply_reduce_fusion.3
  166.3 4.7 select_add_fusion.2
  170.9 0.6 constant_dynamic-slice_fusion.4
  171.5 0.1 all-gather.6.cloned.1.call-update
  171.7 2.5 broadcast_in_dim.31
  174.1 13.2 %reshape.53 = bf16[2362365]{0:T(1024)(128)(2,1)} reshape(bf16[3,513,1535]{2,1,0:T(8,128)(2,1)} %broadcast_in_dim.31) | data formatting | bytes 9449460 | tf_op jit(solution)/shard_map/while
  187.3 7.9 %reshape.54 = bf16[3,787455]{1,0:T(4,128)(2,1)} reshape(bf16[2362365]{0:T(1024)(128)(2,1)} %reshape.53) | data formatting | bytes 9449460 | tf_op jit(solution)/shard_map/while/body/eval_jaxpr/reshape | solution.py:24
  195.2 2.8 slice-done
  198.0 1.1 copy.24
  199.1 0.5 slice.59
  199.6 111.4 %all-gather.6.cloned.1.call-done = bf16[1,512,1536]{2,1,0:T(8,128)(2,1)} async-done(((bf16[1,8,1536]{2,1,0:T(8,128)(2,1)}), bf16[1,512,1536]{2,1,0:T(8,128)(2,1)}) %all-gather.6.cloned.1.call-update) | async-done | bytes 1572880 | tf_op jit(solution)/shard_map/while/body/eval_jaxpr/all_gather | solution.py:59
  311.0 1.8 multiply_reduce_fusion.3
  312.8 5.3 select_add_fusion.2
  318.1 0.6 constant_dynamic-slice_fusion.4
  318.7 0.1 all-gather.6.cloned.1.call-update
  318.8 2.5 broadcast_in_dim.31
  321.3 13.2 %reshape.53 = bf16[2362365]{0:T(1024)(128)(2,1)} reshape(bf16[3,513,1535]{2,1,0:T(8,128)(2,1)} %broadcast_in_dim.31) | data formatting | bytes 9449460 | tf_op jit(solution)/shard_map/while
  334.5 7.9 %reshape.54 = bf16[3,787455]{1,0:T(4,128)(2,1)} reshape(bf16[2362365]{0:T(1024)(128)(2,1)} %reshape.53) | data formatting | bytes 9449460 | tf_op jit(solution)/shard_map/while/body/eval_jaxpr/reshape | solution.py:24
  342.4 2.8 slice-done
  345.2 1.1 copy.24
  346.3 0.5 slice.59
  346.8 111.4 %all-gather.6.cloned.1.call-done = bf16[1,512,1536]{2,1,0:T(8,128)(2,1)} async-done(((bf16[1,8,1536]{2,1,0:T(8,128)(2,1)}), bf16[1,512,1536]{2,1,0:T(8,128)(2,1)}) %all-gather.6.cloned.1.call-update) | async-done | bytes 1572880 | tf_op jit(solution)/shard_map/while/body/eval_jaxpr/all_gather | solution.py:59
  458.2 1.8 multiply_reduce_fusion.3
  460.0 5.3 select_add_fusion.2
  465.3 0.6 constant_dynamic-slice_fusion.4
  465.9 0.0 all-gather.6.cloned.1.call-update
  466.0 2.5 broadcast_in_dim.31
  468.4 13.2 %reshape.53 = bf16[2362365]{0:T(1024)(128)(2,1)} reshape(bf16[3,513,1535]{2,1,0:T(8,128)(2,1)} %broadcast_in_dim.31) | data formatting | bytes 9449460 | tf_op jit(solution)/shard_map/while
  481.6 7.9 %reshape.54 = bf16[3,787455]{1,0:T(4,128)(2,1)} reshape(bf16[2362365]{0:T(1024)(128)(2,1)} %reshape.53) | data formatting | bytes 9449460 | tf_op jit(solution)/shard_map/while/body/eval_jaxpr/reshape | solution.py:24
  489.5 2.8 slice-done
  492.3 1.1 copy.24
  493.4 0.5 slice.59
  493.9 111.2 %all-gather.6.cloned.1.call-done = bf16[1,512,1536]{2,1,0:T(8,128)(2,1)} async-done(((bf16[1,8,1536]{2,1,0:T(8,128)(2,1)}), bf16[1,512,1536]{2,1,0:T(8,128)(2,1)}) %all-gather.6.cloned.1.call-update) | async-done | bytes 1572880 | tf_op jit(solution)/shard_map/while/body/eval_jaxpr/all_gather | solution.py:59
  605.1 1.8 multiply_reduce_fusion.3
  606.9 5.3 select_add_fusion.2
  612.2 0.6 reduce-scatter.2.cloned.1.call-update
  612.7 47.3 %reduce-scatter.2.cloned.1.call-done = f32[64,1024]{1,0:T(8,128)} async-done(((f32[512,1024]{1,0:T(8,128)}), f32[64,1024]{1,0:T(8,128)}) %reduce-scatter.2.cloned.1.call-update) | async-done | bytes 262160 | tf_op jit(solution)/shard_map/reduce_scatter | solution.py:68
  660.0 1.7 broadcast_multiply_fusion
  (29 shorter events, 0.2 us)
Async XLA Ops:
  7.4 0.9 copy-start
  9.2 17.4 %all-to-all-start = ((bf16[4,8,1536]{2,0,1:T(4,128)(2,1)}), bf16[4,8,1536]{2,0,1:T(4,128)(2,1)S(1)}, u32[]{:S(2)}, u32[]{:S(2)}) async-start(bf16[4,8,1536]{2,0,1:T(4,128)(2,1)} %copy.9), calls=%async_computation | async-start | bytes 196608 | tf_op jit(solution)/shard_map/all_to_all | solution.py:53
  20.1 4.7 collective-permute-start
  26.7 137.8 %all-gather.6.cloned.1.call-start = ((), (), s32[]{:S(2)}) async-start(), calls=%async_computation.3 | async-start | bytes 1597440 | tf_op jit(solution)/shard_map/while/body/eval_jaxpr/all_gather | solution.py:59
  51.0 2.8 slice-start
  170.9 140.1 %all-gather.6.cloned.1.call-start = ((), (), s32[]{:S(2)}) async-start(), calls=%async_computation.3 | async-start | bytes 1597440 | tf_op jit(solution)/shard_map/while/body/eval_jaxpr/all_gather | solution.py:59
  195.2 2.8 slice-start
  318.1 140.1 %all-gather.6.cloned.1.call-start = ((), (), s32[]{:S(2)}) async-start(), calls=%async_computation.3 | async-start | bytes 1597440 | tf_op jit(solution)/shard_map/while/body/eval_jaxpr/all_gather | solution.py:59
  342.4 2.8 slice-start
  465.3 139.8 %all-gather.6.cloned.1.call-start = ((), (), s32[]{:S(2)}) async-start(), calls=%async_computation.3 | async-start | bytes 1597440 | tf_op jit(solution)/shard_map/while/body/eval_jaxpr/all_gather | solution.py:59
  489.5 2.8 slice-start
  612.2 47.8 %reduce-scatter.2.cloned.1.call-start = ((), (), s32[]{:S(2)}) async-start(), calls=%async_computation.2 | async-start | bytes 2359296 | tf_op jit(solution)/shard_map/reduce_scatter | solution.py:68
Sparse Core Ops, SparseCore 0:
  30.5 133.9 all-gather.5
  174.7 136.2 all-gather.5
  321.9 136.2 all-gather.5
  468.8 136.2 all-gather.5
Sparse Core Ops, SparseCore 1:
  615.5 44.5 reduce-scatter.1
where the time goes:
time: 671 us; the launch traced here: 669 us
  waiting for transfers between devices  494 us (74%)
  local copies, waits for them, and re-layouts  117 us (17%)
  matrix products  20.9 us (3%)
  between operations  14.6 us (2%)
  starting transfers between devices  11.5 us (2%)
  other arithmetic  10.4 us (2%)
    all_gather x4, waiting for transfers between devices, station_term(): pieces = lax.all_gather(block_rows, 'tm', axis=0, tiled=True)  443 us
    while x8, local copies, waits for them, and re-layouts  57.3 us
    reduce_scatter x1, waiting for transfers between devices, on_device(): stacked = lax.psum_scatter(summed, 'sta', scatter_dimension=0, tiled=True)  47.3 us
    reshape x4, local copies, waits for them, and re-layouts, hankel_rows(): tiled = tiled.reshape(leading + ((L + 1) * length,))  31.5 us
    dot_general x4, matrix products, station_term(): product = jnp.dot(pieces, windows, preferred_element_type=jnp.float32)  20.6 us
  transfers between devices with their start and end apart: 7, of which 6 were waited for; matrix products, arithmetic and copies ran while one was open for 16% of the time, Pallas kernels for 0%

commit v1 on v0

v1 whole, which is shorter than its diff:
```python
import math

import jax
import jax.numpy as jnp
from jax import lax
from jax.experimental import pallas as pl
from jax.experimental.pallas import tpu as pltpu
from jax.sharding import PartitionSpec as P

L = 512
LANES = 128
HALF = 64
SPAN = L + LANES
SLOTS = 4
epsilon = 1e-06


def detect_kernel(
    factor,
    groups_ref,
    templates_ref,
    series_ref,
    out_ref,
    source,
    home,
    count,
    waves,
    norms,
    band,
    shifts,
    energy,
    windows,
    toeplitz,
    share,
    total,
    turned,
):
    group = pl.program_id(0)
    block, spread = groups_ref.shape
    stations = series_ref.shape[1] // 3
    padded = series_ref.shape[2]
    rows = total.shape[1]
    slots = templates_ref.shape[0]
    lane = lax.broadcasted_iota(jnp.int32, (1, LANES), 1)
    low = lane < HALF

    @pl.when(group == 0)
    def _():
        def clear(n, carry):
            source[n] = block * spread
            home[n] = block
            return carry

        lax.fori_loop(0, source.shape[0], clear, 0)
        for n in range(count.shape[0]):
            count[n] = 0
        for r in range(block):
            for i in range(spread):
                named = groups_ref[r, i]
                place = named * SLOTS + count[named]
                source[place] = r * spread + i
                home[place] = r
                count[named] = count[named] + 1
        waves[...] = jnp.zeros_like(waves)
        norms[...] = jnp.zeros_like(norms)
        squares = jnp.zeros((slots, 1), jnp.float32)
        for c in range(3):
            part = templates_ref[:, c * L : (c + 1) * L].astype(jnp.float32)
            waves[0:slots, c * SPAN : c * SPAN + L] = part
            squares = squares + jnp.sum(part * part, axis=1, keepdims=True)
        norms[0:slots, :] = jnp.broadcast_to(lax.rsqrt(squares + epsilon), (slots, LANES))
        r = lax.broadcasted_iota(jnp.int32, (LANES, LANES), 0)
        l = lax.broadcasted_iota(jnp.int32, (LANES, LANES), 1)
        band[0:LANES, :] = jnp.where(r >= l, 1.0, 0.0).astype(jnp.bfloat16)
        band[LANES : 2 * LANES, :] = jnp.ones((LANES, LANES), jnp.bfloat16)
        band[2 * LANES :, :] = jnp.where(r < l, 1.0, 0.0).astype(jnp.bfloat16)
        shifts[...] = jnp.zeros_like(shifts)
        total[...] = jnp.zeros_like(total)

    share[...] = jnp.zeros_like(share)

    def station_term(station, carry):
        squares = jnp.zeros((padded, LANES), jnp.float32)
        for c in range(3):
            plain = series_ref[0, c * stations + station].astype(jnp.float32)
            squares = squares + plain * plain
            shifts[c, 0, 0:padded, :] = plain
            after = shifts[c, 0, 1 : padded + 1, :]
            shifts[c, 1, 0:padded, :] = pltpu.roll(jnp.where(low, after, plain), HALF, 1)
        energy[...] = squares
        middle = energy[1 : rows + 1, :] + energy[2 : rows + 2, :] + energy[3 : rows + 3, :]
        pieces = jnp.concatenate([energy[0:rows, :], middle, energy[4 : rows + 4, :]], axis=1)
        coarse = pieces.astype(jnp.bfloat16)
        fine = (pieces - coarse.astype(jnp.float32)).astype(jnp.bfloat16)
        window_energy = jnp.dot(coarse, band[...], preferred_element_type=jnp.float32)
        window_energy += jnp.dot(fine, band[...], preferred_element_type=jnp.float32)
        scale = lax.rsqrt(window_energy + epsilon)
        scale_other = pltpu.roll(scale, HALF, 1)
        scale_first = jnp.where(low, scale, scale_other)
        scale_second = jnp.where(low, scale_other, scale)

        weight = []
        for j in range(SLOTS):
            row = source[group * SLOTS + j] * stations + station
            weight.append(norms[pl.ds(row, 1), :])
            for c in range(3):
                wave = waves[pl.ds(row, 1), c * SPAN : (c + 1) * SPAN]
                moved = pltpu.roll(
                    jnp.broadcast_to(wave, (HALF, SPAN)), 0, 1, stride=1, stride_axis=0
                )
                toeplitz[j * HALF : (j + 1) * HALF, c * SPAN : (c + 1) * SPAN] = moved.astype(
                    jnp.bfloat16
                )
        for c in range(3):
            for e in range(2):
                for v in range(SPAN // LANES):
                    at = c * SPAN + v * LANES
                    windows[e * rows : (e + 1) * rows, at : at + LANES] = shifts[
                        c, e, v : v + rows, :
                    ].astype(jnp.bfloat16)
        product = lax.dot_general(
            windows[...],
            toeplitz[...],
            (((1,), (1,)), ((), ())),
            preferred_element_type=jnp.float32,
        )
        for p in range(SLOTS // 2):
            both = jnp.where(low, weight[2 * p], weight[2 * p + 1])
            at = p * LANES
            share[0, :, at : at + LANES] += product[0:rows, at : at + LANES] * (scale_first * both)
            share[1, :, at : at + LANES] += product[rows:, at : at + LANES] * (scale_second * both)
        return carry

    lax.fori_loop(0, stations, station_term, 0)
    for j in range(SLOTS):
        at = (j // 2) * LANES
        first = share[0, :, at : at + LANES]
        second = share[1, :, at : at + LANES]
        if j % 2 == 0:
            whole = jnp.where(low, first, pltpu.roll(second, HALF, 1))
        else:
            whole = jnp.where(low, pltpu.roll(first, HALF, 1), second)
        r = home[group * SLOTS + j]
        total[r] = total[r] + whole

    @pl.when(group == pl.num_programs(0) - 1)
    def _():
        for r in range(block):
            turned[:, r, :] = total[r] * factor
        parts, _, samples = out_ref.shape
        for w in range(parts):
            for i in range(samples // LANES):
                out_ref[w, :, i * LANES : (i + 1) * LANES] = turned[w * (samples // LANES) + i]


def detect(groups, templates, series, parts, factor):
    n_group, channels, padded, _ = series.shape
    block, spread = groups.shape
    slots = templates.shape[0]
    rows = padded - 8
    samples = rows * LANES // parts
    spare = -(-(slots + 4) // 8) * 8
    body = lambda *refs: detect_kernel(factor, *refs)
    return pl.pallas_call(
        body,
        grid=(n_group,),
        out_shape=jax.ShapeDtypeStruct((parts, block, samples), jnp.float32),
        in_specs=[
            pl.BlockSpec(memory_space=pltpu.SMEM),
            pl.BlockSpec((slots, 3 * L), lambda g: (0, 0)),
            pl.BlockSpec((1, channels, padded, LANES), lambda g: (g, 0, 0, 0)),
        ],
        out_specs=pl.BlockSpec((parts, block, samples), lambda g: (0, 0, 0)),
        scratch_shapes=[
            pltpu.SMEM((n_group * SLOTS,), jnp.int32),
            pltpu.SMEM((n_group * SLOTS,), jnp.int32),
            pltpu.SMEM((n_group,), jnp.int32),
            pltpu.VMEM((spare, 3 * SPAN), jnp.float32),
            pltpu.VMEM((spare, LANES), jnp.float32),
            pltpu.VMEM((3 * LANES, LANES), jnp.bfloat16),
            pltpu.VMEM((3, 2, padded + 8, LANES), jnp.float32),
            pltpu.VMEM((padded, LANES), jnp.float32),
            pltpu.VMEM((2 * rows, 3 * SPAN), jnp.bfloat16),
            pltpu.VMEM((SLOTS * HALF, 3 * SPAN), jnp.bfloat16),
            pltpu.VMEM((2, rows, SLOTS * HALF), jnp.float32),
            pltpu.VMEM((block + 1, rows, LANES), jnp.float32),
            pltpu.VMEM((rows, block, LANES), jnp.float32),
        ],
        compiler_params=pltpu.CompilerParams(vmem_limit_bytes=32 * 1024 * 1024),
        cost_estimate=pl.CostEstimate(
            flops=2 * n_group * 4 * 2 * rows * 3 * SPAN * SLOTS * HALF,
            bytes_accessed=series.size * 2 + templates.size * 2 + 4 * block * rows * LANES,
            transcendentals=0,
        ),
    )(groups, templates, series)


def copies_to(value, axis, groups=None):
    count = len(groups[0]) if groups else lax.axis_size(axis)
    spread = jnp.broadcast_to(value[None], (count,) + value.shape)
    return lax.all_to_all(spread, axis, 0, 0, axis_index_groups=groups, tiled=True)


def on_device(record, templates, template_groups):
    channels, stations, samples = record.shape
    n_tm, n_sta = lax.axis_size("tm"), lax.axis_size("sta")
    m, s = lax.axis_index("tm"), lax.axis_index("sta")
    n_a = n_sta
    n_b = n_tm // n_a
    near = [[a * n_b + b for b in range(n_b)] for a in range(n_a)]
    far = [[a * n_b + b for a in range(n_a)] for b in range(n_b)]
    spread = template_groups.shape[1]

    turn = [
        ((a * n_b + b) * n_sta + t, (t * n_b + b) * n_sta + a)
        for a in range(n_a)
        for b in range(n_b)
        for t in range(n_sta)
    ]
    lines = templates.reshape(spread * stations, -1)
    own = lax.ppermute(lines, ("tm", "sta"), turn)
    block = copies_to(own, "tm", far)
    block = block.reshape(n_a * spread * stations, -1)
    first = (s * n_b + lax.rem(m, n_b)) * n_a
    groups = lax.dynamic_slice_in_dim(template_groups, first, n_a, 0)

    halo = lax.ppermute(record[:, :, :L], "tm", [(i + 1, i) for i in range(n_tm - 1)])
    lines = channels * stations
    steps = samples // LANES
    piece = jnp.concatenate(
        [record.reshape(lines * steps, LANES), halo.reshape(lines * (L // LANES), LANES)]
    )
    around = copies_to(piece, "tm", near)
    main = around[:, : lines * steps].reshape(n_b, lines, steps, LANES)
    main = main.transpose(1, 0, 2, 3).reshape(lines, n_b * steps, LANES)
    tail = around[-1, lines * steps :].reshape(lines, L // LANES, LANES)
    rest = jnp.zeros((lines, 8 - L // LANES, LANES), record.dtype)
    series = copies_to(jnp.concatenate([main, tail, rest], axis=1), "sta")

    factor = math.sqrt(channels * L / (spread * stations))
    found = detect(groups, block, series, n_b, factor)
    found = lax.all_to_all(found, "tm", 0, 0, axis_index_groups=near, tiled=True)
    return found.reshape(n_b * n_a, samples)


def solution(mesh):
    return jax.shard_map(
        on_device,
        mesh=mesh,
        in_specs=(P(None, "sta", "tm"), P(("tm", "sta"), None, None, None), P()),
        out_specs=P("sta", "tm"),
        check_vma=False,
    )
```

time: 671 us -> 136 us (0.20)
  waiting for transfers between devices: 494 us -> 47 us
  local copies, waits for them, and re-layouts: 117 us -> 6.32 us
  starting transfers between devices: 11.5 us -> 47 us
  Pallas kernels: 0 us -> 23.8 us
  matrix products: 20.9 us -> 0 us
  between operations: 14.6 us -> 0.06 us
  blocking collectives: 0 us -> 11.3 us
  other arithmetic: 10.4 us -> 0.12 us
    all_gather x4 -> x0, waiting for transfers between devices: 443 us -> none  [station_term(): pieces = lax.all_gather(block_rows, 'tm', axis=0, tiled=True)]
    while x8 -> x0, local copies, waits for them, and re-layouts: 57.3 us -> none
    reduce_scatter x1 -> x0, waiting for transfers between devices: 47.3 us -> none  [on_device(): stacked = lax.psum_scatter(summed, 'sta', scatter_dimension=0, tiled=True)]
    all_to_all x1 -> x3, waiting for transfers between devices: 0.01 us -> 42.3 us  [copies_to(): lax.all_to_all(spread, axis, 0, 0, axis_index_groups=groups, tiled=True)]
    reshape x4 -> x5, local copies, waits for them, and re-layouts: 31.5 us -> 1.66 us  [the longest x1 0.78 us: on_device(): lines = templates.reshape(spread * stations, -1)]
    all_to_all x1 -> x3, starting transfers between devices: 10.1 us -> 37.6 us  [copies_to(): lax.all_to_all(spread, axis, 0, 0, axis_index_groups=groups, tiled=True)]
    pallas_call x0 -> x1, Pallas kernels: none -> 23.8 us  [detect(): pl.pallas_call(body, grid=(n_group,), out_shape=jax.ShapeDtypeStruct((par...]
    dot_general x5 -> x0, matrix products: 20.9 us -> none  [the longest x4 20.6 us: station_term(): product = jnp.dot(pieces, windows, preferred_element_type=jnp.float32)]
  transfers between devices with their start and end apart: 7 -> 5, of which waited for: 6 -> 4; matrix products, arithmetic and copies ran while one was open for 16% -> 1% of each run, Pallas kernels for 0% -> 0%
where the time goes in v1:
time: 136 us
  starting transfers between devices  47 us (35%)
  waiting for transfers between devices  47 us (35%)
  Pallas kernels  23.8 us (18%)
  blocking collectives  11.3 us (8%)
  local copies, waits for them, and re-layouts  6.32 us (5%)
    all_to_all x3, waiting for transfers between devices, copies_to(): lax.all_to_all(spread, axis, 0, 0, axis_index_groups=groups, tiled=True)  42.3 us
    all_to_all x3, starting transfers between devices, copies_to(): lax.all_to_all(spread, axis, 0, 0, axis_index_groups=groups, tiled=True)  37.6 us
    pallas_call x1, Pallas kernels, detect(): pl.pallas_call(body, grid=(n_group,), out_shape=jax.ShapeDtypeStruct((par...  23.8 us
    all_to_all x1, blocking collectives, on_device(): lax.all_to_all(found, 'tm', 0, 0, axis_index_groups=near, tiled=True)  11.3 us
    ppermute x1, starting transfers between devices, on_device(): own = lax.ppermute(lines, ('tm', 'sta'), turn)  8.1 us
    broadcast_in_dim x3, local copies, waits for them, and re-layouts, copies_to(): spread = jnp.broadcast_to(value[None], (count,) + value.shape)  2.99 us
    ppermute x1, waiting for transfers between devices, on_device(): lax.ppermute(record[:, :, :L], 'tm', [(i + 1, i) for i in range(n_tm - 1)])  2.97 us
  transfers between devices with their start and end apart: 5, of which 4 were waited for; matrix products, arithmetic and copies ran while one was open for 1% of the time, Pallas kernels for 0%

profile of v1, /device:TPU:1, one launch (start us, length us, event | category | flops | bytes accessed | tf_op | source)
XLA Modules:
  0.0 135.6 jit_solution(10729015655639197807)
XLA Ops:
  0.0 0.0 copy-start
  0.0 0.7 slice.9
  0.7 1.3 collective-permute-start.1
  2.0 0.8 reshape.26
  2.8 3.0 %collective-permute-done.1 = bf16[3,4,512]{2,1,0:T(4,128)(2,1)S(1)} collective-permute-done((bf16[3,4,512]{2,1,0:T(4,128)(2,1)S(1)}, bf16[3,4,512]{2,1,0:T(4,128)(2,1)S(1)}, u32[]{:S(2)}, u32[]{:S(2)}) %collective-permute-start.1) | collective-permute-done | bytes 12320 | tf_op jit(solution)/shard_map/ppermute | solution.py:227
  5.8 0.8 broadcast_in_dim.9
  6.5 7.5 %all-to-all-start.1 = ((bf16[8,144,128]{2,1,0:T(8,128)(2,1)}), bf16[8,144,128]{2,1,0:T(8,128)(2,1)S(1)}, u32[]{:S(2)}, u32[]{:S(2)}) async-start(bf16[8,144,128]{2,1,0:T(8,128)(2,1)} %broadcast_in_dim.9), calls=%async_computation.1 | async-start | bytes 589824 | tf_op jit(solution)/shard_map/all_to_all | solution.py:201
  14.0 0.8 reshape.24
  14.8 8.1 %collective-permute-start = (bf16[12,1536]{1,0:T(8,128)(2,1)S(1)}, bf16[12,1536]{1,0:T(8,128)(2,1)S(1)}, u32[]{:S(2)}, u32[]{:S(2)}) collective-permute-start(bf16[12,1536]{1,0:T(8,128)(2,1)S(1)} %reshape.24), channel_id=1, source_target_pairs={{0,0},{1,64},{2,128},{3,192},{4,256},{5,320},{6,384},{7,448},{8,8}... | collective-permute-start | bytes 110600 | tf_op jit(solution)/shard_map/ppermute | solution.py:221
  22.9 1.8 %collective-permute-done = bf16[12,1536]{1,0:T(8,128)(2,1)S(1)} collective-permute-done((bf16[12,1536]{1,0:T(8,128)(2,1)S(1)}, bf16[12,1536]{1,0:T(8,128)(2,1)S(1)}, u32[]{:S(2)}, u32[]{:S(2)}) %collective-permute-start) | collective-permute-done | bytes 36896 | tf_op jit(solution)/shard_map/ppermute | solution.py:221
  24.6 0.0 all-to-all-done.1
  24.6 0.8 broadcast_in_dim.8
  25.4 20.8 %all-to-all-start = ((bf16[8,12,1536]{2,1,0:T(8,128)(2,1)}), bf16[8,12,1536]{2,1,0:T(8,128)(2,1)S(1)}, u32[]{:S(2)}, u32[]{:S(2)}) async-start(bf16[8,12,1536]{2,1,0:T(8,128)(2,1)} %broadcast_in_dim.8), calls=%async_computation | async-start | bytes 786432 | tf_op jit(solution)/shard_map/all_to_all | solution.py:201
  46.2 0.1 pad.2.clone
  46.3 0.1 maximum_maximum_fusion
  46.5 19.6 %all-to-all-done = bf16[8,12,1536]{2,1,0:T(8,128)(2,1)S(1)} async-done(((bf16[8,12,1536]{2,1,0:T(8,128)(2,1)}), bf16[8,12,1536]{2,1,0:T(8,128)(2,1)S(1)}, u32[]{:S(2)}, u32[]{:S(2)}) %all-to-all-start) | async-done | bytes 294944 | tf_op jit(solution)/shard_map/all_to_all | solution.py:201
  66.1 1.5 %broadcast_in_dim.11 = bf16[8,12,72,128]{3,2,1,0:T(8,128)(2,1)} broadcast(bf16[12,72,128]{2,1,0:T(8,128)(2,1)S(1)} %maximum_maximum_fusion), dimensions={1,2,3} | broadcast | bytes 1990656 | tf_op jit(solution)/shard_map/broadcast_in_dim | solution.py:200
  67.6 9.3 %all-to-all-start.2 = ((bf16[8,12,72,128]{3,2,1,0:T(8,128)(2,1)}), bf16[8,12,72,128]{3,2,1,0:T(8,128)(2,1)S(1)}, u32[]{:S(2)}, u32[]{:S(2)}) async-start(bf16[8,12,72,128]{3,2,1,0:T(8,128)(2,1)} %broadcast_in_dim.11), calls=%async_computation.2 | async-start | bytes 3538944 | tf_op jit(solution)/shard_map/all_to_all | solution.py:201
  76.9 0.0 copy-done
  76.9 0.1 constant_dynamic-slice_fusion
  77.0 0.1 copy.8.refs_0_
  77.1 0.1 reshape.25.refs_1_
  77.1 22.6 %all-to-all-done.2.refs_2_ = bf16[8,12,72,128]{3,2,1,0:T(8,128)(2,1)S(1)} async-done(((bf16[8,12,72,128]{3,2,1,0:T(8,128)(2,1)}), bf16[8,12,72,128]{3,2,1,0:T(8,128)(2,1)S(1)}, u32[]{:S(2)}, u32[]{:S(2)}) %all-to-all-start.2) | async-done | bytes 1769504 | tf_op jit(solution)/shard_map/all_to_all | solution.py:201
  99.8 23.8 %shard_map.37 = f32[8,8,1024]{2,1,0:T(8,128)S(1)} custom-call(s32[8,3]{1,0:T(8,128)S(1)} %copy.8.refs_0_, bf16[96,1536]{1,0:T(8,128)(2,1)S(1)} %reshape.25.refs_1_, bf16[8,12,72,128]{3,2,1,0:T(8,128)(2,1)S(1)} %all-to-all-done.2.refs_2_), custom_call_target="tpu_custom_call" | custom-call | flops 4026531840 | bytes 2326528 | tf_op jit(solution)/shard_map/pallas_call | solution.py:164
  123.6 11.3 %all_to_all.20 = f32[8,8,1024]{2,1,0:T(8,128)S(1)} all-to-all(f32[8,8,1024]{2,1,0:T(8,128)S(1)} %shard_map.37), channel_id=1, replica_groups={{0,8,16,24,32,40,48,56},{64,72,80,88,96,104,112,120},{128,136,144,152,1..., dimensions={0} | all-to-all | bytes 524288 | tf_op jit(solution)/shard_map/all_to_all | solution.py:242
  134.9 0.7 copy.11
  (5 shorter events, 0.1 us)
Async XLA Ops:
  0.0 76.9 %copy-start = (s32[512,3]{0,1:T(4,128)S(1)}, s32[512,3]{0,1:T(4,128)}, u32[]{:S(2)}) copy-start(s32[512,3]{0,1:T(4,128)} %param.5) | copy-start | bytes 18436
  0.7 5.0 %collective-permute-start.1 = (bf16[3,4,512]{2,1,0:T(4,128)(2,1)S(1)}, bf16[3,4,512]{2,1,0:T(4,128)(2,1)S(1)}, u32[]{:S(2)}, u32[]{:S(2)}) collective-permute-start(bf16[3,4,512]{2,1,0:T(4,128)(2,1)S(1)} %slice.9), channel_id=1, source_target_pairs={{8,0},{16,8},{24,16},{32,24},{40,32},{48,40},{56,48},{64,56},{72,6... | collective-permute-start | bytes 36872 | tf_op jit(solution)/shard_map/ppermute | solution.py:227
  6.5 18.1 %all-to-all-start.1 = ((bf16[8,144,128]{2,1,0:T(8,128)(2,1)}), bf16[8,144,128]{2,1,0:T(8,128)(2,1)S(1)}, u32[]{:S(2)}, u32[]{:S(2)}) async-start(bf16[8,144,128]{2,1,0:T(8,128)(2,1)} %broadcast_in_dim.9), calls=%async_computation.1 | async-start | bytes 589824 | tf_op jit(solution)/shard_map/all_to_all | solution.py:201
  14.8 9.9 %collective-permute-start = (bf16[12,1536]{1,0:T(8,128)(2,1)S(1)}, bf16[12,1536]{1,0:T(8,128)(2,1)S(1)}, u32[]{:S(2)}, u32[]{:S(2)}) collective-permute-start(bf16[12,1536]{1,0:T(8,128)(2,1)S(1)} %reshape.24), channel_id=1, source_target_pairs={{0,0},{1,64},{2,128},{3,192},{4,256},{5,320},{6,384},{7,448},{8,8}... | collective-permute-start | bytes 110600 | tf_op jit(solution)/shard_map/ppermute | solution.py:221
  25.4 40.7 %all-to-all-start = ((bf16[8,12,1536]{2,1,0:T(8,128)(2,1)}), bf16[8,12,1536]{2,1,0:T(8,128)(2,1)S(1)}, u32[]{:S(2)}, u32[]{:S(2)}) async-start(bf16[8,12,1536]{2,1,0:T(8,128)(2,1)} %broadcast_in_dim.8), calls=%async_computation | async-start | bytes 786432 | tf_op jit(solution)/shard_map/all_to_all | solution.py:201
  67.6 32.2 %all-to-all-start.2 = ((bf16[8,12,72,128]{3,2,1,0:T(8,128)(2,1)}), bf16[8,12,72,128]{3,2,1,0:T(8,128)(2,1)S(1)}, u32[]{:S(2)}, u32[]{:S(2)}) async-start(bf16[8,12,72,128]{3,2,1,0:T(8,128)(2,1)} %broadcast_in_dim.11), calls=%async_computation.2 | async-start | bytes 3538944 | tf_op jit(solution)/shard_map/all_to_all | solution.py:201

commit v2 on v1

v2 whole, which is shorter than its diff:
```python
import math

import jax
import jax.numpy as jnp
from jax import lax
from jax.experimental import pallas as pl
from jax.experimental.pallas import tpu as pltpu
from jax.sharding import PartitionSpec as P

L = 512
LANES = 128
HALF = 64
SPAN = L + LANES
SLOTS = 4
epsilon = 1e-06


def detect_kernel(
    first_station,
    factor,
    place_ref,
    groups_ref,
    templates_ref,
    series_ref,
    before_ref,
    out_ref,
    source,
    home,
    count,
    waves,
    norms,
    band,
    shifts,
    energy,
    scales,
    windows,
    toeplitz,
    share,
    total,
    turned,
):
    block, spread = groups_ref.shape
    n_group = series_ref.shape[0]
    here = series_ref.shape[1] // 3
    padded = series_ref.shape[2]
    rows = total.shape[1]
    stations = templates_ref.shape[2]
    slots = block * spread * stations
    lane = lax.broadcasted_iota(jnp.int32, (1, LANES), 1)
    low = lane < HALF

    def clear(n, carry):
        source[n] = block * spread
        home[n] = block
        return carry

    lax.fori_loop(0, source.shape[0], clear, 0)
    for n in range(n_group):
        count[n] = 0
    for r in range(block):
        k = r ^ place_ref[0]
        held = (k & 1) * 4 + (k & 2) + k // 4
        for i in range(spread):
            named = groups_ref[r, i]
            slot = named * SLOTS + count[named]
            source[slot] = held * spread + i
            home[slot] = r
            count[named] = count[named] + 1
    spare = waves.shape[0] - slots
    for c in range(3):
        for n in range(block * spread):
            part = templates_ref[n // spread, n % spread, :, c * L : (c + 1) * L]
            at = n * stations
            waves[at : at + stations, c * SPAN : c * SPAN + L] = part.astype(jnp.float32)
        waves[0:slots, c * SPAN + L : (c + 1) * SPAN] = jnp.zeros((slots, LANES), jnp.float32)
    waves[slots:, :] = jnp.zeros((spare, 3 * SPAN), jnp.float32)
    squares = jnp.sum(jnp.square(waves[0:slots, :]), axis=1, keepdims=True)
    norms[0:slots, :] = jnp.broadcast_to(lax.rsqrt(squares + epsilon), (slots, LANES))
    norms[slots:, :] = jnp.zeros((spare, LANES), jnp.float32)
    r = lax.broadcasted_iota(jnp.int32, (LANES, LANES), 0)
    l = lax.broadcasted_iota(jnp.int32, (LANES, LANES), 1)
    band[0:LANES, :] = jnp.where(r >= l, 1.0, 0.0).astype(jnp.bfloat16)
    band[LANES : 2 * LANES, :] = jnp.ones((LANES, LANES), jnp.bfloat16)
    band[2 * LANES :, :] = jnp.where(r < l, 1.0, 0.0).astype(jnp.bfloat16)
    shifts[:, :, padded:, :] = jnp.zeros((3, 2, 8, LANES), jnp.float32)
    if before_ref is None:
        total[...] = jnp.zeros_like(total)
    else:
        total[...] = before_ref[...]

    def prepare(group, station, buffer):
        squares = jnp.zeros((padded, LANES), jnp.float32)
        for c in range(3):
            plain = series_ref[group, c * here + station].astype(jnp.float32)
            squares = squares + plain * plain
            shifts[c, 0, 0:padded, :] = plain
            after = shifts[c, 0, 1 : padded + 1, :]
            shifts[c, 1, 0:padded, :] = pltpu.roll(jnp.where(low, after, plain), HALF, 1)
        energy[...] = squares
        middle = energy[1 : rows + 1, :] + energy[2 : rows + 2, :] + energy[3 : rows + 3, :]
        pieces = jnp.concatenate([energy[0:rows, :], middle, energy[4 : rows + 4, :]], axis=1)
        coarse = pieces.astype(jnp.bfloat16)
        fine = (pieces - coarse.astype(jnp.float32)).astype(jnp.bfloat16)
        window_energy = jnp.dot(coarse, band[...], preferred_element_type=jnp.float32)
        window_energy += jnp.dot(fine, band[...], preferred_element_type=jnp.float32)
        scale = lax.rsqrt(window_energy + epsilon)
        other = pltpu.roll(scale, HALF, 1)
        scales[buffer, 0] = jnp.where(low, scale, other)
        scales[buffer, 1] = jnp.where(low, other, scale)
        for j in range(SLOTS):
            row = source[group * SLOTS + j] * stations + first_station + station
            for c in range(3):
                wave = waves[pl.ds(row, 1), c * SPAN : (c + 1) * SPAN]
                moved = pltpu.roll(
                    jnp.broadcast_to(wave, (HALF, SPAN)), 0, 1, stride=1, stride_axis=0
                )
                toeplitz[buffer, j * HALF : (j + 1) * HALF, c * SPAN : (c + 1) * SPAN] = (
                    moved.astype(jnp.bfloat16)
                )
        for c in range(3):
            for e in range(2):
                for v in range(SPAN // LANES):
                    at = c * SPAN + v * LANES
                    windows[buffer, e * rows : (e + 1) * rows, at : at + LANES] = shifts[
                        c, e, v : v + rows, :
                    ].astype(jnp.bfloat16)

    def combine(group, station, buffer):
        product = lax.dot_general(
            windows[buffer],
            toeplitz[buffer],
            (((1,), (1,)), ((), ())),
            preferred_element_type=jnp.float32,
        )
        weight = []
        for j in range(SLOTS):
            row = source[group * SLOTS + j] * stations + first_station + station
            weight.append(norms[pl.ds(row, 1), :])
        for p in range(SLOTS // 2):
            both = jnp.where(low, weight[2 * p], weight[2 * p + 1])
            at = p * LANES
            for e in range(2):
                term = product[e * rows : (e + 1) * rows, at : at + LANES]
                term = term * (scales[buffer, e] * both)
                if station:
                    term = term + share[e, :, at : at + LANES]
                share[e, :, at : at + LANES] = term

    def group_term(group, carry):
        later = lax.min(group + 1, n_group - 1)
        for station in range(here):
            if station < here - 1:
                prepare(group, station + 1, (station + 1) % 2)
            else:
                prepare(later, 0, (station + 1) % 2)
            combine(group, station, station % 2)
        for j in range(SLOTS):
            at = (j // 2) * LANES
            first = share[0, :, at : at + LANES]
            second = share[1, :, at : at + LANES]
            if j % 2 == 0:
                whole = jnp.where(low, first, pltpu.roll(second, HALF, 1))
            else:
                whole = jnp.where(low, pltpu.roll(first, HALF, 1), second)
            r = home[group * SLOTS + j]
            total[r] = total[r] + whole
        return carry

    prepare(0, 0, 0)
    lax.fori_loop(0, n_group, group_term, 0)
    if factor is None:
        out_ref[...] = total[...]
        return
    for r in range(block):
        turned[:, r, :] = total[r] * factor
    parts, _, samples = out_ref.shape
    for w in range(parts):
        for i in range(samples // LANES):
            out_ref[w, :, i * LANES : (i + 1) * LANES] = turned[w * (samples // LANES) + i]


def detect(place, groups, templates, series, before, first_station, parts, factor):
    n_group, channels, padded, _ = series.shape
    block, spread = groups.shape
    stations = templates.shape[2]
    slots = block * spread * stations
    rows = padded - 8
    samples = rows * LANES // parts
    spare = -(-(slots + stations) // 8) * 8
    if factor is None:
        out_shape = jax.ShapeDtypeStruct((block + 1, rows, LANES), jnp.float32)
    else:
        out_shape = jax.ShapeDtypeStruct((parts, block, samples), jnp.float32)
    operands = [place, groups, templates, series]
    spaces = [pltpu.SMEM, pltpu.SMEM, pltpu.VMEM, pltpu.VMEM]
    if before is not None:
        operands.append(before)
        spaces.append(pltpu.VMEM)

    def body(*refs):
        refs = list(refs)
        if before is None:
            refs.insert(4, None)
        detect_kernel(first_station, factor, *refs)

    return pl.pallas_call(
        body,
        out_shape=out_shape,
        in_specs=[pl.BlockSpec(memory_space=space) for space in spaces],
        out_specs=pl.BlockSpec(memory_space=pltpu.VMEM),
        scratch_shapes=[
            pltpu.SMEM((n_group * SLOTS,), jnp.int32),
            pltpu.SMEM((n_group * SLOTS,), jnp.int32),
            pltpu.SMEM((n_group,), jnp.int32),
            pltpu.VMEM((spare, 3 * SPAN), jnp.float32),
            pltpu.VMEM((spare, LANES), jnp.float32),
            pltpu.VMEM((3 * LANES, LANES), jnp.bfloat16),
            pltpu.VMEM((3, 2, padded + 8, LANES), jnp.float32),
            pltpu.VMEM((padded, LANES), jnp.float32),
            pltpu.VMEM((2, 2, rows, LANES), jnp.float32),
            pltpu.VMEM((2, 2 * rows, 3 * SPAN), jnp.bfloat16),
            pltpu.VMEM((2, SLOTS * HALF, 3 * SPAN), jnp.bfloat16),
            pltpu.VMEM((2, rows, SLOTS * HALF), jnp.float32),
            pltpu.VMEM((block + 1, rows, LANES), jnp.float32),
            pltpu.VMEM((rows, block, LANES), jnp.float32),
        ],
        compiler_params=pltpu.CompilerParams(vmem_limit_bytes=32 * 1024 * 1024),
        cost_estimate=pl.CostEstimate(
            flops=8 * n_group * (channels // 3) * 2 * rows * 3 * SPAN * SLOTS * HALF,
            bytes_accessed=series.size * 2 + templates.size * 2 + 4 * block * rows * LANES,
            transcendentals=0,
        ),
    )(*operands)


def copies_to(value, axis, groups=None):
    count = len(groups[0]) if groups else lax.axis_size(axis)
    spread = jnp.broadcast_to(value[None], (count,) + value.shape)
    return lax.all_to_all(spread, axis, 0, 0, axis_index_groups=groups, tiled=True)


def on_device(record, templates, template_groups):
    channels, stations, samples = record.shape
    n_tm, n_sta = lax.axis_size("tm"), lax.axis_size("sta")
    m, s = lax.axis_index("tm"), lax.axis_index("sta")
    n_a = n_sta
    n_b = n_tm // n_a
    near = [[a * n_b + b for b in range(n_b)] for a in range(n_a)]
    far = [[a * n_b + b for a in range(n_a)] for b in range(n_b)]
    spread = template_groups.shape[1]

    def device(a, b, t):
        return (a * n_b + b) * n_sta + t

    def carried(value, target):
        pairs = [
            (device(a, b, t), device(*target(a, b, t)))
            for a in range(n_a)
            for b in range(n_b)
            for t in range(n_sta)
        ]
        return lax.ppermute(value, ("tm", "sta"), pairs)

    held = templates
    half = n_a // 2
    held = jnp.concatenate(
        [
            carried(held, lambda a, b, t: (t, b, a)),
            carried(held, lambda a, b, t: (t ^ half, b, a)),
        ]
    )
    step = half // 2
    while step:
        held = jnp.concatenate([held, carried(held, lambda a, b, t: (a ^ step, b, t))])
        step //= 2
    place = (m // n_b).reshape(1)
    first = (s * n_b + lax.rem(m, n_b)) * n_a
    groups = lax.dynamic_slice_in_dim(template_groups, first, n_a, 0)

    halo = lax.ppermute(record[:, :, :L], "tm", [(i + 1, i) for i in range(n_tm - 1)])
    lines = channels * stations
    steps = samples // LANES
    piece = jnp.concatenate(
        [record.reshape(lines * steps, LANES), halo.reshape(lines * (L // LANES), LANES)]
    )
    around = copies_to(piece, "tm", near)
    main = around[:, : lines * steps].reshape(n_b, channels, stations, steps, LANES)
    tail = around[-1, lines * steps :].reshape(channels, stations, L // LANES, LANES)
    some = stations // 2
    total = None
    for begin in range(0, stations, some):
        part = main[:, :, begin : begin + some].transpose(1, 2, 0, 3, 4)
        part = part.reshape(channels * some, n_b * steps, LANES)
        end = tail[:, begin : begin + some].reshape(channels * some, L // LANES, LANES)
        rest = jnp.zeros((channels * some, 8 - L // LANES, LANES), record.dtype)
        series = copies_to(jnp.concatenate([part, end, rest], axis=1), "sta")
        last = begin + some == stations
        factor = math.sqrt(channels * L / (spread * stations)) if last else None
        total = detect(place, groups, held, series, total, begin, n_b, factor)

    found = lax.all_to_all(total, "tm", 0, 0, axis_index_groups=near, tiled=True)
    return found.reshape(n_b * n_a, samples)


def solution(mesh):
    return jax.shard_map(
        on_device,
        mesh=mesh,
        in_specs=(P(None, "sta", "tm"), P(("tm", "sta"), None, None, None), P()),
        out_specs=P("sta", "tm"),
        check_vma=False,
    )
```

time: 136 us -> 108 us (0.79)
  waiting for transfers between devices: 47 us -> 22 us
  Pallas kernels: 23.8 us -> 20.6 us
  local copies, waits for them, and re-layouts: 6.32 us -> 4.81 us
    all_to_all x3, waiting for transfers between devices: 42.3 us -> 14.3 us  [copies_to(): lax.all_to_all(spread, axis, 0, 0, axis_index_groups=groups, tiled=True)]
    ppermute x1 -> x4, starting transfers between devices: 8.1 us -> 29.6 us  [carried(): return lax.ppermute(value, ('tm', 'sta'), pairs)]
    all_to_all x3, starting transfers between devices: 37.6 us -> 16.7 us  [copies_to(): lax.all_to_all(spread, axis, 0, 0, axis_index_groups=groups, tiled=True)]
    pallas_call x1 -> x2, Pallas kernels: 23.8 us -> 20.6 us  [detect(): pl.pallas_call(body, out_shape=out_shape, in_specs=[pl.BlockSpec(memory_s...]
    ppermute x1 -> x4, waiting for transfers between devices: 1.76 us -> 3.99 us  [carried(): return lax.ppermute(value, ('tm', 'sta'), pairs)]
  transfers between devices with their start and end apart: 5 -> 8, of which waited for: 4 -> 4; matrix products, arithmetic and copies ran while one was open for 1% -> 3% of each run, Pallas kernels for 0% -> 10%
where the time goes in v2:
time: 108 us; the launch traced here: 107 us
  starting transfers between devices  47.6 us (44%)
  waiting for transfers between devices  22 us (20%)
  Pallas kernels  20.6 us (19%)
  blocking collectives  11.6 us (11%)
  local copies, waits for them, and re-layouts  4.81 us (4%)
    ppermute x4, starting transfers between devices, carried(): return lax.ppermute(value, ('tm', 'sta'), pairs)  29.6 us
    pallas_call x2, Pallas kernels, detect(): pl.pallas_call(body, out_shape=out_shape, in_specs=[pl.BlockSpec(memory_s...  20.6 us
    all_to_all x3, starting transfers between devices, copies_to(): lax.all_to_all(spread, axis, 0, 0, axis_index_groups=groups, tiled=True)  16.7 us
    all_to_all x3, waiting for transfers between devices, copies_to(): lax.all_to_all(spread, axis, 0, 0, axis_index_groups=groups, tiled=True)  14.3 us
    all_to_all x1, blocking collectives, on_device(): lax.all_to_all(total, 'tm', 0, 0, axis_index_groups=near, tiled=True)  11.6 us
    ppermute x4, waiting for transfers between devices, carried(): return lax.ppermute(value, ('tm', 'sta'), pairs)  3.99 us
    ppermute x1, waiting for transfers between devices, on_device(): lax.ppermute(record[:, :, :L], 'tm', [(i + 1, i) for i in range(n_tm - 1)])  3.69 us
    broadcast_in_dim x3, local copies, waits for them, and re-layouts, copies_to(): spread = jnp.broadcast_to(value[None], (count,) + value.shape)  2.82 us
  transfers between devices with their start and end apart: 8, of which 4 were waited for; matrix products, arithmetic and copies ran while one was open for 3% of the time, Pallas kernels for 10%

profile of v2, /device:TPU:1, one launch (start us, length us, event | category | flops | bytes accessed | tf_op | source)
XLA Modules:
  0.0 107.0 jit_solution(1985322324057467851)
XLA Ops:
  0.0 0.0 copy-start
  0.0 0.0 copy-start.1
  0.0 0.8 slice.21
  0.8 1.3 %collective-permute-start.4 = (bf16[3,4,512]{2,1,0:T(4,128)(2,1)S(1)}, bf16[3,4,512]{2,1,0:T(4,128)(2,1)S(1)}, u32[]{:S(2)}, u32[]{:S(2)}) collective-permute-start(bf16[3,4,512]{2,1,0:T(4,128)(2,1)S(1)} %slice.21), channel_id=1, source_target_pairs={{8,0},{16,8},{24,16},{32,24},{40,32},{48,40},{56,48},{64,56},{72,6... | collective-permute-start | bytes 36872 | tf_op jit(solution)/shard_map/ppermute | solution.py:280
  2.1 0.0 copy-done.1
  2.1 3.7 %collective-permute-done.4 = bf16[3,4,512]{2,1,0:T(4,128)(2,1)S(1)} collective-permute-done((bf16[3,4,512]{2,1,0:T(4,128)(2,1)S(1)}, bf16[3,4,512]{2,1,0:T(4,128)(2,1)S(1)}, u32[]{:S(2)}, u32[]{:S(2)}) %collective-permute-start.4) | collective-permute-done | bytes 12320 | tf_op jit(solution)/shard_map/ppermute | solution.py:280
  5.8 0.8 broadcast_in_dim.6
  6.6 0.0 copy-start.2
  6.6 7.6 %all-to-all-start = ((bf16[8,144,128]{2,1,0:T(8,128)(2,1)}), bf16[8,144,128]{2,1,0:T(8,128)(2,1)S(1)}, u32[]{:S(2)}, u32[]{:S(2)}) async-start(bf16[8,144,128]{2,1,0:T(8,128)(2,1)} %broadcast_in_dim.6), calls=%async_computation | async-start | bytes 589824 | tf_op jit(solution)/shard_map/all_to_all | solution.py:239
  14.2 0.0 copy-done.2
  14.2 16.9 %collective-permute-start.1 = (bf16[1,3,4,1536]{3,2,1,0:T(4,128)(2,1)S(1)}, bf16[1,3,4,1536]{3,2,1,0:T(4,128)(2,1)S(1)}, u32[]{:S(2)}, u32[]{:S(2)}) collective-permute-start(bf16[1,3,4,1536]{3,2,1,0:T(4,128)(2,1)S(1)} %copy-done.2), channel_id=1, source_target_pairs={{0,256},{1,320},{2,384},{3,448},{4,0},{5,64},{6,128},{7,192},{8,26... | collective-permute-start | bytes 110600 | tf_op jit(solution)/shard_map/ppermute | solution.py:262
  31.0 1.9 %collective-permute-start = (bf16[1,3,4,1536]{3,2,1,0:T(4,128)(2,1)S(1)}, bf16[1,3,4,1536]{3,2,1,0:T(4,128)(2,1)S(1)}, u32[]{:S(2)}, u32[]{:S(2)}) collective-permute-start(bf16[1,3,4,1536]{3,2,1,0:T(4,128)(2,1)S(1)} %copy-done.2), channel_id=1, source_target_pairs={{0,0},{1,64},{2,128},{3,192},{4,256},{5,320},{6,384},{7,448},{8,8}... | collective-permute-start | bytes 110600 | tf_op jit(solution)/shard_map/ppermute | solution.py:262
  33.0 0.0 copy-done
  33.0 0.1 constant_dynamic-slice_fusion
  33.1 0.1 copy.9.refs_1_
  33.2 0.1 pad.5.clone
  33.2 0.0 collective-permute-done.1
  33.2 4.0 %collective-permute-done = bf16[1,3,4,1536]{3,2,1,0:T(4,128)(2,1)S(1)} collective-permute-done((bf16[1,3,4,1536]{3,2,1,0:T(4,128)(2,1)S(1)}, bf16[1,3,4,1536]{3,2,1,0:T(4,128)(2,1)S(1)}, u32[]{:S(2)}, u32[]{:S(2)}) %collective-permute-start) | collective-permute-done | bytes 36896 | tf_op jit(solution)/shard_map/ppermute | solution.py:262
  37.2 0.1 pad_maximum_fusion.1
  37.3 8.9 %collective-permute-start.2 = (bf16[2,3,4,1536]{3,2,1,0:T(4,128)(2,1)S(1)}, bf16[2,3,4,1536]{3,2,1,0:T(4,128)(2,1)S(1)}, u32[]{:S(2)}, u32[]{:S(2)}) collective-permute-start(bf16[2,3,4,1536]{3,2,1,0:T(4,128)(2,1)S(1)} %pad_maximum_fusion.1), channel_id=1, source_target_pairs={{0,128},{1,129},{2,130},{3,131},{4,132},{5,133},{6,134},{7,135},{8... | collective-permute-start | bytes 221192 | tf_op jit(solution)/shard_map/ppermute | solution.py:262
  46.2 0.0 all-to-all-done
  46.3 0.1 maximum_maximum_fusion.1
  46.5 1.0 broadcast_in_dim.8
  47.5 4.8 %all-to-all-start.2 = ((bf16[8,6,72,128]{3,2,1,0:T(8,128)(2,1)}), bf16[8,6,72,128]{3,2,1,0:T(8,128)(2,1)S(1)}, u32[]{:S(2)}, u32[]{:S(2)}) async-start(bf16[8,6,72,128]{3,2,1,0:T(8,128)(2,1)} %broadcast_in_dim.8), calls=%async_computation.2 | async-start | bytes 1769472 | tf_op jit(solution)/shard_map/all_to_all | solution.py:239
  52.3 0.0 collective-permute-done.2
  52.4 0.1 pad_maximum_fusion
  52.5 1.9 %collective-permute-start.3 = (bf16[4,3,4,1536]{3,2,1,0:T(4,128)(2,1)S(1)}, bf16[4,3,4,1536]{3,2,1,0:T(4,128)(2,1)S(1)}, u32[]{:S(2)}, u32[]{:S(2)}) collective-permute-start(bf16[4,3,4,1536]{3,2,1,0:T(4,128)(2,1)S(1)} %pad_maximum_fusion), channel_id=1, source_target_pairs={{0,64},{1,65},{2,66},{3,67},{4,68},{5,69},{6,70},{7,71},{8,72},{9,... | collective-permute-start | bytes 442376 | tf_op jit(solution)/shard_map/ppermute | solution.py:262
  54.4 11.2 %all-to-all-done.2.refs_3_ = bf16[8,6,72,128]{3,2,1,0:T(8,128)(2,1)S(1)} async-done(((bf16[8,6,72,128]{3,2,1,0:T(8,128)(2,1)}), bf16[8,6,72,128]{3,2,1,0:T(8,128)(2,1)S(1)}, u32[]{:S(2)}, u32[]{:S(2)}) %all-to-all-start.2) | async-done | bytes 884768 | tf_op jit(solution)/shard_map/all_to_all | solution.py:239
  65.6 1.0 broadcast_in_dim.7
  66.7 4.3 %all-to-all-start.1 = ((bf16[8,6,72,128]{3,2,1,0:T(8,128)(2,1)}), bf16[8,6,72,128]{3,2,1,0:T(8,128)(2,1)S(1)}, u32[]{:S(2)}, u32[]{:S(2)}) async-start(bf16[8,6,72,128]{3,2,1,0:T(8,128)(2,1)} %broadcast_in_dim.7), calls=%async_computation.1 | async-start | bytes 1769472 | tf_op jit(solution)/shard_map/all_to_all | solution.py:239
  71.0 0.0 collective-permute-done.3
  71.0 0.1 constant_dynamic-update-slice_fusion.refs_2_
  71.1 10.2 %shard_map.37.refs_4_ = f32[9,64,128]{2,1,0:T(8,128)S(1)} custom-call(s32[1]{0:T(128)} %bitcast.refs_0_, s32[8,3]{1,0:T(8,128)S(1)} %copy.9.refs_1_, bf16[8,3,4,1536]{3,2,1,0:T(4,128)(2,1)S(1)} %constant_dynamic-update-slice_fusion.refs_2_, bf16[8,6,72,128]{3,2,1,0:T(8,128)(2,1)S(1)} %all-to-all-done.2.refs_3_), custom_call_target="tpu_custom_call" | custom-call | flops 8053063680 | bytes 1441792 | tf_op jit(solution)/shard_map/pallas_call | solution.py:206
  81.3 3.1 %all-to-all-done.1.refs_3_ = bf16[8,6,72,128]{3,2,1,0:T(8,128)(2,1)S(1)} async-done(((bf16[8,6,72,128]{3,2,1,0:T(8,128)(2,1)}), bf16[8,6,72,128]{3,2,1,0:T(8,128)(2,1)S(1)}, u32[]{:S(2)}, u32[]{:S(2)}) %all-to-all-start.1) | async-done | bytes 884768 | tf_op jit(solution)/shard_map/all_to_all | solution.py:239
  84.4 10.4 %shard_map.38 = f32[8,8,1024]{2,1,0:T(8,128)S(1)} custom-call(s32[1]{0:T(128)} %bitcast.refs_0_, s32[8,3]{1,0:T(8,128)S(1)} %copy.9.refs_1_, bf16[8,3,4,1536]{3,2,1,0:T(4,128)(2,1)S(1)} %constant_dynamic-update-slice_fusion.refs_2_, bf16[8,6,72,128]{3,2,1,0:T(8,128)(2,1)S(1)} %all-to-all-done.1.refs_3_, f32[9,64,128]{2,1,0:T(8,128)S(1)} %shard_map.37.refs_4_), custom_call_target="tpu_custom_call" | custom-call | flops 8053063680 | bytes 1441792 | tf_op jit(solution)/shard_map/pallas_call | solution.py:206
  94.7 11.6 %all_to_all.20 = f32[8,8,1024]{2,1,0:T(8,128)S(1)} all-to-all(f32[8,8,1024]{2,1,0:T(8,128)S(1)} %shard_map.38), channel_id=1, replica_groups={{0,8,16,24,32,40,48,56},{64,72,80,88,96,104,112,120},{128,136,144,152,1..., dimensions={0} | all-to-all | bytes 524288 | tf_op jit(solution)/shard_map/all_to_all | solution.py:301
  106.3 0.7 copy.14
  (13 shorter events, 0.2 us)
Async XLA Ops:
  0.0 33.0 %copy-start = (s32[512,3]{0,1:T(4,128)S(1)}, s32[512,3]{0,1:T(4,128)}, u32[]{:S(2)}) copy-start(s32[512,3]{0,1:T(4,128)} %param.5) | copy-start | bytes 18436
  0.0 2.1 %copy-start.1 = (bf16[3,4,1024]{2,1,0:T(4,128)(2,1)S(1)}, bf16[3,4,1024]{2,1,0:T(4,128)(2,1)}, u32[]{:S(2)}) copy-start(bf16[3,4,1024]{2,1,0:T(4,128)(2,1)} %param.3) | copy-start | bytes 73732
  0.8 5.0 %collective-permute-start.4 = (bf16[3,4,512]{2,1,0:T(4,128)(2,1)S(1)}, bf16[3,4,512]{2,1,0:T(4,128)(2,1)S(1)}, u32[]{:S(2)}, u32[]{:S(2)}) collective-permute-start(bf16[3,4,512]{2,1,0:T(4,128)(2,1)S(1)} %slice.21), channel_id=1, source_target_pairs={{8,0},{16,8},{24,16},{32,24},{40,32},{48,40},{56,48},{64,56},{72,6... | collective-permute-start | bytes 36872 | tf_op jit(solution)/shard_map/ppermute | solution.py:280
  6.6 7.6 %copy-start.2 = (bf16[1,3,4,1536]{3,2,1,0:T(4,128)(2,1)S(1)}, bf16[1,3,4,1536]{3,2,1,0:T(4,128)(2,1)}, u32[]{:S(2)}) copy-start(bf16[1,3,4,1536]{3,2,1,0:T(4,128)(2,1)} %param.4) | copy-start | bytes 110596
  6.6 39.6 %all-to-all-start = ((bf16[8,144,128]{2,1,0:T(8,128)(2,1)}), bf16[8,144,128]{2,1,0:T(8,128)(2,1)S(1)}, u32[]{:S(2)}, u32[]{:S(2)}) async-start(bf16[8,144,128]{2,1,0:T(8,128)(2,1)} %broadcast_in_dim.6), calls=%async_computation | async-start | bytes 589824 | tf_op jit(solution)/shard_map/all_to_all | solution.py:239
  14.2 19.1 %collective-permute-start.1 = (bf16[1,3,4,1536]{3,2,1,0:T(4,128)(2,1)S(1)}, bf16[1,3,4,1536]{3,2,1,0:T(4,128)(2,1)S(1)}, u32[]{:S(2)}, u32[]{:S(2)}) collective-permute-start(bf16[1,3,4,1536]{3,2,1,0:T(4,128)(2,1)S(1)} %copy-done.2), channel_id=1, source_target_pairs={{0,256},{1,320},{2,384},{3,448},{4,0},{5,64},{6,128},{7,192},{8,26... | collective-permute-start | bytes 110600 | tf_op jit(solution)/shard_map/ppermute | solution.py:262
  31.0 6.2 %collective-permute-start = (bf16[1,3,4,1536]{3,2,1,0:T(4,128)(2,1)S(1)}, bf16[1,3,4,1536]{3,2,1,0:T(4,128)(2,1)S(1)}, u32[]{:S(2)}, u32[]{:S(2)}) collective-permute-start(bf16[1,3,4,1536]{3,2,1,0:T(4,128)(2,1)S(1)} %copy-done.2), channel_id=1, source_target_pairs={{0,0},{1,64},{2,128},{3,192},{4,256},{5,320},{6,384},{7,448},{8,8}... | collective-permute-start | bytes 110600 | tf_op jit(solution)/shard_map/ppermute | solution.py:262
  37.3 15.1 %collective-permute-start.2 = (bf16[2,3,4,1536]{3,2,1,0:T(4,128)(2,1)S(1)}, bf16[2,3,4,1536]{3,2,1,0:T(4,128)(2,1)S(1)}, u32[]{:S(2)}, u32[]{:S(2)}) collective-permute-start(bf16[2,3,4,1536]{3,2,1,0:T(4,128)(2,1)S(1)} %pad_maximum_fusion.1), channel_id=1, source_target_pairs={{0,128},{1,129},{2,130},{3,131},{4,132},{5,133},{6,134},{7,135},{8... | collective-permute-start | bytes 221192 | tf_op jit(solution)/shard_map/ppermute | solution.py:262
  47.5 18.1 %all-to-all-start.2 = ((bf16[8,6,72,128]{3,2,1,0:T(8,128)(2,1)}), bf16[8,6,72,128]{3,2,1,0:T(8,128)(2,1)S(1)}, u32[]{:S(2)}, u32[]{:S(2)}) async-start(bf16[8,6,72,128]{3,2,1,0:T(8,128)(2,1)} %broadcast_in_dim.8), calls=%async_computation.2 | async-start | bytes 1769472 | tf_op jit(solution)/shard_map/all_to_all | solution.py:239
  52.5 18.5 %collective-permute-start.3 = (bf16[4,3,4,1536]{3,2,1,0:T(4,128)(2,1)S(1)}, bf16[4,3,4,1536]{3,2,1,0:T(4,128)(2,1)S(1)}, u32[]{:S(2)}, u32[]{:S(2)}) collective-permute-start(bf16[4,3,4,1536]{3,2,1,0:T(4,128)(2,1)S(1)} %pad_maximum_fusion), channel_id=1, source_target_pairs={{0,64},{1,65},{2,66},{3,67},{4,68},{5,69},{6,70},{7,71},{8,72},{9,... | collective-permute-start | bytes 442376 | tf_op jit(solution)/shard_map/ppermute | solution.py:262
  66.7 17.7 %all-to-all-start.1 = ((bf16[8,6,72,128]{3,2,1,0:T(8,128)(2,1)}), bf16[8,6,72,128]{3,2,1,0:T(8,128)(2,1)S(1)}, u32[]{:S(2)}, u32[]{:S(2)}) async-start(bf16[8,6,72,128]{3,2,1,0:T(8,128)(2,1)} %broadcast_in_dim.7), calls=%async_computation.1 | async-start | bytes 1769472 | tf_op jit(solution)/shard_map/all_to_all | solution.py:239

commit v3 on v2

--- a/solution.py
+++ b/solution.py
@@ -261,18 +261,9 @@
         ]
         return lax.ppermute(value, ("tm", "sta"), pairs)
 
-    held = templates
-    half = n_a // 2
-    held = jnp.concatenate(
-        [
-            carried(held, lambda a, b, t: (t, b, a)),
-            carried(held, lambda a, b, t: (t ^ half, b, a)),
-        ]
-    )
-    step = half // 2
-    while step:
-        held = jnp.concatenate([held, carried(held, lambda a, b, t: (a ^ step, b, t))])
-        step //= 2
+    near_ones = [carried(templates, lambda a, b, t: (t ^ k, b, a)) for k in (0, 4, 2, 6)]
+    held = jnp.concatenate(near_ones)
+    held = jnp.concatenate([held, carried(held, lambda a, b, t: (a ^ 1, b, t))])
     place = (m // n_b).reshape(1)
     first = (s * n_b + lax.rem(m, n_b)) * n_a
     groups = lax.dynamic_slice_in_dim(template_groups, first, n_a, 0)

time: 108 us -> 118 us (1.093)
  starting transfers between devices: 47.6 us -> 58.1 us
    all_to_all x3, starting transfers between devices: 16.7 us -> 22.6 us  [copies_to(): lax.all_to_all(spread, axis, 0, 0, axis_index_groups=groups, tiled=True)]
    ppermute x4 -> x5, starting transfers between devices: 29.6 us -> 34.3 us  [carried(): return lax.ppermute(value, ('tm', 'sta'), pairs)]
    ppermute x4 -> x5, waiting for transfers between devices: 3.99 us -> 1 us  [carried(): return lax.ppermute(value, ('tm', 'sta'), pairs)]
    all_to_all x3, waiting for transfers between devices: 14.3 us -> 16.3 us  [copies_to(): lax.all_to_all(spread, axis, 0, 0, axis_index_groups=groups, tiled=True)]
  transfers between devices with their start and end apart: 8 -> 9, of which waited for: 4 -> 4; matrix products, arithmetic and copies ran while one was open for 3% -> 2% of each run, Pallas kernels for 10% -> 9%
where the time goes in v3:
time: 118 us; the launch traced here: 117 us
  starting transfers between devices  58.1 us (49%)
  waiting for transfers between devices  21 us (18%)
  Pallas kernels  20.6 us (17%)
  blocking collectives  11.6 us (10%)
  local copies, waits for them, and re-layouts  4.81 us (4%)
    ppermute x5, starting transfers between devices, carried(): return lax.ppermute(value, ('tm', 'sta'), pairs)  34.3 us
    all_to_all x3, starting transfers between devices, copies_to(): lax.all_to_all(spread, axis, 0, 0, axis_index_groups=groups, tiled=True)  22.6 us
    pallas_call x2, Pallas kernels, detect(): pl.pallas_call(body, out_shape=out_shape, in_specs=[pl.BlockSpec(memory_s...  20.6 us
    all_to_all x3, waiting for transfers between devices, copies_to(): lax.all_to_all(spread, axis, 0, 0, axis_index_groups=groups, tiled=True)  16.3 us
    all_to_all x1, blocking collectives, on_device(): lax.all_to_all(total, 'tm', 0, 0, axis_index_groups=near, tiled=True)  11.6 us
    ppermute x1, waiting for transfers between devices, on_device(): lax.ppermute(record[:, :, :L], 'tm', [(i + 1, i) for i in range(n_tm - 1)])  3.69 us
    broadcast_in_dim x3, local copies, waits for them, and re-layouts, copies_to(): spread = jnp.broadcast_to(value[None], (count,) + value.shape)  2.81 us
  transfers between devices with their start and end apart: 9, of which 4 were waited for; matrix products, arithmetic and copies ran while one was open for 2% of the time, Pallas kernels for 9%

profile of v3, /device:TPU:1, one launch (start us, length us, event | category | flops | bytes accessed | tf_op | source)
XLA Modules:
  0.0 116.5 jit_solution(17526343790522594224)
XLA Ops:
  0.0 0.0 copy-start
  0.0 0.0 copy-start.1
  0.0 0.8 slice.21
  0.8 1.3 %collective-permute-start.5 = (bf16[3,4,512]{2,1,0:T(4,128)(2,1)S(1)}, bf16[3,4,512]{2,1,0:T(4,128)(2,1)S(1)}, u32[]{:S(2)}, u32[]{:S(2)}) collective-permute-start(bf16[3,4,512]{2,1,0:T(4,128)(2,1)S(1)} %slice.21), channel_id=1, source_target_pairs={{8,0},{16,8},{24,16},{32,24},{40,32},{48,40},{56,48},{64,56},{72,6... | collective-permute-start | bytes 36872 | tf_op jit(solution)/shard_map/ppermute | solution.py:271
  2.1 0.0 copy-done.1
  2.1 3.7 %collective-permute-done.5 = bf16[3,4,512]{2,1,0:T(4,128)(2,1)S(1)} collective-permute-done((bf16[3,4,512]{2,1,0:T(4,128)(2,1)S(1)}, bf16[3,4,512]{2,1,0:T(4,128)(2,1)S(1)}, u32[]{:S(2)}, u32[]{:S(2)}) %collective-permute-start.5) | collective-permute-done | bytes 12320 | tf_op jit(solution)/shard_map/ppermute | solution.py:271
  5.8 0.7 broadcast_in_dim.6
  6.6 0.0 copy-start.2
  6.6 7.6 %all-to-all-start = ((bf16[8,144,128]{2,1,0:T(8,128)(2,1)}), bf16[8,144,128]{2,1,0:T(8,128)(2,1)S(1)}, u32[]{:S(2)}, u32[]{:S(2)}) async-start(bf16[8,144,128]{2,1,0:T(8,128)(2,1)} %broadcast_in_dim.6), calls=%async_computation | async-start | bytes 589824 | tf_op jit(solution)/shard_map/all_to_all | solution.py:239
  14.2 0.0 copy-done.2
  14.2 16.9 %collective-permute-start.1 = (bf16[1,3,4,1536]{3,2,1,0:T(4,128)(2,1)S(1)}, bf16[1,3,4,1536]{3,2,1,0:T(4,128)(2,1)S(1)}, u32[]{:S(2)}, u32[]{:S(2)}) collective-permute-start(bf16[1,3,4,1536]{3,2,1,0:T(4,128)(2,1)S(1)} %copy-done.2), channel_id=1, source_target_pairs={{0,256},{1,320},{2,384},{3,448},{4,0},{5,64},{6,128},{7,192},{8,26... | collective-permute-start | bytes 110600 | tf_op jit(solution)/shard_map/ppermute | solution.py:262
  31.0 1.9 %collective-permute-start = (bf16[1,3,4,1536]{3,2,1,0:T(4,128)(2,1)S(1)}, bf16[1,3,4,1536]{3,2,1,0:T(4,128)(2,1)S(1)}, u32[]{:S(2)}, u32[]{:S(2)}) collective-permute-start(bf16[1,3,4,1536]{3,2,1,0:T(4,128)(2,1)S(1)} %copy-done.2), channel_id=1, source_target_pairs={{0,0},{1,64},{2,128},{3,192},{4,256},{5,320},{6,384},{7,448},{8,8}... | collective-permute-start | bytes 110600 | tf_op jit(solution)/shard_map/ppermute | solution.py:262
  33.0 5.7 %collective-permute-start.3 = (bf16[1,3,4,1536]{3,2,1,0:T(4,128)(2,1)S(1)}, bf16[1,3,4,1536]{3,2,1,0:T(4,128)(2,1)S(1)}, u32[]{:S(2)}, u32[]{:S(2)}) collective-permute-start(bf16[1,3,4,1536]{3,2,1,0:T(4,128)(2,1)S(1)} %copy-done.2), channel_id=1, source_target_pairs={{0,384},{1,448},{2,256},{3,320},{4,128},{5,192},{6,0},{7,64},{8,39... | collective-permute-start | bytes 110600 | tf_op jit(solution)/shard_map/ppermute | solution.py:262
  38.7 7.4 %collective-permute-start.2 = (bf16[1,3,4,1536]{3,2,1,0:T(4,128)(2,1)S(1)}, bf16[1,3,4,1536]{3,2,1,0:T(4,128)(2,1)S(1)}, u32[]{:S(2)}, u32[]{:S(2)}) collective-permute-start(bf16[1,3,4,1536]{3,2,1,0:T(4,128)(2,1)S(1)} %copy-done.2), channel_id=1, source_target_pairs={{0,128},{1,192},{2,0},{3,64},{4,384},{5,448},{6,256},{7,320},{8,13... | collective-permute-start | bytes 110600 | tf_op jit(solution)/shard_map/ppermute | solution.py:262
  46.1 0.0 copy-done
  46.1 0.1 constant_dynamic-slice_fusion
  46.2 0.1 copy.9.refs_1_
  46.3 0.1 pad.5.clone
  46.3 0.0 collective-permute-done.1
  46.3 0.0 collective-permute-done
  46.4 0.0 collective-permute-done.3
  46.4 1.0 collective-permute-done.2
  47.4 0.1 pad_maximum_fusion
  47.5 2.4 %collective-permute-start.4 = (bf16[4,3,4,1536]{3,2,1,0:T(4,128)(2,1)S(1)}, bf16[4,3,4,1536]{3,2,1,0:T(4,128)(2,1)S(1)}, u32[]{:S(2)}, u32[]{:S(2)}) collective-permute-start(bf16[4,3,4,1536]{3,2,1,0:T(4,128)(2,1)S(1)} %pad_maximum_fusion), channel_id=1, source_target_pairs={{0,64},{1,65},{2,66},{3,67},{4,68},{5,69},{6,70},{7,71},{8,72},{9,... | collective-permute-start | bytes 442376 | tf_op jit(solution)/shard_map/ppermute | solution.py:262
  49.9 0.0 all-to-all-done
  50.1 0.1 maximum_maximum_fusion.1
  50.2 1.0 broadcast_in_dim.8
  51.2 10.6 %all-to-all-start.2 = ((bf16[8,6,72,128]{3,2,1,0:T(8,128)(2,1)}), bf16[8,6,72,128]{3,2,1,0:T(8,128)(2,1)S(1)}, u32[]{:S(2)}, u32[]{:S(2)}) async-start(bf16[8,6,72,128]{3,2,1,0:T(8,128)(2,1)} %broadcast_in_dim.8), calls=%async_computation.2 | async-start | bytes 1769472 | tf_op jit(solution)/shard_map/all_to_all | solution.py:239
  61.9 13.2 %all-to-all-done.2.refs_3_ = bf16[8,6,72,128]{3,2,1,0:T(8,128)(2,1)S(1)} async-done(((bf16[8,6,72,128]{3,2,1,0:T(8,128)(2,1)}), bf16[8,6,72,128]{3,2,1,0:T(8,128)(2,1)S(1)}, u32[]{:S(2)}, u32[]{:S(2)}) %all-to-all-start.2) | async-done | bytes 884768 | tf_op jit(solution)/shard_map/all_to_all | solution.py:239
  75.2 1.0 broadcast_in_dim.7
  76.2 4.3 %all-to-all-start.1 = ((bf16[8,6,72,128]{3,2,1,0:T(8,128)(2,1)}), bf16[8,6,72,128]{3,2,1,0:T(8,128)(2,1)S(1)}, u32[]{:S(2)}, u32[]{:S(2)}) async-start(bf16[8,6,72,128]{3,2,1,0:T(8,128)(2,1)} %broadcast_in_dim.7), calls=%async_computation.1 | async-start | bytes 1769472 | tf_op jit(solution)/shard_map/all_to_all | solution.py:239
  80.5 0.0 collective-permute-done.4
  80.5 0.1 constant_dynamic-update-slice_fusion.refs_2_
  80.6 10.2 %shard_map.37.refs_4_ = f32[9,64,128]{2,1,0:T(8,128)S(1)} custom-call(s32[1]{0:T(128)} %bitcast.refs_0_, s32[8,3]{1,0:T(8,128)S(1)} %copy.9.refs_1_, bf16[8,3,4,1536]{3,2,1,0:T(4,128)(2,1)S(1)} %constant_dynamic-update-slice_fusion.refs_2_, bf16[8,6,72,128]{3,2,1,0:T(8,128)(2,1)S(1)} %all-to-all-done.2.refs_3_), custom_call_target="tpu_custom_call" | custom-call | flops 8053063680 | bytes 1441792 | tf_op jit(solution)/shard_map/pallas_call | solution.py:206
  90.8 3.1 %all-to-all-done.1.refs_3_ = bf16[8,6,72,128]{3,2,1,0:T(8,128)(2,1)S(1)} async-done(((bf16[8,6,72,128]{3,2,1,0:T(8,128)(2,1)}), bf16[8,6,72,128]{3,2,1,0:T(8,128)(2,1)S(1)}, u32[]{:S(2)}, u32[]{:S(2)}) %all-to-all-start.1) | async-done | bytes 884768 | tf_op jit(solution)/shard_map/all_to_all | solution.py:239
  93.9 10.4 %shard_map.38 = f32[8,8,1024]{2,1,0:T(8,128)S(1)} custom-call(s32[1]{0:T(128)} %bitcast.refs_0_, s32[8,3]{1,0:T(8,128)S(1)} %copy.9.refs_1_, bf16[8,3,4,1536]{3,2,1,0:T(4,128)(2,1)S(1)} %constant_dynamic-update-slice_fusion.refs_2_, bf16[8,6,72,128]{3,2,1,0:T(8,128)(2,1)S(1)} %all-to-all-done.1.refs_3_, f32[9,64,128]{2,1,0:T(8,128)S(1)} %shard_map.37.refs_4_), custom_call_target="tpu_custom_call" | custom-call | flops 8053063680 | bytes 1441792 | tf_op jit(solution)/shard_map/pallas_call | solution.py:206
  104.3 11.6 %all_to_all.20 = f32[8,8,1024]{2,1,0:T(8,128)S(1)} all-to-all(f32[8,8,1024]{2,1,0:T(8,128)S(1)} %shard_map.38), channel_id=1, replica_groups={{0,8,16,24,32,40,48,56},{64,72,80,88,96,104,112,120},{128,136,144,152,1..., dimensions={0} | all-to-all | bytes 524288 | tf_op jit(solution)/shard_map/all_to_all | solution.py:292
  115.8 0.7 copy.15
  (14 shorter events, 0.2 us)
Async XLA Ops:
  0.0 46.1 %copy-start = (s32[512,3]{0,1:T(4,128)S(1)}, s32[512,3]{0,1:T(4,128)}, u32[]{:S(2)}) copy-start(s32[512,3]{0,1:T(4,128)} %param.5) | copy-start | bytes 18436
  0.0 2.1 %copy-start.1 = (bf16[3,4,1024]{2,1,0:T(4,128)(2,1)S(1)}, bf16[3,4,1024]{2,1,0:T(4,128)(2,1)}, u32[]{:S(2)}) copy-start(bf16[3,4,1024]{2,1,0:T(4,128)(2,1)} %param.3) | copy-start | bytes 73732
  0.8 5.0 %collective-permute-start.5 = (bf16[3,4,512]{2,1,0:T(4,128)(2,1)S(1)}, bf16[3,4,512]{2,1,0:T(4,128)(2,1)S(1)}, u32[]{:S(2)}, u32[]{:S(2)}) collective-permute-start(bf16[3,4,512]{2,1,0:T(4,128)(2,1)S(1)} %slice.21), channel_id=1, source_target_pairs={{8,0},{16,8},{24,16},{32,24},{40,32},{48,40},{56,48},{64,56},{72,6... | collective-permute-start | bytes 36872 | tf_op jit(solution)/shard_map/ppermute | solution.py:271
  6.6 7.6 %copy-start.2 = (bf16[1,3,4,1536]{3,2,1,0:T(4,128)(2,1)S(1)}, bf16[1,3,4,1536]{3,2,1,0:T(4,128)(2,1)}, u32[]{:S(2)}) copy-start(bf16[1,3,4,1536]{3,2,1,0:T(4,128)(2,1)} %param.4) | copy-start | bytes 110596
  6.6 43.3 %all-to-all-start = ((bf16[8,144,128]{2,1,0:T(8,128)(2,1)}), bf16[8,144,128]{2,1,0:T(8,128)(2,1)S(1)}, u32[]{:S(2)}, u32[]{:S(2)}) async-start(bf16[8,144,128]{2,1,0:T(8,128)(2,1)} %broadcast_in_dim.6), calls=%async_computation | async-start | bytes 589824 | tf_op jit(solution)/shard_map/all_to_all | solution.py:239
  14.2 32.2 %collective-permute-start.1 = (bf16[1,3,4,1536]{3,2,1,0:T(4,128)(2,1)S(1)}, bf16[1,3,4,1536]{3,2,1,0:T(4,128)(2,1)S(1)}, u32[]{:S(2)}, u32[]{:S(2)}) collective-permute-start(bf16[1,3,4,1536]{3,2,1,0:T(4,128)(2,1)S(1)} %copy-done.2), channel_id=1, source_target_pairs={{0,256},{1,320},{2,384},{3,448},{4,0},{5,64},{6,128},{7,192},{8,26... | collective-permute-start | bytes 110600 | tf_op jit(solution)/shard_map/ppermute | solution.py:262
  31.0 15.3 %collective-permute-start = (bf16[1,3,4,1536]{3,2,1,0:T(4,128)(2,1)S(1)}, bf16[1,3,4,1536]{3,2,1,0:T(4,128)(2,1)S(1)}, u32[]{:S(2)}, u32[]{:S(2)}) collective-permute-start(bf16[1,3,4,1536]{3,2,1,0:T(4,128)(2,1)S(1)} %copy-done.2), channel_id=1, source_target_pairs={{0,0},{1,64},{2,128},{3,192},{4,256},{5,320},{6,384},{7,448},{8,8}... | collective-permute-start | bytes 110600 | tf_op jit(solution)/shard_map/ppermute | solution.py:262
  33.0 13.4 %collective-permute-start.3 = (bf16[1,3,4,1536]{3,2,1,0:T(4,128)(2,1)S(1)}, bf16[1,3,4,1536]{3,2,1,0:T(4,128)(2,1)S(1)}, u32[]{:S(2)}, u32[]{:S(2)}) collective-permute-start(bf16[1,3,4,1536]{3,2,1,0:T(4,128)(2,1)S(1)} %copy-done.2), channel_id=1, source_target_pairs={{0,384},{1,448},{2,256},{3,320},{4,128},{5,192},{6,0},{7,64},{8,39... | collective-permute-start | bytes 110600 | tf_op jit(solution)/shard_map/ppermute | solution.py:262
  38.7 8.6 %collective-permute-start.2 = (bf16[1,3,4,1536]{3,2,1,0:T(4,128)(2,1)S(1)}, bf16[1,3,4,1536]{3,2,1,0:T(4,128)(2,1)S(1)}, u32[]{:S(2)}, u32[]{:S(2)}) collective-permute-start(bf16[1,3,4,1536]{3,2,1,0:T(4,128)(2,1)S(1)} %copy-done.2), channel_id=1, source_target_pairs={{0,128},{1,192},{2,0},{3,64},{4,384},{5,448},{6,256},{7,320},{8,13... | collective-permute-start | bytes 110600 | tf_op jit(solution)/shard_map/ppermute | solution.py:262
  47.5 33.1 %collective-permute-start.4 = (bf16[4,3,4,1536]{3,2,1,0:T(4,128)(2,1)S(1)}, bf16[4,3,4,1536]{3,2,1,0:T(4,128)(2,1)S(1)}, u32[]{:S(2)}, u32[]{:S(2)}) collective-permute-start(bf16[4,3,4,1536]{3,2,1,0:T(4,128)(2,1)S(1)} %pad_maximum_fusion), channel_id=1, source_target_pairs={{0,64},{1,65},{2,66},{3,67},{4,68},{5,69},{6,70},{7,71},{8,72},{9,... | collective-permute-start | bytes 442376 | tf_op jit(solution)/shard_map/ppermute | solution.py:262
  51.2 24.0 %all-to-all-start.2 = ((bf16[8,6,72,128]{3,2,1,0:T(8,128)(2,1)}), bf16[8,6,72,128]{3,2,1,0:T(8,128)(2,1)S(1)}, u32[]{:S(2)}, u32[]{:S(2)}) async-start(bf16[8,6,72,128]{3,2,1,0:T(8,128)(2,1)} %broadcast_in_dim.8), calls=%async_computation.2 | async-start | bytes 1769472 | tf_op jit(solution)/shard_map/all_to_all | solution.py:239
  76.2 17.7 %all-to-all-start.1 = ((bf16[8,6,72,128]{3,2,1,0:T(8,128)(2,1)}), bf16[8,6,72,128]{3,2,1,0:T(8,128)(2,1)S(1)}, u32[]{:S(2)}, u32[]{:S(2)}) async-start(bf16[8,6,72,128]{3,2,1,0:T(8,128)(2,1)} %broadcast_in_dim.7), calls=%async_computation.1 | async-start | bytes 1769472 | tf_op jit(solution)/shard_map/all_to_all | solution.py:239

commit v4 on v3

--- a/solution.py
+++ b/solution.py
@@ -17,8 +17,9 @@
 
 def detect_kernel(
     first_station,
+    here,
+    padded,
     factor,
-    place_ref,
     groups_ref,
     templates_ref,
     series_ref,
@@ -27,6 +28,7 @@
     source,
     home,
     count,
+    wide,
     waves,
     norms,
     band,
@@ -41,11 +43,10 @@
 ):
     block, spread = groups_ref.shape
     n_group = series_ref.shape[0]
-    here = series_ref.shape[1] // 3
-    padded = series_ref.shape[2]
     rows = total.shape[1]
-    stations = templates_ref.shape[2]
-    slots = block * spread * stations
+    parts = 3 * L // LANES
+    slots = wide.shape[0] // parts
+    stations = slots // (block * spread)
     lane = lax.broadcasted_iota(jnp.int32, (1, LANES), 1)
     low = lane < HALF
 
@@ -58,20 +59,20 @@
     for n in range(n_group):
         count[n] = 0
     for r in range(block):
-        k = r ^ place_ref[0]
-        held = (k & 1) * 4 + (k & 2) + k // 4
         for i in range(spread):
             named = groups_ref[r, i]
             slot = named * SLOTS + count[named]
-            source[slot] = held * spread + i
+            source[slot] = r * spread + i
             home[slot] = r
             count[named] = count[named] + 1
     spare = waves.shape[0] - slots
+    for r in range(block):
+        each = slots // block * parts
+        wide[r * each : (r + 1) * each, :] = templates_ref[r, -each:, :].astype(jnp.float32)
     for c in range(3):
-        for n in range(block * spread):
-            part = templates_ref[n // spread, n % spread, :, c * L : (c + 1) * L]
-            at = n * stations
-            waves[at : at + stations, c * SPAN : c * SPAN + L] = part.astype(jnp.float32)
+        for v in range(L // LANES):
+            at = c * SPAN + v * LANES
+            waves[0:slots, at : at + LANES] = wide[pl.ds(c * L // LANES + v, slots, parts), :]
         waves[0:slots, c * SPAN + L : (c + 1) * SPAN] = jnp.zeros((slots, LANES), jnp.float32)
     waves[slots:, :] = jnp.zeros((spare, 3 * SPAN), jnp.float32)
     squares = jnp.sum(jnp.square(waves[0:slots, :]), axis=1, keepdims=True)
@@ -91,7 +92,8 @@
     def prepare(group, station, buffer):
         squares = jnp.zeros((padded, LANES), jnp.float32)
         for c in range(3):
-            plain = series_ref[group, c * here + station].astype(jnp.float32)
+            at = (c * here + station) * padded
+            plain = series_ref[group, at : at + padded, :].astype(jnp.float32)
             squares = squares + plain * plain
             shifts[c, 0, 0:padded, :] = plain
             after = shifts[c, 0, 1 : padded + 1, :]
@@ -173,16 +175,16 @@
         return
     for r in range(block):
         turned[:, r, :] = total[r] * factor
-    parts, _, samples = out_ref.shape
-    for w in range(parts):
+    n_out, _, samples = out_ref.shape
+    for w in range(n_out):
         for i in range(samples // LANES):
             out_ref[w, :, i * LANES : (i + 1) * LANES] = turned[w * (samples // LANES) + i]
 
 
-def detect(place, groups, templates, series, before, first_station, parts, factor):
-    n_group, channels, padded, _ = series.shape
+def detect(groups, templates, series, before, first_station, here, padded, parts, factor):
+    n_group = templates.shape[0]
     block, spread = groups.shape
-    stations = templates.shape[2]
+    stations = 4
     slots = block * spread * stations
     rows = padded - 8
     samples = rows * LANES // parts
@@ -191,17 +193,20 @@
         out_shape = jax.ShapeDtypeStruct((block + 1, rows, LANES), jnp.float32)
     else:
         out_shape = jax.ShapeDtypeStruct((parts, block, samples), jnp.float32)
-    operands = [place, groups, templates, series]
-    spaces = [pltpu.SMEM, pltpu.SMEM, pltpu.VMEM, pltpu.VMEM]
-    if before is not None:
-        operands.append(before)
-        spaces.append(pltpu.VMEM)
+    operands = [groups, templates]
+    spaces = [pltpu.SMEM, pltpu.VMEM]
+    for other in (series, before):
+        if other is not None:
+            operands.append(other)
+            spaces.append(pltpu.VMEM)
 
     def body(*refs):
         refs = list(refs)
+        if series is None:
+            refs.insert(2, refs[1])
         if before is None:
-            refs.insert(4, None)
-        detect_kernel(first_station, factor, *refs)
+            refs.insert(3, None)
+        detect_kernel(first_station, here, padded, factor, *refs)
 
     return pl.pallas_call(
         body,
@@ -212,6 +217,7 @@
             pltpu.SMEM((n_group * SLOTS,), jnp.int32),
             pltpu.SMEM((n_group * SLOTS,), jnp.int32),
             pltpu.SMEM((n_group,), jnp.int32),
+            pltpu.VMEM((slots * 3 * L // LANES, LANES), jnp.float32),
             pltpu.VMEM((spare, 3 * SPAN), jnp.float32),
             pltpu.VMEM((spare, LANES), jnp.float32),
             pltpu.VMEM((3 * LANES, LANES), jnp.bfloat16),
@@ -226,8 +232,8 @@
         ],
         compiler_params=pltpu.CompilerParams(vmem_limit_bytes=32 * 1024 * 1024),
         cost_estimate=pl.CostEstimate(
-            flops=8 * n_group * (channels // 3) * 2 * rows * 3 * SPAN * SLOTS * HALF,
-            bytes_accessed=series.size * 2 + templates.size * 2 + 4 * block * rows * LANES,
+            flops=16 * n_group * here * 2 * rows * 3 * SPAN * SLOTS * HALF,
+            bytes_accessed=templates.size * 2 + 4 * block * rows * LANES,
             transcendentals=0,
         ),
     )(*operands)
@@ -246,29 +252,21 @@
     n_a = n_sta
     n_b = n_tm // n_a
     near = [[a * n_b + b for b in range(n_b)] for a in range(n_a)]
-    far = [[a * n_b + b for a in range(n_a)] for b in range(n_b)]
+    far = [[a * n_b + b for a in range(o, n_a, 2)] for b in range(n_b) for o in range(2)]
     spread = template_groups.shape[1]
 
-    def device(a, b, t):
-        return (a * n_b + b) * n_sta + t
-
-    def carried(value, target):
-        pairs = [
-            (device(a, b, t), device(*target(a, b, t)))
-            for a in range(n_a)
-            for b in range(n_b)
-            for t in range(n_sta)
-        ]
-        return lax.ppermute(value, ("tm", "sta"), pairs)
-
-    near_ones = [carried(templates, lambda a, b, t: (t ^ k, b, a)) for k in (0, 4, 2, 6)]
-    held = jnp.concatenate(near_ones)
-    held = jnp.concatenate([held, carried(held, lambda a, b, t: (a ^ 1, b, t))])
-    place = (m // n_b).reshape(1)
+    own = templates.reshape(-1, LANES)
+    halo = lax.ppermute(record[:, :, :L], "tm", [(i + 1, i) for i in range(n_tm - 1)])
+    same = copies_to(own, "tm", far)
+    halo, same = lax.optimization_barrier((halo, same))
+    swap = [(a * n_b + b, (a ^ 1) * n_b + b) for a in range(n_a) for b in range(n_b)]
+    other = lax.ppermute(same, "tm", swap)
+    odd = lax.rem(m // n_b, 2) == 1
+    held = jnp.stack([jnp.where(odd, other, same), jnp.where(odd, same, other)], axis=1)
+    held = held.reshape((n_a,) + own.shape)
     first = (s * n_b + lax.rem(m, n_b)) * n_a
     groups = lax.dynamic_slice_in_dim(template_groups, first, n_a, 0)
 
-    halo = lax.ppermute(record[:, :, :L], "tm", [(i + 1, i) for i in range(n_tm - 1)])
     lines = channels * stations
     steps = samples // LANES
     piece = jnp.concatenate(
@@ -278,16 +276,22 @@
     main = around[:, : lines * steps].reshape(n_b, channels, stations, steps, LANES)
     tail = around[-1, lines * steps :].reshape(channels, stations, L // LANES, LANES)
     some = stations // 2
-    total = None
+    padded = n_b * steps + 8
+    flat = []
     for begin in range(0, stations, some):
         part = main[:, :, begin : begin + some].transpose(1, 2, 0, 3, 4)
         part = part.reshape(channels * some, n_b * steps, LANES)
         end = tail[:, begin : begin + some].reshape(channels * some, L // LANES, LANES)
         rest = jnp.zeros((channels * some, 8 - L // LANES, LANES), record.dtype)
-        series = copies_to(jnp.concatenate([part, end, rest], axis=1), "sta")
-        last = begin + some == stations
-        factor = math.sqrt(channels * L / (spread * stations)) if last else None
-        total = detect(place, groups, held, series, total, begin, n_b, factor)
+        part = jnp.concatenate([part, end, rest], axis=1).reshape(-1, LANES)
+        flat.append(jnp.broadcast_to(part[None], (n_sta,) + part.shape))
+    both = jnp.concatenate([flat[0], held], axis=1)
+    both = lax.all_to_all(both, "sta", 0, 0, tiled=True)
+    late, both = lax.optimization_barrier((flat[1], both))
+    late = lax.all_to_all(late, "sta", 0, 0, tiled=True)
+    factor = math.sqrt(channels * L / (spread * stations))
+    total = detect(groups, both, None, None, 0, some, padded, n_b, None)
+    total = detect(groups, both, late, total, some, some, padded, n_b, factor)
 
     found = lax.all_to_all(total, "tm", 0, 0, axis_index_groups=near, tiled=True)
     return found.reshape(n_b * n_a, samples)

time: 118 us -> 113 us (0.958)
  starting transfers between devices: 58.1 us -> 39.8 us
  waiting for transfers between devices: 21 us -> 34.4 us
  blocking collectives: 11.6 us -> 10.2 us
    ppermute x5 -> x1, starting transfers between devices: 34.3 us -> 2.67 us  [on_device(): other = lax.ppermute(same, 'tm', swap)]
    all_to_all x0 -> x2, waiting for transfers between devices: none -> 19.5 us  [the longest x1 16.3 us: on_device(): both = lax.all_to_all(both, 'sta', 0, 0, tiled=True)]
    all_to_all x0 -> x2, starting transfers between devices: none -> 13.9 us  [the longest x1 9.6 us: on_device(): both = lax.all_to_all(both, 'sta', 0, 0, tiled=True)]
    all_to_all x3 -> x2, waiting for transfers between devices: 16.3 us -> 7.53 us  [copies_to(): lax.all_to_all(spread, axis, 0, 0, axis_index_groups=groups, tiled=True)]
    ppermute x5 -> x1, waiting for transfers between devices: 1 us -> 4.93 us  [on_device(): other = lax.ppermute(same, 'tm', swap)]
    all_to_all x1, blocking collectives: 11.6 us -> 10.2 us  [on_device(): lax.all_to_all(total, 'tm', 0, 0, axis_index_groups=near, tiled=True)]
    ppermute x1, waiting for transfers between devices: 3.69 us -> 2.38 us  [on_device(): lax.ppermute(record[:, :, :L], 'tm', [(i + 1, i) for i in range(n_tm - 1)])]
    all_to_all x3 -> x2, starting transfers between devices: 22.6 us -> 22 us  [copies_to(): lax.all_to_all(spread, axis, 0, 0, axis_index_groups=groups, tiled=True)]
  transfers between devices with their start and end apart: 9 -> 6, of which waited for: 4 -> 5; matrix products, arithmetic and copies ran while one was open for 2% -> 2% of each run, Pallas kernels for 9% -> 9%
where the time goes in v4:
time: 113 us; the launch traced here: 112 us
  starting transfers between devices  39.8 us (35%)
  waiting for transfers between devices  34.4 us (30%)
  Pallas kernels  20.5 us (18%)
  blocking collectives  10.2 us (9%)
  local copies, waits for them, and re-layouts  5.87 us (5%)
  other arithmetic  1.29 us (1%)
    all_to_all x2, starting transfers between devices, copies_to(): lax.all_to_all(spread, axis, 0, 0, axis_index_groups=groups, tiled=True)  22 us
    pallas_call x2, Pallas kernels, detect(): pl.pallas_call(body, out_shape=out_shape, in_specs=[pl.BlockSpec(memory_s...  20.5 us
    all_to_all x1, waiting for transfers between devices, on_device(): both = lax.all_to_all(both, 'sta', 0, 0, tiled=True)  16.3 us
    all_to_all x1, blocking collectives, on_device(): lax.all_to_all(total, 'tm', 0, 0, axis_index_groups=near, tiled=True)  10.2 us
    all_to_all x1, starting transfers between devices, on_device(): both = lax.all_to_all(both, 'sta', 0, 0, tiled=True)  9.6 us
    all_to_all x2, waiting for transfers between devices, copies_to(): lax.all_to_all(spread, axis, 0, 0, axis_index_groups=groups, tiled=True)  7.53 us
    ppermute x1, waiting for transfers between devices, on_device(): other = lax.ppermute(same, 'tm', swap)  4.93 us
    all_to_all x1, starting transfers between devices, on_device(): late = lax.all_to_all(late, 'sta', 0, 0, tiled=True)  4.32 us
  transfers between devices with their start and end apart: 6, of which 5 were waited for; matrix products, arithmetic and copies ran while one was open for 2% of the time, Pallas kernels for 9%

profile of v4, /device:TPU:1, one launch (start us, length us, event | category | flops | bytes accessed | tf_op | source)
XLA Modules:
  0.0 112.2 jit_solution(17197426772707613492)
XLA Ops:
  0.0 0.0 copy-start
  0.0 0.8 broadcast_in_dim.27
  0.8 0.7 broadcast_in_dim.28
  1.5 15.6 %all-to-all-start = ((bf16[4,144,128]{2,1,0:T(8,128)(2,1)}), bf16[4,144,128]{2,1,0:T(8,128)(2,1)S(1)}, u32[]{:S(2)}, u32[]{:S(2)}) async-start(bf16[4,144,128]{2,1,0:T(8,128)(2,1)} %broadcast_in_dim.28), calls=%async_computation | async-start | bytes 294912 | tf_op jit(solution)/shard_map/all_to_all | solution.py:245
  17.1 0.7 slice.21
  17.8 1.3 %collective-permute-start = (bf16[3,4,512]{2,1,0:T(4,128)(2,1)S(1)}, bf16[3,4,512]{2,1,0:T(4,128)(2,1)S(1)}, u32[]{:S(2)}, u32[]{:S(2)}) collective-permute-start(bf16[3,4,512]{2,1,0:T(4,128)(2,1)S(1)} %slice.21), channel_id=1, source_target_pairs={{8,0},{16,8},{24,16},{32,24},{40,32},{48,40},{56,48},{64,56},{72,6... | collective-permute-start | bytes 36872 | tf_op jit(solution)/shard_map/ppermute | solution.py:259
  19.1 0.8 reshape.31
  19.9 2.4 %collective-permute-done = bf16[3,4,512]{2,1,0:T(4,128)(2,1)S(1)} collective-permute-done((bf16[3,4,512]{2,1,0:T(4,128)(2,1)S(1)}, bf16[3,4,512]{2,1,0:T(4,128)(2,1)S(1)}, u32[]{:S(2)}, u32[]{:S(2)}) %collective-permute-start) | collective-permute-done | bytes 12320 | tf_op jit(solution)/shard_map/ppermute | solution.py:259
  22.3 7.5 %all-to-all-done = bf16[4,144,128]{2,1,0:T(8,128)(2,1)S(1)} async-done(((bf16[4,144,128]{2,1,0:T(8,128)(2,1)}), bf16[4,144,128]{2,1,0:T(8,128)(2,1)S(1)}, u32[]{:S(2)}, u32[]{:S(2)}) %all-to-all-start) | async-done | bytes 147488 | tf_op jit(solution)/shard_map/all_to_all | solution.py:245
  29.8 0.7 broadcast_in_dim.29
  30.6 6.3 %all-to-all-start.1 = ((bf16[8,144,128]{2,1,0:T(8,128)(2,1)}), bf16[8,144,128]{2,1,0:T(8,128)(2,1)S(1)}, u32[]{:S(2)}, u32[]{:S(2)}) async-start(bf16[8,144,128]{2,1,0:T(8,128)(2,1)} %broadcast_in_dim.29), calls=%async_computation.1 | async-start | bytes 589824 | tf_op jit(solution)/shard_map/all_to_all | solution.py:245
  36.9 2.7 %collective-permute-start.1 = (bf16[4,144,128]{2,1,0:T(8,128)(2,1)S(1)}, bf16[4,144,128]{2,1,0:T(8,128)(2,1)S(1)}, u32[]{:S(2)}, u32[]{:S(2)}) collective-permute-start(bf16[4,144,128]{2,1,0:T(8,128)(2,1)S(1)} %all-to-all-done), channel_id=1, source_target_pairs={{0,64},{8,72},{16,80},{24,88},{32,96},{40,104},{48,112},{56,120},{... | collective-permute-start | bytes 442376 | tf_op jit(solution)/shard_map/ppermute | solution.py:263
  39.6 0.1 pad.9.clone
  39.7 4.9 %collective-permute-done.1 = bf16[4,144,128]{2,1,0:T(8,128)(2,1)S(1)} collective-permute-done((bf16[4,144,128]{2,1,0:T(8,128)(2,1)S(1)}, bf16[4,144,128]{2,1,0:T(8,128)(2,1)S(1)}, u32[]{:S(2)}, u32[]{:S(2)}) %collective-permute-start.1) | collective-permute-done | bytes 147488 | tf_op jit(solution)/shard_map/ppermute | solution.py:263
  44.7 0.0 all-to-all-done.1
  44.8 0.1 maximum_maximum_fusion.1
  44.9 0.1 broadcast_in_dim.33
  45.0 1.1 pad_maximum_fusion
  46.2 9.6 %all-to-all-start.2 = ((bf16[8,576,128]{2,1,0:T(8,128)(2,1)}), bf16[8,576,128]{2,1,0:T(8,128)(2,1)S(1)}, u32[]{:S(2)}, u32[]{:S(2)}) async-start(bf16[8,576,128]{2,1,0:T(8,128)(2,1)} %pad_maximum_fusion), calls=%async_computation.2 | async-start | bytes 2359296 | tf_op jit(solution)/shard_map/all_to_all | solution.py:289
  55.8 0.0 copy-done
  55.8 0.1 constant_dynamic-slice_fusion
  55.8 0.1 copy.12.refs_0_
  55.9 16.3 %all-to-all-done.2.refs_1_ = bf16[8,576,128]{2,1,0:T(8,128)(2,1)S(1)} async-done(((bf16[8,576,128]{2,1,0:T(8,128)(2,1)}), bf16[8,576,128]{2,1,0:T(8,128)(2,1)S(1)}, u32[]{:S(2)}, u32[]{:S(2)}) %all-to-all-start.2) | async-done | bytes 1179680 | tf_op jit(solution)/shard_map/all_to_all | solution.py:289
  72.3 1.0 broadcast_in_dim.31
  73.3 4.3 %all-to-all-start.3 = ((bf16[8,432,128]{2,1,0:T(8,128)(2,1)}), bf16[8,432,128]{2,1,0:T(8,128)(2,1)S(1)}, u32[]{:S(2)}, u32[]{:S(2)}) async-start(bf16[8,432,128]{2,1,0:T(8,128)(2,1)} %broadcast_in_dim.31), calls=%async_computation.3 | async-start | bytes 1769472 | tf_op jit(solution)/shard_map/all_to_all | solution.py:291
  77.6 10.2 %shard_map.37.refs_3_ = f32[9,64,128]{2,1,0:T(8,128)S(1)} custom-call(s32[8,3]{1,0:T(8,128)S(1)} %copy.12.refs_0_, bf16[8,576,128]{2,1,0:T(8,128)(2,1)S(1)} %all-to-all-done.2.refs_1_), custom_call_target="tpu_custom_call" | custom-call | flops 16106127360 | bytes 1441792 | tf_op jit(solution)/shard_map/pallas_call | solution.py:211
  87.8 3.2 %all-to-all-done.3.refs_2_ = bf16[8,432,128]{2,1,0:T(8,128)(2,1)S(1)} async-done(((bf16[8,432,128]{2,1,0:T(8,128)(2,1)}), bf16[8,432,128]{2,1,0:T(8,128)(2,1)S(1)}, u32[]{:S(2)}, u32[]{:S(2)}) %all-to-all-start.3) | async-done | bytes 884768 | tf_op jit(solution)/shard_map/all_to_all | solution.py:291
  91.0 10.3 %shard_map.38 = f32[8,8,1024]{2,1,0:T(8,128)S(1)} custom-call(s32[8,3]{1,0:T(8,128)S(1)} %copy.12.refs_0_, bf16[8,576,128]{2,1,0:T(8,128)(2,1)S(1)} %all-to-all-done.2.refs_1_, bf16[8,432,128]{2,1,0:T(8,128)(2,1)S(1)} %all-to-all-done.3.refs_2_, f32[9,64,128]{2,1,0:T(8,128)S(1)} %shard_map.37.refs_3_), custom_call_target="tpu_custom_call" | custom-call | flops 16106127360 | bytes 1441792 | tf_op jit(solution)/shard_map/pallas_call | solution.py:211
  101.3 10.2 %all_to_all.25 = f32[8,8,1024]{2,1,0:T(8,128)S(1)} all-to-all(f32[8,8,1024]{2,1,0:T(8,128)S(1)} %shard_map.38), channel_id=1, replica_groups={{0,8,16,24,32,40,48,56},{64,72,80,88,96,104,112,120},{128,136,144,152,1..., dimensions={0} | all-to-all | bytes 524288 | tf_op jit(solution)/shard_map/all_to_all | solution.py:296
  111.5 0.7 copy.14
  (11 shorter events, 0.2 us)
Async XLA Ops:
  0.0 55.8 %copy-start = (s32[512,3]{0,1:T(4,128)S(1)}, s32[512,3]{0,1:T(4,128)}, u32[]{:S(2)}) copy-start(s32[512,3]{0,1:T(4,128)} %param.5) | copy-start | bytes 18436
  1.5 28.3 %all-to-all-start = ((bf16[4,144,128]{2,1,0:T(8,128)(2,1)}), bf16[4,144,128]{2,1,0:T(8,128)(2,1)S(1)}, u32[]{:S(2)}, u32[]{:S(2)}) async-start(bf16[4,144,128]{2,1,0:T(8,128)(2,1)} %broadcast_in_dim.28), calls=%async_computation | async-start | bytes 294912 | tf_op jit(solution)/shard_map/all_to_all | solution.py:245
  17.8 4.4 %collective-permute-start = (bf16[3,4,512]{2,1,0:T(4,128)(2,1)S(1)}, bf16[3,4,512]{2,1,0:T(4,128)(2,1)S(1)}, u32[]{:S(2)}, u32[]{:S(2)}) collective-permute-start(bf16[3,4,512]{2,1,0:T(4,128)(2,1)S(1)} %slice.21), channel_id=1, source_target_pairs={{8,0},{16,8},{24,16},{32,24},{40,32},{48,40},{56,48},{64,56},{72,6... | collective-permute-start | bytes 36872 | tf_op jit(solution)/shard_map/ppermute | solution.py:259
  30.6 14.1 %all-to-all-start.1 = ((bf16[8,144,128]{2,1,0:T(8,128)(2,1)}), bf16[8,144,128]{2,1,0:T(8,128)(2,1)S(1)}, u32[]{:S(2)}, u32[]{:S(2)}) async-start(bf16[8,144,128]{2,1,0:T(8,128)(2,1)} %broadcast_in_dim.29), calls=%async_computation.1 | async-start | bytes 589824 | tf_op jit(solution)/shard_map/all_to_all | solution.py:245
  36.9 7.7 %collective-permute-start.1 = (bf16[4,144,128]{2,1,0:T(8,128)(2,1)S(1)}, bf16[4,144,128]{2,1,0:T(8,128)(2,1)S(1)}, u32[]{:S(2)}, u32[]{:S(2)}) collective-permute-start(bf16[4,144,128]{2,1,0:T(8,128)(2,1)S(1)} %all-to-all-done), channel_id=1, source_target_pairs={{0,64},{8,72},{16,80},{24,88},{32,96},{40,104},{48,112},{56,120},{... | collective-permute-start | bytes 442376 | tf_op jit(solution)/shard_map/ppermute | solution.py:263
  46.2 26.1 %all-to-all-start.2 = ((bf16[8,576,128]{2,1,0:T(8,128)(2,1)}), bf16[8,576,128]{2,1,0:T(8,128)(2,1)S(1)}, u32[]{:S(2)}, u32[]{:S(2)}) async-start(bf16[8,576,128]{2,1,0:T(8,128)(2,1)} %pad_maximum_fusion), calls=%async_computation.2 | async-start | bytes 2359296 | tf_op jit(solution)/shard_map/all_to_all | solution.py:289
  73.3 17.7 %all-to-all-start.3 = ((bf16[8,432,128]{2,1,0:T(8,128)(2,1)}), bf16[8,432,128]{2,1,0:T(8,128)(2,1)S(1)}, u32[]{:S(2)}, u32[]{:S(2)}) async-start(bf16[8,432,128]{2,1,0:T(8,128)(2,1)} %broadcast_in_dim.31), calls=%async_computation.3 | async-start | bytes 1769472 | tf_op jit(solution)/shard_map/all_to_all | solution.py:291

commit v5 on v4

--- a/solution.py
+++ b/solution.py
@@ -16,18 +16,18 @@
 
 
 def detect_kernel(
-    first_station,
-    here,
     padded,
     factor,
+    order_ref,
     groups_ref,
     templates_ref,
-    series_ref,
+    pieces_refs,
     before_ref,
     out_ref,
     source,
     home,
     count,
+    series,
     wide,
     waves,
     norms,
@@ -42,7 +42,7 @@
     turned,
 ):
     block, spread = groups_ref.shape
-    n_group = series_ref.shape[0]
+    n_group = len(pieces_refs)
     rows = total.shape[1]
     parts = 3 * L // LANES
     slots = wide.shape[0] // parts
@@ -56,8 +56,10 @@
         return carry
 
     lax.fori_loop(0, source.shape[0], clear, 0)
+    for n in range(count.shape[0]):
+        count[n] = 0
     for n in range(n_group):
-        count[n] = 0
+        series[n] = pieces_refs[n][...]
     for r in range(block):
         for i in range(spread):
             named = groups_ref[r, i]
@@ -92,8 +94,8 @@
     def prepare(group, station, buffer):
         squares = jnp.zeros((padded, LANES), jnp.float32)
         for c in range(3):
-            at = (c * here + station) * padded
-            plain = series_ref[group, at : at + padded, :].astype(jnp.float32)
+            at = (c * stations + station) * padded
+            plain = series[group, at : at + padded, :].astype(jnp.float32)
             squares = squares + plain * plain
             shifts[c, 0, 0:padded, :] = plain
             after = shifts[c, 0, 1 : padded + 1, :]
@@ -110,7 +112,7 @@
         scales[buffer, 0] = jnp.where(low, scale, other)
         scales[buffer, 1] = jnp.where(low, other, scale)
         for j in range(SLOTS):
-            row = source[group * SLOTS + j] * stations + first_station + station
+            row = source[order_ref[group] * SLOTS + j] * stations + station
             for c in range(3):
                 wave = waves[pl.ds(row, 1), c * SPAN : (c + 1) * SPAN]
                 moved = pltpu.roll(
@@ -136,7 +138,7 @@
         )
         weight = []
         for j in range(SLOTS):
-            row = source[group * SLOTS + j] * stations + first_station + station
+            row = source[order_ref[group] * SLOTS + j] * stations + station
             weight.append(norms[pl.ds(row, 1), :])
         for p in range(SLOTS // 2):
             both = jnp.where(low, weight[2 * p], weight[2 * p + 1])
@@ -150,8 +152,8 @@
 
     def group_term(group, carry):
         later = lax.min(group + 1, n_group - 1)
-        for station in range(here):
-            if station < here - 1:
+        for station in range(stations):
+            if station < stations - 1:
                 prepare(group, station + 1, (station + 1) % 2)
             else:
                 prepare(later, 0, (station + 1) % 2)
@@ -164,7 +166,7 @@
                 whole = jnp.where(low, first, pltpu.roll(second, HALF, 1))
             else:
                 whole = jnp.where(low, pltpu.roll(first, HALF, 1), second)
-            r = home[group * SLOTS + j]
+            r = home[order_ref[group] * SLOTS + j]
             total[r] = total[r] + whole
         return carry
 
@@ -181,8 +183,7 @@
             out_ref[w, :, i * LANES : (i + 1) * LANES] = turned[w * (samples // LANES) + i]
 
 
-def detect(groups, templates, series, before, first_station, here, padded, parts, factor):
-    n_group = templates.shape[0]
+def detect(order, groups, templates, pieces, before, n_all, padded, parts, factor):
     block, spread = groups.shape
     stations = 4
     slots = block * spread * stations
@@ -193,20 +194,17 @@
         out_shape = jax.ShapeDtypeStruct((block + 1, rows, LANES), jnp.float32)
     else:
         out_shape = jax.ShapeDtypeStruct((parts, block, samples), jnp.float32)
-    operands = [groups, templates]
-    spaces = [pltpu.SMEM, pltpu.VMEM]
-    for other in (series, before):
-        if other is not None:
-            operands.append(other)
-            spaces.append(pltpu.VMEM)
+    operands = [order, groups, templates, *pieces]
+    spaces = [pltpu.SMEM, pltpu.SMEM] + [pltpu.VMEM] * (1 + len(pieces))
+    if before is not None:
+        operands.append(before)
+        spaces.append(pltpu.VMEM)
 
     def body(*refs):
-        refs = list(refs)
-        if series is None:
-            refs.insert(2, refs[1])
-        if before is None:
-            refs.insert(3, None)
-        detect_kernel(first_station, here, padded, factor, *refs)
+        end = 3 + len(pieces)
+        taken = refs[end] if before is not None else None
+        rest = refs[end + (before is not None) :]
+        detect_kernel(padded, factor, *refs[:3], refs[3:end], taken, *rest)
 
     return pl.pallas_call(
         body,
@@ -214,9 +212,10 @@
         in_specs=[pl.BlockSpec(memory_space=space) for space in spaces],
         out_specs=pl.BlockSpec(memory_space=pltpu.VMEM),
         scratch_shapes=[
-            pltpu.SMEM((n_group * SLOTS,), jnp.int32),
-            pltpu.SMEM((n_group * SLOTS,), jnp.int32),
-            pltpu.SMEM((n_group,), jnp.int32),
+            pltpu.SMEM((n_all * SLOTS,), jnp.int32),
+            pltpu.SMEM((n_all * SLOTS,), jnp.int32),
+            pltpu.SMEM((n_all,), jnp.int32),
+            pltpu.VMEM((len(pieces),) + pieces[0].shape, jnp.bfloat16),
             pltpu.VMEM((slots * 3 * L // LANES, LANES), jnp.float32),
             pltpu.VMEM((spare, 3 * SPAN), jnp.float32),
             pltpu.VMEM((spare, LANES), jnp.float32),
@@ -232,7 +231,7 @@
         ],
         compiler_params=pltpu.CompilerParams(vmem_limit_bytes=32 * 1024 * 1024),
         cost_estimate=pl.CostEstimate(
-            flops=16 * n_group * here * 2 * rows * 3 * SPAN * SLOTS * HALF,
+            flops=16 * len(pieces) * stations * 2 * rows * 3 * SPAN * SLOTS * HALF,
             bytes_accessed=templates.size * 2 + 4 * block * rows * LANES,
             transcendentals=0,
         ),
@@ -252,18 +251,17 @@
     n_a = n_sta
     n_b = n_tm // n_a
     near = [[a * n_b + b for b in range(n_b)] for a in range(n_a)]
-    far = [[a * n_b + b for a in range(o, n_a, 2)] for b in range(n_b) for o in range(2)]
+    far = [[a * n_b + b for a in range(n_a)] for b in range(n_b)]
     spread = template_groups.shape[1]
 
-    own = templates.reshape(-1, LANES)
+    turn = [
+        ((a * n_b + b) * n_sta + t, (t * n_b + b) * n_sta + a)
+        for a in range(n_a)
+        for b in range(n_b)
+        for t in range(n_sta)
+    ]
     halo = lax.ppermute(record[:, :, :L], "tm", [(i + 1, i) for i in range(n_tm - 1)])
-    same = copies_to(own, "tm", far)
-    halo, same = lax.optimization_barrier((halo, same))
-    swap = [(a * n_b + b, (a ^ 1) * n_b + b) for a in range(n_a) for b in range(n_b)]
-    other = lax.ppermute(same, "tm", swap)
-    odd = lax.rem(m // n_b, 2) == 1
-    held = jnp.stack([jnp.where(odd, other, same), jnp.where(odd, same, other)], axis=1)
-    held = held.reshape((n_a,) + own.shape)
+    own = lax.ppermute(templates.reshape(-1, LANES), ("tm", "sta"), turn)
     first = (s * n_b + lax.rem(m, n_b)) * n_a
     groups = lax.dynamic_slice_in_dim(template_groups, first, n_a, 0)
 
@@ -273,25 +271,28 @@
         [record.reshape(lines * steps, LANES), halo.reshape(lines * (L // LANES), LANES)]
     )
     around = copies_to(piece, "tm", near)
-    main = around[:, : lines * steps].reshape(n_b, channels, stations, steps, LANES)
-    tail = around[-1, lines * steps :].reshape(channels, stations, L // LANES, LANES)
-    some = stations // 2
+    around, own = lax.optimization_barrier((around, own))
+    block = copies_to(own, "tm", far)
+    main = around[:, : lines * steps].reshape(n_b, lines, steps, LANES)
+    main = main.transpose(1, 0, 2, 3).reshape(lines, n_b * steps, LANES)
+    tail = around[-1, lines * steps :].reshape(lines, L // LANES, LANES)
+    rest = jnp.zeros((lines, 8 - L // LANES, LANES), record.dtype)
     padded = n_b * steps + 8
-    flat = []
-    for begin in range(0, stations, some):
-        part = main[:, :, begin : begin + some].transpose(1, 2, 0, 3, 4)
-        part = part.reshape(channels * some, n_b * steps, LANES)
-        end = tail[:, begin : begin + some].reshape(channels * some, L // LANES, LANES)
-        rest = jnp.zeros((channels * some, 8 - L // LANES, LANES), record.dtype)
-        part = jnp.concatenate([part, end, rest], axis=1).reshape(-1, LANES)
-        flat.append(jnp.broadcast_to(part[None], (n_sta,) + part.shape))
-    both = jnp.concatenate([flat[0], held], axis=1)
-    both = lax.all_to_all(both, "sta", 0, 0, tiled=True)
-    late, both = lax.optimization_barrier((flat[1], both))
-    late = lax.all_to_all(late, "sta", 0, 0, tiled=True)
+    mine = jnp.concatenate([main, tail, rest], axis=1).reshape(-1, LANES)
+
+    cores = 2
+    n_y = n_sta // cores
+    y, core = s // cores, lax.rem(s, cores)
+    pieces = [mine]
+    for k in range(1, n_y):
+        pairs = [(t, (t + k * cores) % n_sta) for t in range(n_sta)]
+        pieces.append(lax.ppermute(mine, "sta", pairs))
+    swap = [(t, t ^ 1) for t in range(n_sta)]
+    others = [lax.ppermute(value, "sta", swap) for value in pieces]
+    rows_of_y = lax.rem(y - jnp.arange(n_y, dtype=jnp.int32) + n_y, n_y) * cores
     factor = math.sqrt(channels * L / (spread * stations))
-    total = detect(groups, both, None, None, 0, some, padded, n_b, None)
-    total = detect(groups, both, late, total, some, some, padded, n_b, factor)
+    total = detect(rows_of_y + core, groups, block, pieces, None, n_sta, padded, n_b, None)
+    total = detect(rows_of_y + 1 - core, groups, block, others, total, n_sta, padded, n_b, factor)
 
     found = lax.all_to_all(total, "tm", 0, 0, axis_index_groups=near, tiled=True)
     return found.reshape(n_b * n_a, samples)

time: 113 us -> 98.8 us (0.87)
  waiting for transfers between devices: 34.4 us -> 5.59 us
  starting transfers between devices: 39.8 us -> 59.4 us
  local copies, waits for them, and re-layouts: 5.87 us -> 3.34 us
  Pallas kernels: 20.5 us -> 18.2 us
  other arithmetic: 1.29 us -> 0.13 us
    ppermute x1 -> x8, starting transfers between devices: 2.67 us -> 30.3 us  [the longest x4 13.8 us: on_device(): others = [lax.ppermute(value, 'sta', swap) for value in pieces]]
    all_to_all x2 -> x0, waiting for transfers between devices: 19.5 us -> none  [the longest x1 16.3 us: on_device(): both = lax.all_to_all(both, 'sta', 0, 0, tiled=True)]
    all_to_all x2 -> x0, starting transfers between devices: 13.9 us -> none  [the longest x1 9.6 us: on_device(): both = lax.all_to_all(both, 'sta', 0, 0, tiled=True)]
    all_to_all x2, waiting for transfers between devices: 7.53 us -> 0.01 us  [copies_to(): lax.all_to_all(spread, axis, 0, 0, axis_index_groups=groups, tiled=True)]
    all_to_all x2, starting transfers between devices: 22 us -> 27.9 us  [copies_to(): lax.all_to_all(spread, axis, 0, 0, axis_index_groups=groups, tiled=True)]
    ppermute x1 -> x8, waiting for transfers between devices: 4.93 us -> 1.89 us  [the longest x1 1.88 us: on_device(): own = lax.ppermute(templates.reshape(-1, LANES), ('tm', 'sta'), turn)]
    pallas_call x2, Pallas kernels: 20.5 us -> 18.2 us  [detect(): pl.pallas_call(body, out_shape=out_shape, in_specs=[pl.BlockSpec(memory_s...]
    ppermute x1, waiting for transfers between devices: 2.38 us -> 3.69 us  [on_device(): lax.ppermute(record[:, :, :L], 'tm', [(i + 1, i) for i in range(n_tm - 1)])]
  transfers between devices with their start and end apart: 6 -> 11, of which waited for: 5 -> 2; matrix products, arithmetic and copies ran while one was open for 2% -> 0% of each run, Pallas kernels for 9% -> 9%
where the time goes in v5:
time: 98.8 us; the launch traced here: 98.1 us
  starting transfers between devices  59.4 us (60%)
  Pallas kernels  18.2 us (18%)
  blocking collectives  11.2 us (11%)
  waiting for transfers between devices  5.59 us (6%)
  local copies, waits for them, and re-layouts  3.34 us (3%)
    all_to_all x2, starting transfers between devices, copies_to(): lax.all_to_all(spread, axis, 0, 0, axis_index_groups=groups, tiled=True)  27.9 us
    pallas_call x2, Pallas kernels, detect(): pl.pallas_call(body, out_shape=out_shape, in_specs=[pl.BlockSpec(memory_s...  18.2 us
    ppermute x4, starting transfers between devices, on_device(): others = [lax.ppermute(value, 'sta', swap) for value in pieces]  13.8 us
    all_to_all x1, blocking collectives, on_device(): lax.all_to_all(total, 'tm', 0, 0, axis_index_groups=near, tiled=True)  11.2 us
    ppermute x3, starting transfers between devices, on_device(): pieces.append(lax.ppermute(mine, 'sta', pairs))  8.41 us
    ppermute x1, starting transfers between devices, on_device(): own = lax.ppermute(templates.reshape(-1, LANES), ('tm', 'sta'), turn)  8.1 us
    ppermute x1, waiting for transfers between devices, on_device(): lax.ppermute(record[:, :, :L], 'tm', [(i + 1, i) for i in range(n_tm - 1)])  3.69 us
  transfers between devices with their start and end apart: 11, of which 2 were waited for; matrix products, arithmetic and copies ran while one was open for 0% of the time, Pallas kernels for 9%

profile of v5, /device:TPU:1, one launch (start us, length us, event | category | flops | bytes accessed | tf_op | source)
XLA Modules:
  0.0 98.1 jit_solution(7332244661073363990)
XLA Ops:
  0.0 0.0 copy-start
  0.0 0.0 copy-start.1
  0.0 0.8 slice.9
  0.8 1.3 %collective-permute-start = (bf16[3,4,512]{2,1,0:T(4,128)(2,1)S(1)}, bf16[3,4,512]{2,1,0:T(4,128)(2,1)S(1)}, u32[]{:S(2)}, u32[]{:S(2)}) collective-permute-start(bf16[3,4,512]{2,1,0:T(4,128)(2,1)S(1)} %slice.9), channel_id=1, source_target_pairs={{8,0},{16,8},{24,16},{32,24},{40,32},{48,40},{56,48},{64,56},{72,6... | collective-permute-start | bytes 36872 | tf_op jit(solution)/shard_map/ppermute | solution.py:263
  2.1 0.0 copy-done.1
  2.1 3.7 %collective-permute-done = bf16[3,4,512]{2,1,0:T(4,128)(2,1)S(1)} collective-permute-done((bf16[3,4,512]{2,1,0:T(4,128)(2,1)S(1)}, bf16[3,4,512]{2,1,0:T(4,128)(2,1)S(1)}, u32[]{:S(2)}, u32[]{:S(2)}) %collective-permute-start) | collective-permute-done | bytes 12320 | tf_op jit(solution)/shard_map/ppermute | solution.py:263
  5.8 0.8 broadcast_in_dim.6
  6.6 0.0 copy-start.2
  6.6 7.6 %all-to-all-start = ((bf16[8,144,128]{2,1,0:T(8,128)(2,1)}), bf16[8,144,128]{2,1,0:T(8,128)(2,1)S(1)}, u32[]{:S(2)}, u32[]{:S(2)}) async-start(bf16[8,144,128]{2,1,0:T(8,128)(2,1)} %broadcast_in_dim.6), calls=%async_computation | async-start | bytes 589824 | tf_op jit(solution)/shard_map/all_to_all | solution.py:244
  14.2 0.0 copy-done.2
  14.2 8.1 %collective-permute-start.1 = (bf16[144,128]{1,0:T(8,128)(2,1)S(1)}, bf16[144,128]{1,0:T(8,128)(2,1)S(1)}, u32[]{:S(2)}, u32[]{:S(2)}) collective-permute-start(bf16[144,128]{1,0:T(8,128)(2,1)S(1)} %reshape.25), channel_id=1, source_target_pairs={{0,0},{1,64},{2,128},{3,192},{4,256},{5,320},{6,384},{7,448},{8,8}... | collective-permute-start | bytes 110600 | tf_op jit(solution)/shard_map/ppermute | solution.py:264
  22.3 1.9 %collective-permute-done.1 = bf16[144,128]{1,0:T(8,128)(2,1)S(1)} collective-permute-done((bf16[144,128]{1,0:T(8,128)(2,1)S(1)}, bf16[144,128]{1,0:T(8,128)(2,1)S(1)}, u32[]{:S(2)}, u32[]{:S(2)}) %collective-permute-start.1) | collective-permute-done | bytes 36896 | tf_op jit(solution)/shard_map/ppermute | solution.py:264
  24.2 0.0 all-to-all-done
  24.2 0.8 broadcast_in_dim.7
  24.9 20.3 %all-to-all-start.1 = ((bf16[8,144,128]{2,1,0:T(8,128)(2,1)}), bf16[8,144,128]{2,1,0:T(8,128)(2,1)S(1)}, u32[]{:S(2)}, u32[]{:S(2)}) async-start(bf16[8,144,128]{2,1,0:T(8,128)(2,1)} %broadcast_in_dim.7), calls=%async_computation.1 | async-start | bytes 589824 | tf_op jit(solution)/shard_map/all_to_all | solution.py:244
  45.2 0.1 pad.2.clone
  45.4 0.1 maximum_maximum_fusion
  45.5 1.9 %collective-permute-start.3 = (bf16[864,128]{1,0:T(8,128)(2,1)S(1)}, bf16[864,128]{1,0:T(8,128)(2,1)S(1)}, u32[]{:S(2)}, u32[]{:S(2)}) collective-permute-start(bf16[864,128]{1,0:T(8,128)(2,1)S(1)} %bitcast.10), channel_id=1, source_target_pairs={{0,2},{1,3},{2,4},{3,5},{4,6},{5,7},{6,0},{7,1},{8,10},{9,11},{10,... | collective-permute-start | bytes 663560 | tf_op jit(solution)/shard_map/ppermute | solution.py:289
  47.4 3.5 %collective-permute-start.5 = (bf16[864,128]{1,0:T(8,128)(2,1)S(1)}, bf16[864,128]{1,0:T(8,128)(2,1)S(1)}, u32[]{:S(2)}, u32[]{:S(2)}) collective-permute-start(bf16[864,128]{1,0:T(8,128)(2,1)S(1)} %bitcast.11), channel_id=1, source_target_pairs={{0,4},{1,5},{2,6},{3,7},{4,0},{5,1},{6,2},{7,3},{8,12},{9,13},{10,... | collective-permute-start | bytes 663560 | tf_op jit(solution)/shard_map/ppermute | solution.py:289
  50.9 3.0 %collective-permute-start.7 = (bf16[864,128]{1,0:T(8,128)(2,1)S(1)}, bf16[864,128]{1,0:T(8,128)(2,1)S(1)}, u32[]{:S(2)}, u32[]{:S(2)}) collective-permute-start(bf16[864,128]{1,0:T(8,128)(2,1)S(1)} %bitcast.12), channel_id=1, source_target_pairs={{0,6},{1,7},{2,0},{3,1},{4,2},{5,3},{6,4},{7,5},{8,14},{9,15},{10,... | collective-permute-start | bytes 663560 | tf_op jit(solution)/shard_map/ppermute | solution.py:289
  53.9 0.0 copy-done
  53.9 0.1 constant_dynamic-slice_fusion
  54.0 0.1 copy.6.refs_1_
  54.1 5.5 %collective-permute-start.2 = (bf16[864,128]{1,0:T(8,128)(2,1)S(1)}, bf16[864,128]{1,0:T(8,128)(2,1)S(1)}, u32[]{:S(2)}, u32[]{:S(2)}) collective-permute-start(bf16[864,128]{1,0:T(8,128)(2,1)S(1)} %bitcast.13), channel_id=1, source_target_pairs={{0,1},{1,0},{2,3},{3,2},{4,5},{5,4},{6,7},{7,6},{8,9},{9,8},{10,11... | collective-permute-start | bytes 663560 | tf_op jit(solution)/shard_map/ppermute | solution.py:291
  59.6 0.0 collective-permute-done.3.refs_4_
  59.6 4.0 %collective-permute-start.4 = (bf16[864,128]{1,0:T(8,128)(2,1)S(1)}, bf16[864,128]{1,0:T(8,128)(2,1)S(1)}, u32[]{:S(2)}, u32[]{:S(2)}) collective-permute-start(bf16[864,128]{1,0:T(8,128)(2,1)S(1)} %collective-permute-done.3.refs_4_), channel_id=1, source_target_pairs={{0,1},{1,0},{2,3},{3,2},{4,5},{5,4},{6,7},{7,6},{8,9},{9,8},{10,11... | collective-permute-start | bytes 663560 | tf_op jit(solution)/shard_map/ppermute | solution.py:291
  63.6 0.0 collective-permute-done.5.refs_5_
  63.6 1.9 %collective-permute-start.6 = (bf16[864,128]{1,0:T(8,128)(2,1)S(1)}, bf16[864,128]{1,0:T(8,128)(2,1)S(1)}, u32[]{:S(2)}, u32[]{:S(2)}) collective-permute-start(bf16[864,128]{1,0:T(8,128)(2,1)S(1)} %collective-permute-done.5.refs_5_), channel_id=1, source_target_pairs={{0,1},{1,0},{2,3},{3,2},{4,5},{5,4},{6,7},{7,6},{8,9},{9,8},{10,11... | collective-permute-start | bytes 663560 | tf_op jit(solution)/shard_map/ppermute | solution.py:291
  65.5 0.0 collective-permute-done.7.refs_6_
  65.5 2.4 %collective-permute-start.8 = (bf16[864,128]{1,0:T(8,128)(2,1)S(1)}, bf16[864,128]{1,0:T(8,128)(2,1)S(1)}, u32[]{:S(2)}, u32[]{:S(2)}) collective-permute-start(bf16[864,128]{1,0:T(8,128)(2,1)S(1)} %collective-permute-done.7.refs_6_), channel_id=1, source_target_pairs={{0,1},{1,0},{2,3},{3,2},{4,5},{5,4},{6,7},{7,6},{8,9},{9,8},{10,11... | collective-permute-start | bytes 663560 | tf_op jit(solution)/shard_map/ppermute | solution.py:291
  67.9 0.0 all-to-all-done.1.refs_2_
  67.9 9.0 %shard_map.37.refs_7_ = f32[9,64,128]{2,1,0:T(8,128)S(1)} custom-call(s32[4]{0:T(128)S(1)} %get-tuple-element.10.refs_0_, s32[8,3]{1,0:T(8,128)S(1)} %copy.6.refs_1_, bf16[8,144,128]{2,1,0:T(8,128)(2,1)S(1)} %all-to-all-done.1.refs_2_, bf16[864,128]{1,0:T(8,128)(2,1)S(1)} %bitcast.14, bf16[864,128]{1,0:T(8,128)(2,1)S(1)} %collective-permute-done.3.refs_4_, ...), custom_call_target="tpu_custom_call" | custom-call | flops 16106127360 | bytes 557056 | tf_op jit(solution)/shard_map/pallas_call | solution.py:209
  77.0 0.0 collective-permute-done.2.refs_3_
  77.0 0.0 collective-permute-done.4.refs_4_
  77.0 0.0 collective-permute-done.6.refs_5_
  77.0 0.0 collective-permute-done.8.refs_6_
  77.0 9.1 %shard_map.38 = f32[8,8,1024]{2,1,0:T(8,128)S(1)} custom-call(s32[4]{0:T(128)S(1)} %get-tuple-element.9.refs_0_, s32[8,3]{1,0:T(8,128)S(1)} %copy.6.refs_1_, bf16[8,144,128]{2,1,0:T(8,128)(2,1)S(1)} %all-to-all-done.1.refs_2_, bf16[864,128]{1,0:T(8,128)(2,1)S(1)} %collective-permute-done.2.refs_3_, bf16[864,128]{1,0:T(8,128)(2,1)S(1)} %collective-permute-done.4.refs_4_, ...), custom_call_target="tpu_custom_call" | custom-call | flops 16106127360 | bytes 557056 | tf_op jit(solution)/shard_map/pallas_call | solution.py:209
  86.2 11.2 %all_to_all.15 = f32[8,8,1024]{2,1,0:T(8,128)S(1)} all-to-all(f32[8,8,1024]{2,1,0:T(8,128)S(1)} %shard_map.38), channel_id=1, replica_groups={{0,8,16,24,32,40,48,56},{64,72,80,88,96,104,112,120},{128,136,144,152,1..., dimensions={0} | all-to-all | bytes 524288 | tf_op jit(solution)/shard_map/all_to_all | solution.py:297
  97.4 0.7 copy.9
  (8 shorter events, 0.1 us)
Async XLA Ops:
  0.0 53.9 %copy-start = (s32[512,3]{0,1:T(4,128)S(1)}, s32[512,3]{0,1:T(4,128)}, u32[]{:S(2)}) copy-start(s32[512,3]{0,1:T(4,128)} %param.5) | copy-start | bytes 18436
  0.0 2.1 %copy-start.1 = (bf16[3,4,1024]{2,1,0:T(4,128)(2,1)S(1)}, bf16[3,4,1024]{2,1,0:T(4,128)(2,1)}, u32[]{:S(2)}) copy-start(bf16[3,4,1024]{2,1,0:T(4,128)(2,1)} %param.3) | copy-start | bytes 73732
  0.8 5.0 %collective-permute-start = (bf16[3,4,512]{2,1,0:T(4,128)(2,1)S(1)}, bf16[3,4,512]{2,1,0:T(4,128)(2,1)S(1)}, u32[]{:S(2)}, u32[]{:S(2)}) collective-permute-start(bf16[3,4,512]{2,1,0:T(4,128)(2,1)S(1)} %slice.9), channel_id=1, source_target_pairs={{8,0},{16,8},{24,16},{32,24},{40,32},{48,40},{56,48},{64,56},{72,6... | collective-permute-start | bytes 36872 | tf_op jit(solution)/shard_map/ppermute | solution.py:263
  6.6 7.6 %copy-start.2 = (bf16[1,3,4,1536]{3,2,1,0:T(4,128)(2,1)S(1)}, bf16[1,3,4,1536]{3,2,1,0:T(4,128)(2,1)}, u32[]{:S(2)}) copy-start(bf16[1,3,4,1536]{3,2,1,0:T(4,128)(2,1)} %param.4) | copy-start | bytes 110596
  6.6 17.6 %all-to-all-start = ((bf16[8,144,128]{2,1,0:T(8,128)(2,1)}), bf16[8,144,128]{2,1,0:T(8,128)(2,1)S(1)}, u32[]{:S(2)}, u32[]{:S(2)}) async-start(bf16[8,144,128]{2,1,0:T(8,128)(2,1)} %broadcast_in_dim.6), calls=%async_computation | async-start | bytes 589824 | tf_op jit(solution)/shard_map/all_to_all | solution.py:244
  14.2 10.0 %collective-permute-start.1 = (bf16[144,128]{1,0:T(8,128)(2,1)S(1)}, bf16[144,128]{1,0:T(8,128)(2,1)S(1)}, u32[]{:S(2)}, u32[]{:S(2)}) collective-permute-start(bf16[144,128]{1,0:T(8,128)(2,1)S(1)} %reshape.25), channel_id=1, source_target_pairs={{0,0},{1,64},{2,128},{3,192},{4,256},{5,320},{6,384},{7,448},{8,8}... | collective-permute-start | bytes 110600 | tf_op jit(solution)/shard_map/ppermute | solution.py:264
  24.9 43.0 %all-to-all-start.1 = ((bf16[8,144,128]{2,1,0:T(8,128)(2,1)}), bf16[8,144,128]{2,1,0:T(8,128)(2,1)S(1)}, u32[]{:S(2)}, u32[]{:S(2)}) async-start(bf16[8,144,128]{2,1,0:T(8,128)(2,1)} %broadcast_in_dim.7), calls=%async_computation.1 | async-start | bytes 589824 | tf_op jit(solution)/shard_map/all_to_all | solution.py:244
  45.5 14.1 %collective-permute-start.3 = (bf16[864,128]{1,0:T(8,128)(2,1)S(1)}, bf16[864,128]{1,0:T(8,128)(2,1)S(1)}, u32[]{:S(2)}, u32[]{:S(2)}) collective-permute-start(bf16[864,128]{1,0:T(8,128)(2,1)S(1)} %bitcast.10), channel_id=1, source_target_pairs={{0,2},{1,3},{2,4},{3,5},{4,6},{5,7},{6,0},{7,1},{8,10},{9,11},{10,... | collective-permute-start | bytes 663560 | tf_op jit(solution)/shard_map/ppermute | solution.py:289
  47.4 16.2 %collective-permute-start.5 = (bf16[864,128]{1,0:T(8,128)(2,1)S(1)}, bf16[864,128]{1,0:T(8,128)(2,1)S(1)}, u32[]{:S(2)}, u32[]{:S(2)}) collective-permute-start(bf16[864,128]{1,0:T(8,128)(2,1)S(1)} %bitcast.11), channel_id=1, source_target_pairs={{0,4},{1,5},{2,6},{3,7},{4,0},{5,1},{6,2},{7,3},{8,12},{9,13},{10,... | collective-permute-start | bytes 663560 | tf_op jit(solution)/shard_map/ppermute | solution.py:289
  50.9 14.6 %collective-permute-start.7 = (bf16[864,128]{1,0:T(8,128)(2,1)S(1)}, bf16[864,128]{1,0:T(8,128)(2,1)S(1)}, u32[]{:S(2)}, u32[]{:S(2)}) collective-permute-start(bf16[864,128]{1,0:T(8,128)(2,1)S(1)} %bitcast.12), channel_id=1, source_target_pairs={{0,6},{1,7},{2,0},{3,1},{4,2},{5,3},{6,4},{7,5},{8,14},{9,15},{10,... | collective-permute-start | bytes 663560 | tf_op jit(solution)/shard_map/ppermute | solution.py:289
  54.1 22.9 %collective-permute-start.2 = (bf16[864,128]{1,0:T(8,128)(2,1)S(1)}, bf16[864,128]{1,0:T(8,128)(2,1)S(1)}, u32[]{:S(2)}, u32[]{:S(2)}) collective-permute-start(bf16[864,128]{1,0:T(8,128)(2,1)S(1)} %bitcast.13), channel_id=1, source_target_pairs={{0,1},{1,0},{2,3},{3,2},{4,5},{5,4},{6,7},{7,6},{8,9},{9,8},{10,11... | collective-permute-start | bytes 663560 | tf_op jit(solution)/shard_map/ppermute | solution.py:291
  59.6 17.4 %collective-permute-start.4 = (bf16[864,128]{1,0:T(8,128)(2,1)S(1)}, bf16[864,128]{1,0:T(8,128)(2,1)S(1)}, u32[]{:S(2)}, u32[]{:S(2)}) collective-permute-start(bf16[864,128]{1,0:T(8,128)(2,1)S(1)} %collective-permute-done.3.refs_4_), channel_id=1, source_target_pairs={{0,1},{1,0},{2,3},{3,2},{4,5},{5,4},{6,7},{7,6},{8,9},{9,8},{10,11... | collective-permute-start | bytes 663560 | tf_op jit(solution)/shard_map/ppermute | solution.py:291
  63.6 13.4 %collective-permute-start.6 = (bf16[864,128]{1,0:T(8,128)(2,1)S(1)}, bf16[864,128]{1,0:T(8,128)(2,1)S(1)}, u32[]{:S(2)}, u32[]{:S(2)}) collective-permute-start(bf16[864,128]{1,0:T(8,128)(2,1)S(1)} %collective-permute-done.5.refs_5_), channel_id=1, source_target_pairs={{0,1},{1,0},{2,3},{3,2},{4,5},{5,4},{6,7},{7,6},{8,9},{9,8},{10,11... | collective-permute-start | bytes 663560 | tf_op jit(solution)/shard_map/ppermute | solution.py:291
  65.5 11.5 %collective-permute-start.8 = (bf16[864,128]{1,0:T(8,128)(2,1)S(1)}, bf16[864,128]{1,0:T(8,128)(2,1)S(1)}, u32[]{:S(2)}, u32[]{:S(2)}) collective-permute-start(bf16[864,128]{1,0:T(8,128)(2,1)S(1)} %collective-permute-done.7.refs_6_), channel_id=1, source_target_pairs={{0,1},{1,0},{2,3},{3,2},{4,5},{5,4},{6,7},{7,6},{8,9},{9,8},{10,11... | collective-permute-start | bytes 663560 | tf_op jit(solution)/shard_map/ppermute | solution.py:291

commit v6 on v5

--- a/solution.py
+++ b/solution.py
@@ -260,22 +260,19 @@
         for b in range(n_b)
         for t in range(n_sta)
     ]
-    halo = lax.ppermute(record[:, :, :L], "tm", [(i + 1, i) for i in range(n_tm - 1)])
     own = lax.ppermute(templates.reshape(-1, LANES), ("tm", "sta"), turn)
     first = (s * n_b + lax.rem(m, n_b)) * n_a
     groups = lax.dynamic_slice_in_dim(template_groups, first, n_a, 0)
 
     lines = channels * stations
     steps = samples // LANES
-    piece = jnp.concatenate(
-        [record.reshape(lines * steps, LANES), halo.reshape(lines * (L // LANES), LANES)]
-    )
-    around = copies_to(piece, "tm", near)
-    around, own = lax.optimization_barrier((around, own))
+    around = copies_to(record.reshape(lines * steps, LANES), "tm", near)
+    front = around[0].reshape(lines, steps, LANES)[:, : L // LANES]
+    tail = lax.ppermute(front, "tm", [(i + n_b, i) for i in range(n_tm - n_b)])
+    tail, own = lax.optimization_barrier((tail, own))
     block = copies_to(own, "tm", far)
-    main = around[:, : lines * steps].reshape(n_b, lines, steps, LANES)
+    main = around.reshape(n_b, lines, steps, LANES)
     main = main.transpose(1, 0, 2, 3).reshape(lines, n_b * steps, LANES)
-    tail = around[-1, lines * steps :].reshape(lines, L // LANES, LANES)
     rest = jnp.zeros((lines, 8 - L // LANES, LANES), record.dtype)
     padded = n_b * steps + 8
     mine = jnp.concatenate([main, tail, rest], axis=1).reshape(-1, LANES)

time: 98.8 us -> 91.4 us (0.925)
  starting transfers between devices: 59.4 us -> 52.7 us
    all_to_all x2, starting transfers between devices: 27.9 us -> 23.5 us  [copies_to(): lax.all_to_all(spread, axis, 0, 0, axis_index_groups=groups, tiled=True)]
    ppermute x1, starting transfers between devices: 8.1 us -> 5.74 us  [on_device(): own = lax.ppermute(templates.reshape(-1, LANES), ('tm', 'sta'), turn)]
    ppermute x1, waiting for transfers between devices: 1.88 us -> 0.32 us  [on_device(): own = lax.ppermute(templates.reshape(-1, LANES), ('tm', 'sta'), turn)]
    broadcast_in_dim x2 -> x3, local copies, waits for them, and re-layouts: 1.5 us -> 2.21 us  [copies_to(): spread = jnp.broadcast_to(value[None], (count,) + value.shape)]
  transfers between devices with their start and end apart: 11 -> 11, of which waited for: 2 -> 2; matrix products, arithmetic and copies ran while one was open for 0% -> 0% of each run, Pallas kernels for 9% -> 10%
where the time goes in v6:
time: 91.4 us; the launch traced here: 90.7 us
  starting transfers between devices  52.7 us (58%)
  Pallas kernels  18.1 us (20%)
  blocking collectives  11.6 us (13%)
  waiting for transfers between devices  4.78 us (5%)
  local copies, waits for them, and re-layouts  3.23 us (4%)
    all_to_all x2, starting transfers between devices, copies_to(): lax.all_to_all(spread, axis, 0, 0, axis_index_groups=groups, tiled=True)  23.5 us
    pallas_call x2, Pallas kernels, detect(): pl.pallas_call(body, out_shape=out_shape, in_specs=[pl.BlockSpec(memory_s...  18.1 us
    ppermute x4, starting transfers between devices, on_device(): others = [lax.ppermute(value, 'sta', swap) for value in pieces]  13.8 us
    all_to_all x1, blocking collectives, on_device(): lax.all_to_all(total, 'tm', 0, 0, axis_index_groups=near, tiled=True)  11.6 us
    ppermute x3, starting transfers between devices, on_device(): pieces.append(lax.ppermute(mine, 'sta', pairs))  8.41 us
    ppermute x1, starting transfers between devices, on_device(): own = lax.ppermute(templates.reshape(-1, LANES), ('tm', 'sta'), turn)  5.74 us
    ppermute x1, waiting for transfers between devices, on_device(): tail = lax.ppermute(front, 'tm', [(i + n_b, i) for i in range(n_tm - n_b)])  4.43 us
    broadcast_in_dim x3, local copies, waits for them, and re-layouts, copies_to(): spread = jnp.broadcast_to(value[None], (count,) + value.shape)  2.21 us
  transfers between devices with their start and end apart: 11, of which 2 were waited for; matrix products, arithmetic and copies ran while one was open for 0% of the time, Pallas kernels for 10%

profile of v6, /device:TPU:1, one launch (start us, length us, event | category | flops | bytes accessed | tf_op | source)
XLA Modules:
  0.0 90.7 jit_solution(11947436572486501037)
XLA Ops:
  0.0 0.0 copy-start
  0.0 0.8 broadcast_in_dim.16
  0.8 0.7 broadcast_in_dim.17
  1.5 0.0 copy-start.1
  1.5 6.3 %all-to-all-start = ((bf16[8,96,128]{2,1,0:T(8,128)(2,1)}), bf16[8,96,128]{2,1,0:T(8,128)(2,1)S(1)}, u32[]{:S(2)}, u32[]{:S(2)}) async-start(bf16[8,96,128]{2,1,0:T(8,128)(2,1)} %broadcast_in_dim.17), calls=%async_computation | async-start | bytes 393216 | tf_op jit(solution)/shard_map/all_to_all | solution.py:244
  7.8 0.0 copy-done.1
  7.8 5.7 %collective-permute-start.1 = (bf16[144,128]{1,0:T(8,128)(2,1)S(1)}, bf16[144,128]{1,0:T(8,128)(2,1)S(1)}, u32[]{:S(2)}, u32[]{:S(2)}) collective-permute-start(bf16[144,128]{1,0:T(8,128)(2,1)S(1)} %reshape.17), channel_id=1, source_target_pairs={{0,0},{1,64},{2,128},{3,192},{4,256},{5,320},{6,384},{7,448},{8,8}... | collective-permute-start | bytes 110600 | tf_op jit(solution)/shard_map/ppermute | solution.py:263
  13.6 0.0 all-to-all-done
  13.6 1.3 %collective-permute-start = (bf16[12,4,128]{2,1,0:T(4,128)(2,1)S(1)}, bf16[12,4,128]{2,1,0:T(4,128)(2,1)S(1)}, u32[]{:S(2)}, u32[]{:S(2)}) collective-permute-start(bf16[12,4,128]{2,1,0:T(4,128)(2,1)S(1)} %slice.9), channel_id=1, source_target_pairs={{64,0},{72,8},{80,16},{88,24},{96,32},{104,40},{112,48},{120,56},{... | collective-permute-start | bytes 36872 | tf_op jit(solution)/shard_map/ppermute | solution.py:271
  14.9 0.3 collective-permute-done.1
  15.3 4.4 %collective-permute-done = bf16[12,4,128]{2,1,0:T(4,128)(2,1)S(1)} collective-permute-done((bf16[12,4,128]{2,1,0:T(4,128)(2,1)S(1)}, bf16[12,4,128]{2,1,0:T(4,128)(2,1)S(1)}, u32[]{:S(2)}, u32[]{:S(2)}) %collective-permute-start) | collective-permute-done | bytes 12320 | tf_op jit(solution)/shard_map/ppermute | solution.py:271
  19.7 0.7 broadcast_in_dim.18
  20.4 17.1 %all-to-all-start.1 = ((bf16[8,144,128]{2,1,0:T(8,128)(2,1)}), bf16[8,144,128]{2,1,0:T(8,128)(2,1)S(1)}, u32[]{:S(2)}, u32[]{:S(2)}) async-start(bf16[8,144,128]{2,1,0:T(8,128)(2,1)} %broadcast_in_dim.18), calls=%async_computation.1 | async-start | bytes 589824 | tf_op jit(solution)/shard_map/all_to_all | solution.py:244
  37.6 0.1 pad.2.clone
  37.7 0.1 maximum_maximum_fusion
  37.8 1.9 %collective-permute-start.3 = (bf16[864,128]{1,0:T(8,128)(2,1)S(1)}, bf16[864,128]{1,0:T(8,128)(2,1)S(1)}, u32[]{:S(2)}, u32[]{:S(2)}) collective-permute-start(bf16[864,128]{1,0:T(8,128)(2,1)S(1)} %bitcast.11), channel_id=1, source_target_pairs={{0,2},{1,3},{2,4},{3,5},{4,6},{5,7},{6,0},{7,1},{8,10},{9,11},{10,... | collective-permute-start | bytes 663560 | tf_op jit(solution)/shard_map/ppermute | solution.py:286
  39.7 3.6 %collective-permute-start.5 = (bf16[864,128]{1,0:T(8,128)(2,1)S(1)}, bf16[864,128]{1,0:T(8,128)(2,1)S(1)}, u32[]{:S(2)}, u32[]{:S(2)}) collective-permute-start(bf16[864,128]{1,0:T(8,128)(2,1)S(1)} %bitcast.12), channel_id=1, source_target_pairs={{0,4},{1,5},{2,6},{3,7},{4,0},{5,1},{6,2},{7,3},{8,12},{9,13},{10,... | collective-permute-start | bytes 663560 | tf_op jit(solution)/shard_map/ppermute | solution.py:286
  43.3 2.9 %collective-permute-start.7 = (bf16[864,128]{1,0:T(8,128)(2,1)S(1)}, bf16[864,128]{1,0:T(8,128)(2,1)S(1)}, u32[]{:S(2)}, u32[]{:S(2)}) collective-permute-start(bf16[864,128]{1,0:T(8,128)(2,1)S(1)} %bitcast.13), channel_id=1, source_target_pairs={{0,6},{1,7},{2,0},{3,1},{4,2},{5,3},{6,4},{7,5},{8,14},{9,15},{10,... | collective-permute-start | bytes 663560 | tf_op jit(solution)/shard_map/ppermute | solution.py:286
  46.2 0.0 copy-done
  46.2 0.1 constant_dynamic-slice_fusion
  46.3 0.1 copy.6.refs_1_
  46.4 5.6 %collective-permute-start.2 = (bf16[864,128]{1,0:T(8,128)(2,1)S(1)}, bf16[864,128]{1,0:T(8,128)(2,1)S(1)}, u32[]{:S(2)}, u32[]{:S(2)}) collective-permute-start(bf16[864,128]{1,0:T(8,128)(2,1)S(1)} %bitcast.14), channel_id=1, source_target_pairs={{0,1},{1,0},{2,3},{3,2},{4,5},{5,4},{6,7},{7,6},{8,9},{9,8},{10,11... | collective-permute-start | bytes 663560 | tf_op jit(solution)/shard_map/ppermute | solution.py:288
  52.0 0.0 collective-permute-done.3.refs_4_
  52.0 3.8 %collective-permute-start.4 = (bf16[864,128]{1,0:T(8,128)(2,1)S(1)}, bf16[864,128]{1,0:T(8,128)(2,1)S(1)}, u32[]{:S(2)}, u32[]{:S(2)}) collective-permute-start(bf16[864,128]{1,0:T(8,128)(2,1)S(1)} %collective-permute-done.3.refs_4_), channel_id=1, source_target_pairs={{0,1},{1,0},{2,3},{3,2},{4,5},{5,4},{6,7},{7,6},{8,9},{9,8},{10,11... | collective-permute-start | bytes 663560 | tf_op jit(solution)/shard_map/ppermute | solution.py:288
  55.9 0.0 collective-permute-done.5.refs_5_
  55.9 1.9 %collective-permute-start.6 = (bf16[864,128]{1,0:T(8,128)(2,1)S(1)}, bf16[864,128]{1,0:T(8,128)(2,1)S(1)}, u32[]{:S(2)}, u32[]{:S(2)}) collective-permute-start(bf16[864,128]{1,0:T(8,128)(2,1)S(1)} %collective-permute-done.5.refs_5_), channel_id=1, source_target_pairs={{0,1},{1,0},{2,3},{3,2},{4,5},{5,4},{6,7},{7,6},{8,9},{9,8},{10,11... | collective-permute-start | bytes 663560 | tf_op jit(solution)/shard_map/ppermute | solution.py:288
  57.8 0.0 collective-permute-done.7.refs_6_
  57.9 2.4 %collective-permute-start.8 = (bf16[864,128]{1,0:T(8,128)(2,1)S(1)}, bf16[864,128]{1,0:T(8,128)(2,1)S(1)}, u32[]{:S(2)}, u32[]{:S(2)}) collective-permute-start(bf16[864,128]{1,0:T(8,128)(2,1)S(1)} %collective-permute-done.7.refs_6_), channel_id=1, source_target_pairs={{0,1},{1,0},{2,3},{3,2},{4,5},{5,4},{6,7},{7,6},{8,9},{9,8},{10,11... | collective-permute-start | bytes 663560 | tf_op jit(solution)/shard_map/ppermute | solution.py:288
  60.3 0.0 all-to-all-done.1.refs_2_
  60.3 9.0 %shard_map.37.refs_7_ = f32[9,64,128]{2,1,0:T(8,128)S(1)} custom-call(s32[4]{0:T(128)S(1)} %get-tuple-element.10.refs_0_, s32[8,3]{1,0:T(8,128)S(1)} %copy.6.refs_1_, bf16[8,144,128]{2,1,0:T(8,128)(2,1)S(1)} %all-to-all-done.1.refs_2_, bf16[864,128]{1,0:T(8,128)(2,1)S(1)} %bitcast.15, bf16[864,128]{1,0:T(8,128)(2,1)S(1)} %collective-permute-done.3.refs_4_, ...), custom_call_target="tpu_custom_call" | custom-call | flops 16106127360 | bytes 557056 | tf_op jit(solution)/shard_map/pallas_call | solution.py:209
  69.3 0.0 collective-permute-done.2.refs_3_
  69.3 0.0 collective-permute-done.4.refs_4_
  69.3 0.0 collective-permute-done.6.refs_5_
  69.3 0.0 collective-permute-done.8.refs_6_
  69.3 9.1 %shard_map.38 = f32[8,8,1024]{2,1,0:T(8,128)S(1)} custom-call(s32[4]{0:T(128)S(1)} %get-tuple-element.9.refs_0_, s32[8,3]{1,0:T(8,128)S(1)} %copy.6.refs_1_, bf16[8,144,128]{2,1,0:T(8,128)(2,1)S(1)} %all-to-all-done.1.refs_2_, bf16[864,128]{1,0:T(8,128)(2,1)S(1)} %collective-permute-done.2.refs_3_, bf16[864,128]{1,0:T(8,128)(2,1)S(1)} %collective-permute-done.4.refs_4_, ...), custom_call_target="tpu_custom_call" | custom-call | flops 16106127360 | bytes 557056 | tf_op jit(solution)/shard_map/pallas_call | solution.py:209
  78.5 11.6 %all_to_all.15 = f32[8,8,1024]{2,1,0:T(8,128)S(1)} all-to-all(f32[8,8,1024]{2,1,0:T(8,128)S(1)} %shard_map.38), channel_id=1, replica_groups={{0,8,16,24,32,40,48,56},{64,72,80,88,96,104,112,120},{128,136,144,152,1..., dimensions={0} | all-to-all | bytes 524288 | tf_op jit(solution)/shard_map/all_to_all | solution.py:294
  90.0 0.7 copy.9
  (6 shorter events, 0.1 us)
Async XLA Ops:
  0.0 46.2 %copy-start = (s32[512,3]{0,1:T(4,128)S(1)}, s32[512,3]{0,1:T(4,128)}, u32[]{:S(2)}) copy-start(s32[512,3]{0,1:T(4,128)} %param.5) | copy-start | bytes 18436
  1.5 6.3 %copy-start.1 = (bf16[1,3,4,1536]{3,2,1,0:T(4,128)(2,1)S(1)}, bf16[1,3,4,1536]{3,2,1,0:T(4,128)(2,1)}, u32[]{:S(2)}) copy-start(bf16[1,3,4,1536]{3,2,1,0:T(4,128)(2,1)} %param.4) | copy-start | bytes 110596
  1.5 12.1 %all-to-all-start = ((bf16[8,96,128]{2,1,0:T(8,128)(2,1)}), bf16[8,96,128]{2,1,0:T(8,128)(2,1)S(1)}, u32[]{:S(2)}, u32[]{:S(2)}) async-start(bf16[8,96,128]{2,1,0:T(8,128)(2,1)} %broadcast_in_dim.17), calls=%async_computation | async-start | bytes 393216 | tf_op jit(solution)/shard_map/all_to_all | solution.py:244
  7.8 7.4 %collective-permute-start.1 = (bf16[144,128]{1,0:T(8,128)(2,1)S(1)}, bf16[144,128]{1,0:T(8,128)(2,1)S(1)}, u32[]{:S(2)}, u32[]{:S(2)}) collective-permute-start(bf16[144,128]{1,0:T(8,128)(2,1)S(1)} %reshape.17), channel_id=1, source_target_pairs={{0,0},{1,64},{2,128},{3,192},{4,256},{5,320},{6,384},{7,448},{8,8}... | collective-permute-start | bytes 110600 | tf_op jit(solution)/shard_map/ppermute | solution.py:263
  13.6 6.1 %collective-permute-start = (bf16[12,4,128]{2,1,0:T(4,128)(2,1)S(1)}, bf16[12,4,128]{2,1,0:T(4,128)(2,1)S(1)}, u32[]{:S(2)}, u32[]{:S(2)}) collective-permute-start(bf16[12,4,128]{2,1,0:T(4,128)(2,1)S(1)} %slice.9), channel_id=1, source_target_pairs={{64,0},{72,8},{80,16},{88,24},{96,32},{104,40},{112,48},{120,56},{... | collective-permute-start | bytes 36872 | tf_op jit(solution)/shard_map/ppermute | solution.py:271
  20.4 39.8 %all-to-all-start.1 = ((bf16[8,144,128]{2,1,0:T(8,128)(2,1)}), bf16[8,144,128]{2,1,0:T(8,128)(2,1)S(1)}, u32[]{:S(2)}, u32[]{:S(2)}) async-start(bf16[8,144,128]{2,1,0:T(8,128)(2,1)} %broadcast_in_dim.18), calls=%async_computation.1 | async-start | bytes 589824 | tf_op jit(solution)/shard_map/all_to_all | solution.py:244
  37.8 14.2 %collective-permute-start.3 = (bf16[864,128]{1,0:T(8,128)(2,1)S(1)}, bf16[864,128]{1,0:T(8,128)(2,1)S(1)}, u32[]{:S(2)}, u32[]{:S(2)}) collective-permute-start(bf16[864,128]{1,0:T(8,128)(2,1)S(1)} %bitcast.11), channel_id=1, source_target_pairs={{0,2},{1,3},{2,4},{3,5},{4,6},{5,7},{6,0},{7,1},{8,10},{9,11},{10,... | collective-permute-start | bytes 663560 | tf_op jit(solution)/shard_map/ppermute | solution.py:286
  39.7 16.2 %collective-permute-start.5 = (bf16[864,128]{1,0:T(8,128)(2,1)S(1)}, bf16[864,128]{1,0:T(8,128)(2,1)S(1)}, u32[]{:S(2)}, u32[]{:S(2)}) collective-permute-start(bf16[864,128]{1,0:T(8,128)(2,1)S(1)} %bitcast.12), channel_id=1, source_target_pairs={{0,4},{1,5},{2,6},{3,7},{4,0},{5,1},{6,2},{7,3},{8,12},{9,13},{10,... | collective-permute-start | bytes 663560 | tf_op jit(solution)/shard_map/ppermute | solution.py:286
  43.3 14.5 %collective-permute-start.7 = (bf16[864,128]{1,0:T(8,128)(2,1)S(1)}, bf16[864,128]{1,0:T(8,128)(2,1)S(1)}, u32[]{:S(2)}, u32[]{:S(2)}) collective-permute-start(bf16[864,128]{1,0:T(8,128)(2,1)S(1)} %bitcast.13), channel_id=1, source_target_pairs={{0,6},{1,7},{2,0},{3,1},{4,2},{5,3},{6,4},{7,5},{8,14},{9,15},{10,... | collective-permute-start | bytes 663560 | tf_op jit(solution)/shard_map/ppermute | solution.py:286
  46.4 22.9 %collective-permute-start.2 = (bf16[864,128]{1,0:T(8,128)(2,1)S(1)}, bf16[864,128]{1,0:T(8,128)(2,1)S(1)}, u32[]{:S(2)}, u32[]{:S(2)}) collective-permute-start(bf16[864,128]{1,0:T(8,128)(2,1)S(1)} %bitcast.14), channel_id=1, source_target_pairs={{0,1},{1,0},{2,3},{3,2},{4,5},{5,4},{6,7},{7,6},{8,9},{9,8},{10,11... | collective-permute-start | bytes 663560 | tf_op jit(solution)/shard_map/ppermute | solution.py:288
  52.0 17.2 %collective-permute-start.4 = (bf16[864,128]{1,0:T(8,128)(2,1)S(1)}, bf16[864,128]{1,0:T(8,128)(2,1)S(1)}, u32[]{:S(2)}, u32[]{:S(2)}) collective-permute-start(bf16[864,128]{1,0:T(8,128)(2,1)S(1)} %collective-permute-done.3.refs_4_), channel_id=1, source_target_pairs={{0,1},{1,0},{2,3},{3,2},{4,5},{5,4},{6,7},{7,6},{8,9},{9,8},{10,11... | collective-permute-start | bytes 663560 | tf_op jit(solution)/shard_map/ppermute | solution.py:288
  55.9 13.4 %collective-permute-start.6 = (bf16[864,128]{1,0:T(8,128)(2,1)S(1)}, bf16[864,128]{1,0:T(8,128)(2,1)S(1)}, u32[]{:S(2)}, u32[]{:S(2)}) collective-permute-start(bf16[864,128]{1,0:T(8,128)(2,1)S(1)} %collective-permute-done.5.refs_5_), channel_id=1, source_target_pairs={{0,1},{1,0},{2,3},{3,2},{4,5},{5,4},{6,7},{7,6},{8,9},{9,8},{10,11... | collective-permute-start | bytes 663560 | tf_op jit(solution)/shard_map/ppermute | solution.py:288
  57.9 11.5 %collective-permute-start.8 = (bf16[864,128]{1,0:T(8,128)(2,1)S(1)}, bf16[864,128]{1,0:T(8,128)(2,1)S(1)}, u32[]{:S(2)}, u32[]{:S(2)}) collective-permute-start(bf16[864,128]{1,0:T(8,128)(2,1)S(1)} %collective-permute-done.7.refs_6_), channel_id=1, source_target_pairs={{0,1},{1,0},{2,3},{3,2},{4,5},{5,4},{6,7},{7,6},{8,9},{9,8},{10,11... | collective-permute-start | bytes 663560 | tf_op jit(solution)/shard_map/ppermute | solution.py:288

commit v7 on v6

--- a/solution.py
+++ b/solution.py
@@ -21,13 +21,12 @@
     order_ref,
     groups_ref,
     templates_ref,
-    pieces_refs,
+    series_ref,
     before_ref,
     out_ref,
     source,
     home,
     count,
-    series,
     wide,
     waves,
     norms,
@@ -42,7 +41,7 @@
     turned,
 ):
     block, spread = groups_ref.shape
-    n_group = len(pieces_refs)
+    n_group = series_ref.shape[0]
     rows = total.shape[1]
     parts = 3 * L // LANES
     slots = wide.shape[0] // parts
@@ -58,8 +57,6 @@
     lax.fori_loop(0, source.shape[0], clear, 0)
     for n in range(count.shape[0]):
         count[n] = 0
-    for n in range(n_group):
-        series[n] = pieces_refs[n][...]
     for r in range(block):
         for i in range(spread):
             named = groups_ref[r, i]
@@ -95,7 +92,7 @@
         squares = jnp.zeros((padded, LANES), jnp.float32)
         for c in range(3):
             at = (c * stations + station) * padded
-            plain = series[group, at : at + padded, :].astype(jnp.float32)
+            plain = series_ref[group, at : at + padded, :].astype(jnp.float32)
             squares = squares + plain * plain
             shifts[c, 0, 0:padded, :] = plain
             after = shifts[c, 0, 1 : padded + 1, :]
@@ -183,7 +180,7 @@
             out_ref[w, :, i * LANES : (i + 1) * LANES] = turned[w * (samples // LANES) + i]
 
 
-def detect(order, groups, templates, pieces, before, n_all, padded, parts, factor):
+def detect(order, groups, templates, series, before, n_all, padded, parts, factor):
     block, spread = groups.shape
     stations = 4
     slots = block * spread * stations
@@ -194,17 +191,17 @@
         out_shape = jax.ShapeDtypeStruct((block + 1, rows, LANES), jnp.float32)
     else:
         out_shape = jax.ShapeDtypeStruct((parts, block, samples), jnp.float32)
-    operands = [order, groups, templates, *pieces]
-    spaces = [pltpu.SMEM, pltpu.SMEM] + [pltpu.VMEM] * (1 + len(pieces))
+    operands = [order, groups, templates, series]
+    spaces = [pltpu.SMEM, pltpu.SMEM, pltpu.VMEM, pltpu.VMEM]
     if before is not None:
         operands.append(before)
         spaces.append(pltpu.VMEM)
 
     def body(*refs):
-        end = 3 + len(pieces)
-        taken = refs[end] if before is not None else None
-        rest = refs[end + (before is not None) :]
-        detect_kernel(padded, factor, *refs[:3], refs[3:end], taken, *rest)
+        refs = list(refs)
+        if before is None:
+            refs.insert(4, None)
+        detect_kernel(padded, factor, *refs)
 
     return pl.pallas_call(
         body,
@@ -215,7 +212,6 @@
             pltpu.SMEM((n_all * SLOTS,), jnp.int32),
             pltpu.SMEM((n_all * SLOTS,), jnp.int32),
             pltpu.SMEM((n_all,), jnp.int32),
-            pltpu.VMEM((len(pieces),) + pieces[0].shape, jnp.bfloat16),
             pltpu.VMEM((slots * 3 * L // LANES, LANES), jnp.float32),
             pltpu.VMEM((spare, 3 * SPAN), jnp.float32),
             pltpu.VMEM((spare, LANES), jnp.float32),
@@ -231,7 +227,7 @@
         ],
         compiler_params=pltpu.CompilerParams(vmem_limit_bytes=32 * 1024 * 1024),
         cost_estimate=pl.CostEstimate(
-            flops=16 * len(pieces) * stations * 2 * rows * 3 * SPAN * SLOTS * HALF,
+            flops=16 * series.shape[0] * stations * 2 * rows * 3 * SPAN * SLOTS * HALF,
             bytes_accessed=templates.size * 2 + 4 * block * rows * LANES,
             transcendentals=0,
         ),
@@ -267,9 +263,9 @@
     lines = channels * stations
     steps = samples // LANES
     around = copies_to(record.reshape(lines * steps, LANES), "tm", near)
+    around, own = lax.optimization_barrier((around, own))
     front = around[0].reshape(lines, steps, LANES)[:, : L // LANES]
     tail = lax.ppermute(front, "tm", [(i + n_b, i) for i in range(n_tm - n_b)])
-    tail, own = lax.optimization_barrier((tail, own))
     block = copies_to(own, "tm", far)
     main = around.reshape(n_b, lines, steps, LANES)
     main = main.transpose(1, 0, 2, 3).reshape(lines, n_b * steps, LANES)
@@ -285,7 +281,8 @@
         pairs = [(t, (t + k * cores) % n_sta) for t in range(n_sta)]
         pieces.append(lax.ppermute(mine, "sta", pairs))
     swap = [(t, t ^ 1) for t in range(n_sta)]
-    others = [lax.ppermute(value, "sta", swap) for value in pieces]
+    pieces = jnp.stack(pieces)
+    others = lax.ppermute(pieces, "sta", swap)
     rows_of_y = lax.rem(y - jnp.arange(n_y, dtype=jnp.int32) + n_y, n_y) * cores
     factor = math.sqrt(channels * L / (spread * stations))
     total = detect(rows_of_y + core, groups, block, pieces, None, n_sta, padded, n_b, None)

time: 91.4 us -> 101 us (1.11)
  waiting for transfers between devices: 4.78 us -> 12.9 us
  blocking collectives: 11.6 us -> 13.3 us
  starting transfers between devices: 52.7 us -> 51.5 us
    ppermute x3, waiting for transfers between devices: 0.01 us -> 6.38 us  [on_device(): pieces.append(lax.ppermute(mine, 'sta', pairs))]
    ppermute x4 -> x1, starting transfers between devices: 13.8 us -> 8.97 us  [on_device(): others = lax.ppermute(pieces, 'sta', swap)]
    all_to_all x2, starting transfers between devices: 23.5 us -> 27.9 us  [copies_to(): lax.all_to_all(spread, axis, 0, 0, axis_index_groups=groups, tiled=True)]
    all_to_all x1, blocking collectives: 11.6 us -> 13.3 us  [on_device(): lax.all_to_all(total, 'tm', 0, 0, axis_index_groups=near, tiled=True)]
    ppermute x1, waiting for transfers between devices: 0.32 us -> 1.39 us  [on_device(): own = lax.ppermute(templates.reshape(-1, LANES), ('tm', 'sta'), turn)]
  transfers between devices with their start and end apart: 11 -> 8, of which waited for: 2 -> 4; matrix products, arithmetic and copies ran while one was open for 0% -> 1% of each run, Pallas kernels for 10% -> 9%
where the time goes in v7:
time: 101 us; the launch traced here: 99.4 us
  starting transfers between devices  51.5 us (51%)
  Pallas kernels  18.1 us (18%)
  blocking collectives  13.3 us (13%)
  waiting for transfers between devices  12.9 us (13%)
  local copies, waits for them, and re-layouts  3.24 us (3%)
    all_to_all x2, starting transfers between devices, copies_to(): lax.all_to_all(spread, axis, 0, 0, axis_index_groups=groups, tiled=True)  27.9 us
    pallas_call x2, Pallas kernels, detect(): pl.pallas_call(body, out_shape=out_shape, in_specs=[pl.BlockSpec(memory_s...  18.1 us
    all_to_all x1, blocking collectives, on_device(): lax.all_to_all(total, 'tm', 0, 0, axis_index_groups=near, tiled=True)  13.3 us
    ppermute x1, starting transfers between devices, on_device(): others = lax.ppermute(pieces, 'sta', swap)  8.97 us
    ppermute x3, starting transfers between devices, on_device(): pieces.append(lax.ppermute(mine, 'sta', pairs))  7.63 us
    ppermute x3, waiting for transfers between devices, on_device(): pieces.append(lax.ppermute(mine, 'sta', pairs))  6.38 us
    ppermute x1, starting transfers between devices, on_device(): own = lax.ppermute(templates.reshape(-1, LANES), ('tm', 'sta'), turn)  5.74 us
    ppermute x1, waiting for transfers between devices, on_device(): tail = lax.ppermute(front, 'tm', [(i + n_b, i) for i in range(n_tm - n_b)])  5.1 us
  transfers between devices with their start and end apart: 8, of which 4 were waited for; matrix products, arithmetic and copies ran while one was open for 1% of the time, Pallas kernels for 9%

profile of v7, /device:TPU:1, one launch (start us, length us, event | category | flops | bytes accessed | tf_op | source)
XLA Modules:
  0.0 99.4 jit_solution(14691289878022172765)
XLA Ops:
  0.0 0.0 copy-start
  0.0 0.8 broadcast_in_dim.16
  0.8 0.7 broadcast_in_dim.17
  1.5 0.0 copy-start.1
  1.5 6.3 %all-to-all-start = ((bf16[8,96,128]{2,1,0:T(8,128)(2,1)}), bf16[8,96,128]{2,1,0:T(8,128)(2,1)S(1)}, u32[]{:S(2)}, u32[]{:S(2)}) async-start(bf16[8,96,128]{2,1,0:T(8,128)(2,1)} %broadcast_in_dim.17), calls=%async_computation | async-start | bytes 393216 | tf_op jit(solution)/shard_map/all_to_all | solution.py:240
  7.8 0.0 copy-done.1
  7.8 5.7 %collective-permute-start = (bf16[144,128]{1,0:T(8,128)(2,1)S(1)}, bf16[144,128]{1,0:T(8,128)(2,1)S(1)}, u32[]{:S(2)}, u32[]{:S(2)}) collective-permute-start(bf16[144,128]{1,0:T(8,128)(2,1)S(1)} %reshape.17), channel_id=1, source_target_pairs={{0,0},{1,64},{2,128},{3,192},{4,256},{5,320},{6,384},{7,448},{8,8}... | collective-permute-start | bytes 110600 | tf_op jit(solution)/shard_map/ppermute | solution.py:259
  13.6 0.0 copy-done
  13.6 0.1 constant_dynamic-slice_fusion
  13.7 0.1 copy.6.refs_1_
  13.8 0.1 pad.6.clone
  13.9 1.4 %collective-permute-done = bf16[144,128]{1,0:T(8,128)(2,1)S(1)} collective-permute-done((bf16[144,128]{1,0:T(8,128)(2,1)S(1)}, bf16[144,128]{1,0:T(8,128)(2,1)S(1)}, u32[]{:S(2)}, u32[]{:S(2)}) %collective-permute-start) | collective-permute-done | bytes 36896 | tf_op jit(solution)/shard_map/ppermute | solution.py:259
  15.3 0.0 all-to-all-done
  15.3 0.7 broadcast_in_dim.18
  16.0 21.5 %all-to-all-start.1 = ((bf16[8,144,128]{2,1,0:T(8,128)(2,1)}), bf16[8,144,128]{2,1,0:T(8,128)(2,1)S(1)}, u32[]{:S(2)}, u32[]{:S(2)}) async-start(bf16[8,144,128]{2,1,0:T(8,128)(2,1)} %broadcast_in_dim.18), calls=%async_computation.1 | async-start | bytes 589824 | tf_op jit(solution)/shard_map/all_to_all | solution.py:240
  37.6 1.3 %collective-permute-start.1 = (bf16[12,4,128]{2,1,0:T(4,128)(2,1)S(1)}, bf16[12,4,128]{2,1,0:T(4,128)(2,1)S(1)}, u32[]{:S(2)}, u32[]{:S(2)}) collective-permute-start(bf16[12,4,128]{2,1,0:T(4,128)(2,1)S(1)} %slice.8), channel_id=1, source_target_pairs={{64,0},{72,8},{80,16},{88,24},{96,32},{104,40},{112,48},{120,56},{... | collective-permute-start | bytes 36872 | tf_op jit(solution)/shard_map/ppermute | solution.py:268
  38.9 5.1 %collective-permute-done.1 = bf16[12,4,128]{2,1,0:T(4,128)(2,1)S(1)} collective-permute-done((bf16[12,4,128]{2,1,0:T(4,128)(2,1)S(1)}, bf16[12,4,128]{2,1,0:T(4,128)(2,1)S(1)}, u32[]{:S(2)}, u32[]{:S(2)}) %collective-permute-start.1) | collective-permute-done | bytes 12320 | tf_op jit(solution)/shard_map/ppermute | solution.py:268
  44.0 0.1 maximum_maximum_fusion
  44.1 3.2 %collective-permute-start.4 = (bf16[864,128]{1,0:T(8,128)(2,1)S(1)}, bf16[864,128]{1,0:T(8,128)(2,1)S(1)}, u32[]{:S(2)}, u32[]{:S(2)}) collective-permute-start(bf16[864,128]{1,0:T(8,128)(2,1)S(1)} %bitcast.16), channel_id=1, source_target_pairs={{0,6},{1,7},{2,0},{3,1},{4,2},{5,3},{6,4},{7,5},{8,14},{9,15},{10,... | collective-permute-start | bytes 663560 | tf_op jit(solution)/shard_map/ppermute | solution.py:282
  47.4 1.9 %collective-permute-start.3 = (bf16[864,128]{1,0:T(8,128)(2,1)S(1)}, bf16[864,128]{1,0:T(8,128)(2,1)S(1)}, u32[]{:S(2)}, u32[]{:S(2)}) collective-permute-start(bf16[864,128]{1,0:T(8,128)(2,1)S(1)} %bitcast.17), channel_id=1, source_target_pairs={{0,4},{1,5},{2,6},{3,7},{4,0},{5,1},{6,2},{7,3},{8,12},{9,13},{10,... | collective-permute-start | bytes 663560 | tf_op jit(solution)/shard_map/ppermute | solution.py:282
  49.3 2.5 %collective-permute-start.2 = (bf16[864,128]{1,0:T(8,128)(2,1)S(1)}, bf16[864,128]{1,0:T(8,128)(2,1)S(1)}, u32[]{:S(2)}, u32[]{:S(2)}) collective-permute-start(bf16[864,128]{1,0:T(8,128)(2,1)S(1)} %bitcast.18), channel_id=1, source_target_pairs={{0,2},{1,3},{2,4},{3,5},{4,6},{5,7},{6,0},{7,1},{8,10},{9,11},{10,... | collective-permute-start | bytes 663560 | tf_op jit(solution)/shard_map/ppermute | solution.py:282
  51.8 0.0 collective-permute-done.4
  51.8 3.8 %collective-permute-done.3 = bf16[864,128]{1,0:T(8,128)(2,1)S(1)} collective-permute-done((bf16[864,128]{1,0:T(8,128)(2,1)S(1)}, bf16[864,128]{1,0:T(8,128)(2,1)S(1)}, u32[]{:S(2)}, u32[]{:S(2)}) %collective-permute-start.3) | collective-permute-done | bytes 221216 | tf_op jit(solution)/shard_map/ppermute | solution.py:282
  55.6 2.6 %collective-permute-done.2 = bf16[864,128]{1,0:T(8,128)(2,1)S(1)} collective-permute-done((bf16[864,128]{1,0:T(8,128)(2,1)S(1)}, bf16[864,128]{1,0:T(8,128)(2,1)S(1)}, u32[]{:S(2)}, u32[]{:S(2)}) %collective-permute-start.2) | collective-permute-done | bytes 221216 | tf_op jit(solution)/shard_map/ppermute | solution.py:282
  58.2 0.1 pad_maximum_fusion.refs_3_
  58.3 9.0 %collective-permute-start.5 = (bf16[4,864,128]{2,1,0:T(8,128)(2,1)S(1)}, bf16[4,864,128]{2,1,0:T(8,128)(2,1)S(1)}, u32[]{:S(2)}, u32[]{:S(2)}) collective-permute-start(bf16[4,864,128]{2,1,0:T(8,128)(2,1)S(1)} %pad_maximum_fusion.refs_3_), channel_id=1, source_target_pairs={{0,1},{1,0},{2,3},{3,2},{4,5},{5,4},{6,7},{7,6},{8,9},{9,8},{10,11... | collective-permute-start | bytes 2654216 | tf_op jit(solution)/shard_map/ppermute | solution.py:285
  67.3 0.0 all-to-all-done.1.refs_2_
  67.3 9.0 %shard_map.37.refs_4_ = f32[9,64,128]{2,1,0:T(8,128)S(1)} custom-call(s32[4]{0:T(128)S(1)} %broadcast_add_fusion.refs_0_, s32[8,3]{1,0:T(8,128)S(1)} %copy.6.refs_1_, bf16[8,144,128]{2,1,0:T(8,128)(2,1)S(1)} %all-to-all-done.1.refs_2_, bf16[4,864,128]{2,1,0:T(8,128)(2,1)S(1)} %pad_maximum_fusion.refs_3_), custom_call_target="tpu_custom_call" | custom-call | flops 16106127360 | bytes 557056 | tf_op jit(solution)/shard_map/pallas_call | solution.py:206
  76.3 0.0 collective-permute-done.5.refs_3_
  76.3 9.1 %shard_map.38 = f32[8,8,1024]{2,1,0:T(8,128)S(1)} custom-call(s32[4]{0:T(128)S(1)} %add_subtract_fusion.refs_0_, s32[8,3]{1,0:T(8,128)S(1)} %copy.6.refs_1_, bf16[8,144,128]{2,1,0:T(8,128)(2,1)S(1)} %all-to-all-done.1.refs_2_, bf16[4,864,128]{2,1,0:T(8,128)(2,1)S(1)} %collective-permute-done.5.refs_3_, f32[9,64,128]{2,1,0:T(8,128)S(1)} %shard_map.37.refs_4_), custom_call_target="tpu_custom_call" | custom-call | flops 16106127360 | bytes 557056 | tf_op jit(solution)/shard_map/pallas_call | solution.py:206
  85.5 13.3 %all_to_all.15 = f32[8,8,1024]{2,1,0:T(8,128)S(1)} all-to-all(f32[8,8,1024]{2,1,0:T(8,128)S(1)} %shard_map.38), channel_id=1, replica_groups={{0,8,16,24,32,40,48,56},{64,72,80,88,96,104,112,120},{128,136,144,152,1..., dimensions={0} | all-to-all | bytes 524288 | tf_op jit(solution)/shard_map/all_to_all | solution.py:291
  98.7 0.7 copy.9
  (7 shorter events, 0.1 us)
Async XLA Ops:
  0.0 13.6 %copy-start = (s32[512,3]{0,1:T(4,128)S(1)}, s32[512,3]{0,1:T(4,128)}, u32[]{:S(2)}) copy-start(s32[512,3]{0,1:T(4,128)} %param.5) | copy-start | bytes 18436
  1.5 6.3 %copy-start.1 = (bf16[1,3,4,1536]{3,2,1,0:T(4,128)(2,1)S(1)}, bf16[1,3,4,1536]{3,2,1,0:T(4,128)(2,1)}, u32[]{:S(2)}) copy-start(bf16[1,3,4,1536]{3,2,1,0:T(4,128)(2,1)} %param.4) | copy-start | bytes 110596
  1.5 13.8 %all-to-all-start = ((bf16[8,96,128]{2,1,0:T(8,128)(2,1)}), bf16[8,96,128]{2,1,0:T(8,128)(2,1)S(1)}, u32[]{:S(2)}, u32[]{:S(2)}) async-start(bf16[8,96,128]{2,1,0:T(8,128)(2,1)} %broadcast_in_dim.17), calls=%async_computation | async-start | bytes 393216 | tf_op jit(solution)/shard_map/all_to_all | solution.py:240
  7.8 7.4 %collective-permute-start = (bf16[144,128]{1,0:T(8,128)(2,1)S(1)}, bf16[144,128]{1,0:T(8,128)(2,1)S(1)}, u32[]{:S(2)}, u32[]{:S(2)}) collective-permute-start(bf16[144,128]{1,0:T(8,128)(2,1)S(1)} %reshape.17), channel_id=1, source_target_pairs={{0,0},{1,64},{2,128},{3,192},{4,256},{5,320},{6,384},{7,448},{8,8}... | collective-permute-start | bytes 110600 | tf_op jit(solution)/shard_map/ppermute | solution.py:259
  16.0 51.3 %all-to-all-start.1 = ((bf16[8,144,128]{2,1,0:T(8,128)(2,1)}), bf16[8,144,128]{2,1,0:T(8,128)(2,1)S(1)}, u32[]{:S(2)}, u32[]{:S(2)}) async-start(bf16[8,144,128]{2,1,0:T(8,128)(2,1)} %broadcast_in_dim.18), calls=%async_computation.1 | async-start | bytes 589824 | tf_op jit(solution)/shard_map/all_to_all | solution.py:240
  37.6 6.4 %collective-permute-start.1 = (bf16[12,4,128]{2,1,0:T(4,128)(2,1)S(1)}, bf16[12,4,128]{2,1,0:T(4,128)(2,1)S(1)}, u32[]{:S(2)}, u32[]{:S(2)}) collective-permute-start(bf16[12,4,128]{2,1,0:T(4,128)(2,1)S(1)} %slice.8), channel_id=1, source_target_pairs={{64,0},{72,8},{80,16},{88,24},{96,32},{104,40},{112,48},{120,56},{... | collective-permute-start | bytes 36872 | tf_op jit(solution)/shard_map/ppermute | solution.py:268
  44.1 7.7 %collective-permute-start.4 = (bf16[864,128]{1,0:T(8,128)(2,1)S(1)}, bf16[864,128]{1,0:T(8,128)(2,1)S(1)}, u32[]{:S(2)}, u32[]{:S(2)}) collective-permute-start(bf16[864,128]{1,0:T(8,128)(2,1)S(1)} %bitcast.16), channel_id=1, source_target_pairs={{0,6},{1,7},{2,0},{3,1},{4,2},{5,3},{6,4},{7,5},{8,14},{9,15},{10,... | collective-permute-start | bytes 663560 | tf_op jit(solution)/shard_map/ppermute | solution.py:282
  47.4 8.3 %collective-permute-start.3 = (bf16[864,128]{1,0:T(8,128)(2,1)S(1)}, bf16[864,128]{1,0:T(8,128)(2,1)S(1)}, u32[]{:S(2)}, u32[]{:S(2)}) collective-permute-start(bf16[864,128]{1,0:T(8,128)(2,1)S(1)} %bitcast.17), channel_id=1, source_target_pairs={{0,4},{1,5},{2,6},{3,7},{4,0},{5,1},{6,2},{7,3},{8,12},{9,13},{10,... | collective-permute-start | bytes 663560 | tf_op jit(solution)/shard_map/ppermute | solution.py:282
  49.3 8.9 %collective-permute-start.2 = (bf16[864,128]{1,0:T(8,128)(2,1)S(1)}, bf16[864,128]{1,0:T(8,128)(2,1)S(1)}, u32[]{:S(2)}, u32[]{:S(2)}) collective-permute-start(bf16[864,128]{1,0:T(8,128)(2,1)S(1)} %bitcast.18), channel_id=1, source_target_pairs={{0,2},{1,3},{2,4},{3,5},{4,6},{5,7},{6,0},{7,1},{8,10},{9,11},{10,... | collective-permute-start | bytes 663560 | tf_op jit(solution)/shard_map/ppermute | solution.py:282
  58.3 18.0 %collective-permute-start.5 = (bf16[4,864,128]{2,1,0:T(8,128)(2,1)S(1)}, bf16[4,864,128]{2,1,0:T(8,128)(2,1)S(1)}, u32[]{:S(2)}, u32[]{:S(2)}) collective-permute-start(bf16[4,864,128]{2,1,0:T(8,128)(2,1)S(1)} %pad_maximum_fusion.refs_3_), channel_id=1, source_target_pairs={{0,1},{1,0},{2,3},{3,2},{4,5},{5,4},{6,7},{7,6},{8,9},{9,8},{10,11... | collective-permute-start | bytes 2654216 | tf_op jit(solution)/shard_map/ppermute | solution.py:285

commit v8 on v7

--- a/solution.py
+++ b/solution.py
@@ -263,9 +263,9 @@
     lines = channels * stations
     steps = samples // LANES
     around = copies_to(record.reshape(lines * steps, LANES), "tm", near)
-    around, own = lax.optimization_barrier((around, own))
     front = around[0].reshape(lines, steps, LANES)[:, : L // LANES]
     tail = lax.ppermute(front, "tm", [(i + n_b, i) for i in range(n_tm - n_b)])
+    tail, own = lax.optimization_barrier((tail, own))
     block = copies_to(own, "tm", far)
     main = around.reshape(n_b, lines, steps, LANES)
     main = main.transpose(1, 0, 2, 3).reshape(lines, n_b * steps, LANES)

time: 101 us -> 90 us (0.89)
  starting transfers between devices: 51.5 us -> 42.6 us
  blocking collectives: 13.3 us -> 11.3 us
    all_to_all x2, starting transfers between devices: 27.9 us -> 23.5 us  [copies_to(): lax.all_to_all(spread, axis, 0, 0, axis_index_groups=groups, tiled=True)]
    ppermute x1, starting transfers between devices: 8.97 us -> 4.91 us  [on_device(): others = lax.ppermute(pieces, 'sta', swap)]
    all_to_all x1, blocking collectives: 13.3 us -> 11.3 us  [on_device(): lax.all_to_all(total, 'tm', 0, 0, axis_index_groups=near, tiled=True)]
    ppermute x3, waiting for transfers between devices: 6.38 us -> 8.13 us  [on_device(): pieces.append(lax.ppermute(mine, 'sta', pairs))]
    ppermute x1, waiting for transfers between devices: 1.39 us -> 0.32 us  [on_device(): own = lax.ppermute(templates.reshape(-1, LANES), ('tm', 'sta'), turn)]
  transfers between devices with their start and end apart: 8 -> 8, of which waited for: 4 -> 4; matrix products, arithmetic and copies ran while one was open for 1% -> 1% of each run, Pallas kernels for 9% -> 10%
where the time goes in v8:
time: 90 us; the launch traced here: 88.6 us
  starting transfers between devices  42.6 us (47%)
  Pallas kernels  18.1 us (20%)
  waiting for transfers between devices  12.9 us (14%)
  blocking collectives  11.3 us (13%)
  local copies, waits for them, and re-layouts  3.24 us (4%)
    all_to_all x2, starting transfers between devices, copies_to(): lax.all_to_all(spread, axis, 0, 0, axis_index_groups=groups, tiled=True)  23.5 us
    pallas_call x2, Pallas kernels, detect(): pl.pallas_call(body, out_shape=out_shape, in_specs=[pl.BlockSpec(memory_s...  18.1 us
    all_to_all x1, blocking collectives, on_device(): lax.all_to_all(total, 'tm', 0, 0, axis_index_groups=near, tiled=True)  11.3 us
    ppermute x3, waiting for transfers between devices, on_device(): pieces.append(lax.ppermute(mine, 'sta', pairs))  8.13 us
    ppermute x3, starting transfers between devices, on_device(): pieces.append(lax.ppermute(mine, 'sta', pairs))  7.2 us
    ppermute x1, starting transfers between devices, on_device(): own = lax.ppermute(templates.reshape(-1, LANES), ('tm', 'sta'), turn)  5.74 us
    ppermute x1, starting transfers between devices, on_device(): others = lax.ppermute(pieces, 'sta', swap)  4.91 us
    ppermute x1, waiting for transfers between devices, on_device(): tail = lax.ppermute(front, 'tm', [(i + n_b, i) for i in range(n_tm - n_b)])  4.43 us
  transfers between devices with their start and end apart: 8, of which 4 were waited for; matrix products, arithmetic and copies ran while one was open for 1% of the time, Pallas kernels for 10%

profile of v8, /device:TPU:1, one launch (start us, length us, event | category | flops | bytes accessed | tf_op | source)
XLA Modules:
  0.0 88.6 jit_solution(1722655640348119753)
XLA Ops:
  0.0 0.0 copy-start
  0.0 0.8 broadcast_in_dim.16
  0.8 0.7 broadcast_in_dim.17
  1.5 0.0 copy-start.1
  1.5 6.3 %all-to-all-start = ((bf16[8,96,128]{2,1,0:T(8,128)(2,1)}), bf16[8,96,128]{2,1,0:T(8,128)(2,1)S(1)}, u32[]{:S(2)}, u32[]{:S(2)}) async-start(bf16[8,96,128]{2,1,0:T(8,128)(2,1)} %broadcast_in_dim.17), calls=%async_computation | async-start | bytes 393216 | tf_op jit(solution)/shard_map/all_to_all | solution.py:240
  7.8 0.0 copy-done.1
  7.8 5.7 %collective-permute-start.1 = (bf16[144,128]{1,0:T(8,128)(2,1)S(1)}, bf16[144,128]{1,0:T(8,128)(2,1)S(1)}, u32[]{:S(2)}, u32[]{:S(2)}) collective-permute-start(bf16[144,128]{1,0:T(8,128)(2,1)S(1)} %reshape.17), channel_id=1, source_target_pairs={{0,0},{1,64},{2,128},{3,192},{4,256},{5,320},{6,384},{7,448},{8,8}... | collective-permute-start | bytes 110600 | tf_op jit(solution)/shard_map/ppermute | solution.py:259
  13.6 0.0 all-to-all-done
  13.6 1.3 %collective-permute-start = (bf16[12,4,128]{2,1,0:T(4,128)(2,1)S(1)}, bf16[12,4,128]{2,1,0:T(4,128)(2,1)S(1)}, u32[]{:S(2)}, u32[]{:S(2)}) collective-permute-start(bf16[12,4,128]{2,1,0:T(4,128)(2,1)S(1)} %slice.9), channel_id=1, source_target_pairs={{64,0},{72,8},{80,16},{88,24},{96,32},{104,40},{112,48},{120,56},{... | collective-permute-start | bytes 36872 | tf_op jit(solution)/shard_map/ppermute | solution.py:267
  14.9 0.3 collective-permute-done.1
  15.3 4.4 %collective-permute-done = bf16[12,4,128]{2,1,0:T(4,128)(2,1)S(1)} collective-permute-done((bf16[12,4,128]{2,1,0:T(4,128)(2,1)S(1)}, bf16[12,4,128]{2,1,0:T(4,128)(2,1)S(1)}, u32[]{:S(2)}, u32[]{:S(2)}) %collective-permute-start) | collective-permute-done | bytes 12320 | tf_op jit(solution)/shard_map/ppermute | solution.py:267
  19.7 0.7 broadcast_in_dim.18
  20.4 17.1 %all-to-all-start.1 = ((bf16[8,144,128]{2,1,0:T(8,128)(2,1)}), bf16[8,144,128]{2,1,0:T(8,128)(2,1)S(1)}, u32[]{:S(2)}, u32[]{:S(2)}) async-start(bf16[8,144,128]{2,1,0:T(8,128)(2,1)} %broadcast_in_dim.18), calls=%async_computation.1 | async-start | bytes 589824 | tf_op jit(solution)/shard_map/all_to_all | solution.py:240
  37.6 0.0 copy-done
  37.6 0.1 constant_dynamic-slice_fusion
  37.6 0.1 copy.6.refs_1_
  37.7 0.1 pad.6.clone
  37.8 0.1 maximum_maximum_fusion
  38.0 2.4 %collective-permute-start.4 = (bf16[864,128]{1,0:T(8,128)(2,1)S(1)}, bf16[864,128]{1,0:T(8,128)(2,1)S(1)}, u32[]{:S(2)}, u32[]{:S(2)}) collective-permute-start(bf16[864,128]{1,0:T(8,128)(2,1)S(1)} %bitcast.16), channel_id=1, source_target_pairs={{0,6},{1,7},{2,0},{3,1},{4,2},{5,3},{6,4},{7,5},{8,14},{9,15},{10,... | collective-permute-start | bytes 663560 | tf_op jit(solution)/shard_map/ppermute | solution.py:282
  40.4 1.9 %collective-permute-start.3 = (bf16[864,128]{1,0:T(8,128)(2,1)S(1)}, bf16[864,128]{1,0:T(8,128)(2,1)S(1)}, u32[]{:S(2)}, u32[]{:S(2)}) collective-permute-start(bf16[864,128]{1,0:T(8,128)(2,1)S(1)} %bitcast.17), channel_id=1, source_target_pairs={{0,4},{1,5},{2,6},{3,7},{4,0},{5,1},{6,2},{7,3},{8,12},{9,13},{10,... | collective-permute-start | bytes 663560 | tf_op jit(solution)/shard_map/ppermute | solution.py:282
  42.3 2.9 %collective-permute-start.2 = (bf16[864,128]{1,0:T(8,128)(2,1)S(1)}, bf16[864,128]{1,0:T(8,128)(2,1)S(1)}, u32[]{:S(2)}, u32[]{:S(2)}) collective-permute-start(bf16[864,128]{1,0:T(8,128)(2,1)S(1)} %bitcast.18), channel_id=1, source_target_pairs={{0,2},{1,3},{2,4},{3,5},{4,6},{5,7},{6,0},{7,1},{8,10},{9,11},{10,... | collective-permute-start | bytes 663560 | tf_op jit(solution)/shard_map/ppermute | solution.py:282
  45.2 0.0 collective-permute-done.4
  45.2 3.3 %collective-permute-done.3 = bf16[864,128]{1,0:T(8,128)(2,1)S(1)} collective-permute-done((bf16[864,128]{1,0:T(8,128)(2,1)S(1)}, bf16[864,128]{1,0:T(8,128)(2,1)S(1)}, u32[]{:S(2)}, u32[]{:S(2)}) %collective-permute-start.3) | collective-permute-done | bytes 221216 | tf_op jit(solution)/shard_map/ppermute | solution.py:282
  48.6 4.8 %collective-permute-done.2 = bf16[864,128]{1,0:T(8,128)(2,1)S(1)} collective-permute-done((bf16[864,128]{1,0:T(8,128)(2,1)S(1)}, bf16[864,128]{1,0:T(8,128)(2,1)S(1)}, u32[]{:S(2)}, u32[]{:S(2)}) %collective-permute-start.2) | collective-permute-done | bytes 221216 | tf_op jit(solution)/shard_map/ppermute | solution.py:282
  53.4 0.1 pad_maximum_fusion.refs_3_
  53.5 4.9 %collective-permute-start.5 = (bf16[4,864,128]{2,1,0:T(8,128)(2,1)S(1)}, bf16[4,864,128]{2,1,0:T(8,128)(2,1)S(1)}, u32[]{:S(2)}, u32[]{:S(2)}) collective-permute-start(bf16[4,864,128]{2,1,0:T(8,128)(2,1)S(1)} %pad_maximum_fusion.refs_3_), channel_id=1, source_target_pairs={{0,1},{1,0},{2,3},{3,2},{4,5},{5,4},{6,7},{7,6},{8,9},{9,8},{10,11... | collective-permute-start | bytes 2654216 | tf_op jit(solution)/shard_map/ppermute | solution.py:285
  58.4 0.0 all-to-all-done.1.refs_2_
  58.4 9.0 %shard_map.37.refs_4_ = f32[9,64,128]{2,1,0:T(8,128)S(1)} custom-call(s32[4]{0:T(128)S(1)} %broadcast_add_fusion.refs_0_, s32[8,3]{1,0:T(8,128)S(1)} %copy.6.refs_1_, bf16[8,144,128]{2,1,0:T(8,128)(2,1)S(1)} %all-to-all-done.1.refs_2_, bf16[4,864,128]{2,1,0:T(8,128)(2,1)S(1)} %pad_maximum_fusion.refs_3_), custom_call_target="tpu_custom_call" | custom-call | flops 16106127360 | bytes 557056 | tf_op jit(solution)/shard_map/pallas_call | solution.py:206
  67.4 0.0 collective-permute-done.5.refs_3_
  67.4 9.2 %shard_map.38 = f32[8,8,1024]{2,1,0:T(8,128)S(1)} custom-call(s32[4]{0:T(128)S(1)} %add_subtract_fusion.refs_0_, s32[8,3]{1,0:T(8,128)S(1)} %copy.6.refs_1_, bf16[8,144,128]{2,1,0:T(8,128)(2,1)S(1)} %all-to-all-done.1.refs_2_, bf16[4,864,128]{2,1,0:T(8,128)(2,1)S(1)} %collective-permute-done.5.refs_3_, f32[9,64,128]{2,1,0:T(8,128)S(1)} %shard_map.37.refs_4_), custom_call_target="tpu_custom_call" | custom-call | flops 16106127360 | bytes 557056 | tf_op jit(solution)/shard_map/pallas_call | solution.py:206
  76.6 11.3 %all_to_all.15 = f32[8,8,1024]{2,1,0:T(8,128)S(1)} all-to-all(f32[8,8,1024]{2,1,0:T(8,128)S(1)} %shard_map.38), channel_id=1, replica_groups={{0,8,16,24,32,40,48,56},{64,72,80,88,96,104,112,120},{128,136,144,152,1..., dimensions={0} | all-to-all | bytes 524288 | tf_op jit(solution)/shard_map/all_to_all | solution.py:291
  87.9 0.7 copy.9
  (7 shorter events, 0.1 us)
Async XLA Ops:
  0.0 37.6 %copy-start = (s32[512,3]{0,1:T(4,128)S(1)}, s32[512,3]{0,1:T(4,128)}, u32[]{:S(2)}) copy-start(s32[512,3]{0,1:T(4,128)} %param.5) | copy-start | bytes 18436
  1.5 6.3 %copy-start.1 = (bf16[1,3,4,1536]{3,2,1,0:T(4,128)(2,1)S(1)}, bf16[1,3,4,1536]{3,2,1,0:T(4,128)(2,1)}, u32[]{:S(2)}) copy-start(bf16[1,3,4,1536]{3,2,1,0:T(4,128)(2,1)} %param.4) | copy-start | bytes 110596
  1.5 12.1 %all-to-all-start = ((bf16[8,96,128]{2,1,0:T(8,128)(2,1)}), bf16[8,96,128]{2,1,0:T(8,128)(2,1)S(1)}, u32[]{:S(2)}, u32[]{:S(2)}) async-start(bf16[8,96,128]{2,1,0:T(8,128)(2,1)} %broadcast_in_dim.17), calls=%async_computation | async-start | bytes 393216 | tf_op jit(solution)/shard_map/all_to_all | solution.py:240
  7.8 7.4 %collective-permute-start.1 = (bf16[144,128]{1,0:T(8,128)(2,1)S(1)}, bf16[144,128]{1,0:T(8,128)(2,1)S(1)}, u32[]{:S(2)}, u32[]{:S(2)}) collective-permute-start(bf16[144,128]{1,0:T(8,128)(2,1)S(1)} %reshape.17), channel_id=1, source_target_pairs={{0,0},{1,64},{2,128},{3,192},{4,256},{5,320},{6,384},{7,448},{8,8}... | collective-permute-start | bytes 110600 | tf_op jit(solution)/shard_map/ppermute | solution.py:259
  13.6 6.1 %collective-permute-start = (bf16[12,4,128]{2,1,0:T(4,128)(2,1)S(1)}, bf16[12,4,128]{2,1,0:T(4,128)(2,1)S(1)}, u32[]{:S(2)}, u32[]{:S(2)}) collective-permute-start(bf16[12,4,128]{2,1,0:T(4,128)(2,1)S(1)} %slice.9), channel_id=1, source_target_pairs={{64,0},{72,8},{80,16},{88,24},{96,32},{104,40},{112,48},{120,56},{... | collective-permute-start | bytes 36872 | tf_op jit(solution)/shard_map/ppermute | solution.py:267
  20.4 38.0 %all-to-all-start.1 = ((bf16[8,144,128]{2,1,0:T(8,128)(2,1)}), bf16[8,144,128]{2,1,0:T(8,128)(2,1)S(1)}, u32[]{:S(2)}, u32[]{:S(2)}) async-start(bf16[8,144,128]{2,1,0:T(8,128)(2,1)} %broadcast_in_dim.18), calls=%async_computation.1 | async-start | bytes 589824 | tf_op jit(solution)/shard_map/all_to_all | solution.py:240
  38.0 7.3 %collective-permute-start.4 = (bf16[864,128]{1,0:T(8,128)(2,1)S(1)}, bf16[864,128]{1,0:T(8,128)(2,1)S(1)}, u32[]{:S(2)}, u32[]{:S(2)}) collective-permute-start(bf16[864,128]{1,0:T(8,128)(2,1)S(1)} %bitcast.16), channel_id=1, source_target_pairs={{0,6},{1,7},{2,0},{3,1},{4,2},{5,3},{6,4},{7,5},{8,14},{9,15},{10,... | collective-permute-start | bytes 663560 | tf_op jit(solution)/shard_map/ppermute | solution.py:282
  40.4 8.2 %collective-permute-start.3 = (bf16[864,128]{1,0:T(8,128)(2,1)S(1)}, bf16[864,128]{1,0:T(8,128)(2,1)S(1)}, u32[]{:S(2)}, u32[]{:S(2)}) collective-permute-start(bf16[864,128]{1,0:T(8,128)(2,1)S(1)} %bitcast.17), channel_id=1, source_target_pairs={{0,4},{1,5},{2,6},{3,7},{4,0},{5,1},{6,2},{7,3},{8,12},{9,13},{10,... | collective-permute-start | bytes 663560 | tf_op jit(solution)/shard_map/ppermute | solution.py:282
  42.3 11.1 %collective-permute-start.2 = (bf16[864,128]{1,0:T(8,128)(2,1)S(1)}, bf16[864,128]{1,0:T(8,128)(2,1)S(1)}, u32[]{:S(2)}, u32[]{:S(2)}) collective-permute-start(bf16[864,128]{1,0:T(8,128)(2,1)S(1)} %bitcast.18), channel_id=1, source_target_pairs={{0,2},{1,3},{2,4},{3,5},{4,6},{5,7},{6,0},{7,1},{8,10},{9,11},{10,... | collective-permute-start | bytes 663560 | tf_op jit(solution)/shard_map/ppermute | solution.py:282
  53.5 13.9 %collective-permute-start.5 = (bf16[4,864,128]{2,1,0:T(8,128)(2,1)S(1)}, bf16[4,864,128]{2,1,0:T(8,128)(2,1)S(1)}, u32[]{:S(2)}, u32[]{:S(2)}) collective-permute-start(bf16[4,864,128]{2,1,0:T(8,128)(2,1)S(1)} %pad_maximum_fusion.refs_3_), channel_id=1, source_target_pairs={{0,1},{1,0},{2,3},{3,2},{4,5},{5,4},{6,7},{7,6},{8,9},{9,8},{10,11... | collective-permute-start | bytes 2654216 | tf_op jit(solution)/shard_map/ppermute | solution.py:285

commit v9 on v8

--- a/solution.py
+++ b/solution.py
@@ -250,23 +250,17 @@
     far = [[a * n_b + b for a in range(n_a)] for b in range(n_b)]
     spread = template_groups.shape[1]
 
-    turn = [
-        ((a * n_b + b) * n_sta + t, (t * n_b + b) * n_sta + a)
-        for a in range(n_a)
-        for b in range(n_b)
-        for t in range(n_sta)
-    ]
-    own = lax.ppermute(templates.reshape(-1, LANES), ("tm", "sta"), turn)
     first = (s * n_b + lax.rem(m, n_b)) * n_a
     groups = lax.dynamic_slice_in_dim(template_groups, first, n_a, 0)
 
     lines = channels * stations
     steps = samples // LANES
     around = copies_to(record.reshape(lines * steps, LANES), "tm", near)
+    around, own = lax.optimization_barrier((around, templates.reshape(-1, LANES)))
+    block = copies_to(own, "tm", far)
+    block = lax.all_to_all(block, "sta", 0, 0, tiled=True)
     front = around[0].reshape(lines, steps, LANES)[:, : L // LANES]
     tail = lax.ppermute(front, "tm", [(i + n_b, i) for i in range(n_tm - n_b)])
-    tail, own = lax.optimization_barrier((tail, own))
-    block = copies_to(own, "tm", far)
     main = around.reshape(n_b, lines, steps, LANES)
     main = main.transpose(1, 0, 2, 3).reshape(lines, n_b * steps, LANES)
     rest = jnp.zeros((lines, 8 - L // LANES, LANES), record.dtype)

time: 90 us -> 93.7 us (1.041)
  the two profiles are of different devices: /device:TPU:1 before, /device:TPU:64 now
where the time goes in v9:
time: 93.7 us; the launch traced here: 93.1 us
  starting transfers between devices  37.4 us (40%)
  waiting for transfers between devices  24.4 us (26%)
  Pallas kernels  18.1 us (19%)
  blocking collectives  9.64 us (10%)
  local copies, waits for them, and re-layouts  3.23 us (3%)
    all_to_all x2, starting transfers between devices, copies_to(): lax.all_to_all(spread, axis, 0, 0, axis_index_groups=groups, tiled=True)  19.6 us
    pallas_call x2, Pallas kernels, detect(): pl.pallas_call(body, out_shape=out_shape, in_specs=[pl.BlockSpec(memory_s...  18.1 us
    ppermute x1, waiting for transfers between devices, on_device(): tail = lax.ppermute(front, 'tm', [(i + n_b, i) for i in range(n_tm - n_b)])  11.7 us
    ppermute x3, starting transfers between devices, on_device(): pieces.append(lax.ppermute(mine, 'sta', pairs))  10.3 us
    all_to_all x1, blocking collectives, on_device(): lax.all_to_all(total, 'tm', 0, 0, axis_index_groups=near, tiled=True)  9.64 us
    all_to_all x2, waiting for transfers between devices, copies_to(): lax.all_to_all(spread, axis, 0, 0, axis_index_groups=groups, tiled=True)  6.9 us
    ppermute x3, waiting for transfers between devices, on_device(): pieces.append(lax.ppermute(mine, 'sta', pairs))  3.97 us
    all_to_all x1, starting transfers between devices, on_device(): block = lax.all_to_all(block, 'sta', 0, 0, tiled=True)  3.55 us
  transfers between devices with their start and end apart: 8, of which 5 were waited for; matrix products, arithmetic and copies ran while one was open for 1% of the time, Pallas kernels for 10%

profile of v9, /device:TPU:64, one launch (start us, length us, event | category | flops | bytes accessed | tf_op | source)
XLA Modules:
  0.0 93.1 jit_solution(867432139945958753)
XLA Ops:
  0.0 0.0 copy-start
  0.0 0.8 broadcast_in_dim.16
  0.8 0.7 broadcast_in_dim.17
  1.5 0.0 copy-start.1
  1.5 5.8 %all-to-all-start = ((bf16[8,96,128]{2,1,0:T(8,128)(2,1)}), bf16[8,96,128]{2,1,0:T(8,128)(2,1)S(1)}, u32[]{:S(2)}, u32[]{:S(2)}) async-start(bf16[8,96,128]{2,1,0:T(8,128)(2,1)} %broadcast_in_dim.17), calls=%async_computation | async-start | bytes 393216 | tf_op jit(solution)/shard_map/all_to_all | solution.py:240
  7.3 0.0 copy-done.1
  7.3 6.9 %all-to-all-done = bf16[8,96,128]{2,1,0:T(8,128)(2,1)S(1)} async-done(((bf16[8,96,128]{2,1,0:T(8,128)(2,1)}), bf16[8,96,128]{2,1,0:T(8,128)(2,1)S(1)}, u32[]{:S(2)}, u32[]{:S(2)}) %all-to-all-start) | async-done | bytes 196640 | tf_op jit(solution)/shard_map/all_to_all | solution.py:240
  14.2 0.7 broadcast_in_dim.18
  14.9 13.8 %all-to-all-start.1 = ((bf16[8,144,128]{2,1,0:T(8,128)(2,1)}), bf16[8,144,128]{2,1,0:T(8,128)(2,1)}, u32[]{:S(2)}, u32[]{:S(2)}) async-start(bf16[8,144,128]{2,1,0:T(8,128)(2,1)} %broadcast_in_dim.18), calls=%async_computation.1 | async-start | bytes 589824 | tf_op jit(solution)/shard_map/all_to_all | solution.py:240
  28.8 0.1 pad.6.clone
  28.9 0.0 copy-done
  28.9 0.1 constant_dynamic-slice_fusion
  29.0 1.9 %collective-permute-start = (bf16[12,4,128]{2,1,0:T(4,128)(2,1)S(1)}, bf16[12,4,128]{2,1,0:T(4,128)(2,1)S(1)}, u32[]{:S(2)}, u32[]{:S(2)}) collective-permute-start(bf16[12,4,128]{2,1,0:T(4,128)(2,1)S(1)} %slice.8), channel_id=1, source_target_pairs={{64,0},{72,8},{80,16},{88,24},{96,32},{104,40},{112,48},{120,56},{... | collective-permute-start | bytes 36872 | tf_op jit(solution)/shard_map/ppermute | solution.py:263
  30.9 11.7 %collective-permute-done = bf16[12,4,128]{2,1,0:T(4,128)(2,1)S(1)} collective-permute-done((bf16[12,4,128]{2,1,0:T(4,128)(2,1)S(1)}, bf16[12,4,128]{2,1,0:T(4,128)(2,1)S(1)}, u32[]{:S(2)}, u32[]{:S(2)}) %collective-permute-start) | collective-permute-done | bytes 12320 | tf_op jit(solution)/shard_map/ppermute | solution.py:263
  42.6 0.1 maximum_maximum_fusion
  42.8 4.9 %collective-permute-start.3 = (bf16[864,128]{1,0:T(8,128)(2,1)S(1)}, bf16[864,128]{1,0:T(8,128)(2,1)S(1)}, u32[]{:S(2)}, u32[]{:S(2)}) collective-permute-start(bf16[864,128]{1,0:T(8,128)(2,1)S(1)} %bitcast.16), channel_id=1, source_target_pairs={{0,6},{1,7},{2,0},{3,1},{4,2},{5,3},{6,4},{7,5},{8,14},{9,15},{10,... | collective-permute-start | bytes 663560 | tf_op jit(solution)/shard_map/ppermute | solution.py:276
  47.7 2.5 %collective-permute-start.2 = (bf16[864,128]{1,0:T(8,128)(2,1)S(1)}, bf16[864,128]{1,0:T(8,128)(2,1)S(1)}, u32[]{:S(2)}, u32[]{:S(2)}) collective-permute-start(bf16[864,128]{1,0:T(8,128)(2,1)S(1)} %bitcast.17), channel_id=1, source_target_pairs={{0,4},{1,5},{2,6},{3,7},{4,0},{5,1},{6,2},{7,3},{8,12},{9,13},{10,... | collective-permute-start | bytes 663560 | tf_op jit(solution)/shard_map/ppermute | solution.py:276
  50.2 2.9 %collective-permute-start.1 = (bf16[864,128]{1,0:T(8,128)(2,1)S(1)}, bf16[864,128]{1,0:T(8,128)(2,1)S(1)}, u32[]{:S(2)}, u32[]{:S(2)}) collective-permute-start(bf16[864,128]{1,0:T(8,128)(2,1)S(1)} %bitcast.18), channel_id=1, source_target_pairs={{0,2},{1,3},{2,4},{3,5},{4,6},{5,7},{6,0},{7,1},{8,10},{9,11},{10,... | collective-permute-start | bytes 663560 | tf_op jit(solution)/shard_map/ppermute | solution.py:276
  53.1 0.0 all-to-all-done.1
  53.1 3.6 %all-to-all-start.2 = ((bf16[8,144,128]{2,1,0:T(8,128)(2,1)}), bf16[8,144,128]{2,1,0:T(8,128)(2,1)S(1)}, u32[]{:S(2)}, u32[]{:S(2)}) async-start(bf16[8,144,128]{2,1,0:T(8,128)(2,1)} %all-to-all-done.1), calls=%async_computation.2 | async-start | bytes 589824 | tf_op jit(solution)/shard_map/all_to_all | solution.py:261
  56.7 0.1 copy.6.refs_1_
  56.8 0.0 collective-permute-done.3
  56.8 1.7 %collective-permute-done.2 = bf16[864,128]{1,0:T(8,128)(2,1)S(1)} collective-permute-done((bf16[864,128]{1,0:T(8,128)(2,1)S(1)}, bf16[864,128]{1,0:T(8,128)(2,1)S(1)}, u32[]{:S(2)}, u32[]{:S(2)}) %collective-permute-start.2) | collective-permute-done | bytes 221216 | tf_op jit(solution)/shard_map/ppermute | solution.py:276
  58.5 2.3 %collective-permute-done.1 = bf16[864,128]{1,0:T(8,128)(2,1)S(1)} collective-permute-done((bf16[864,128]{1,0:T(8,128)(2,1)S(1)}, bf16[864,128]{1,0:T(8,128)(2,1)S(1)}, u32[]{:S(2)}, u32[]{:S(2)}) %collective-permute-start.1) | collective-permute-done | bytes 221216 | tf_op jit(solution)/shard_map/ppermute | solution.py:276
  60.8 0.1 pad_maximum_fusion.refs_3_
  60.9 1.9 %collective-permute-start.4 = (bf16[4,864,128]{2,1,0:T(8,128)(2,1)S(1)}, bf16[4,864,128]{2,1,0:T(8,128)(2,1)S(1)}, u32[]{:S(2)}, u32[]{:S(2)}) collective-permute-start(bf16[4,864,128]{2,1,0:T(8,128)(2,1)S(1)} %pad_maximum_fusion.refs_3_), channel_id=1, source_target_pairs={{0,1},{1,0},{2,3},{3,2},{4,5},{5,4},{6,7},{7,6},{8,9},{9,8},{10,11... | collective-permute-start | bytes 2654216 | tf_op jit(solution)/shard_map/ppermute | solution.py:279
  62.8 1.8 %all-to-all-done.2.refs_2_ = bf16[8,144,128]{2,1,0:T(8,128)(2,1)S(1)} async-done(((bf16[8,144,128]{2,1,0:T(8,128)(2,1)}), bf16[8,144,128]{2,1,0:T(8,128)(2,1)S(1)}, u32[]{:S(2)}, u32[]{:S(2)}) %all-to-all-start.2) | async-done | bytes 294944 | tf_op jit(solution)/shard_map/all_to_all | solution.py:261
  64.6 9.0 %shard_map.37.refs_4_ = f32[9,64,128]{2,1,0:T(8,128)S(1)} custom-call(s32[4]{0:T(128)S(1)} %broadcast_add_fusion.refs_0_, s32[8,3]{1,0:T(8,128)S(1)} %copy.6.refs_1_, bf16[8,144,128]{2,1,0:T(8,128)(2,1)S(1)} %all-to-all-done.2.refs_2_, bf16[4,864,128]{2,1,0:T(8,128)(2,1)S(1)} %pad_maximum_fusion.refs_3_), custom_call_target="tpu_custom_call" | custom-call | flops 16106127360 | bytes 557056 | tf_op jit(solution)/shard_map/pallas_call | solution.py:206
  73.6 0.0 collective-permute-done.4.refs_3_
  73.6 9.2 %shard_map.38 = f32[8,8,1024]{2,1,0:T(8,128)S(1)} custom-call(s32[4]{0:T(128)S(1)} %add_subtract_fusion.refs_0_, s32[8,3]{1,0:T(8,128)S(1)} %copy.6.refs_1_, bf16[8,144,128]{2,1,0:T(8,128)(2,1)S(1)} %all-to-all-done.2.refs_2_, bf16[4,864,128]{2,1,0:T(8,128)(2,1)S(1)} %collective-permute-done.4.refs_3_, f32[9,64,128]{2,1,0:T(8,128)S(1)} %shard_map.37.refs_4_), custom_call_target="tpu_custom_call" | custom-call | flops 16106127360 | bytes 557056 | tf_op jit(solution)/shard_map/pallas_call | solution.py:206
  82.7 9.6 %all_to_all.20 = f32[8,8,1024]{2,1,0:T(8,128)S(1)} all-to-all(f32[8,8,1024]{2,1,0:T(8,128)S(1)} %shard_map.38), channel_id=1, replica_groups={{0,8,16,24,32,40,48,56},{64,72,80,88,96,104,112,120},{128,136,144,152,1..., dimensions={0} | all-to-all | bytes 524288 | tf_op jit(solution)/shard_map/all_to_all | solution.py:285
  92.4 0.7 copy.9
  (7 shorter events, 0.1 us)
Async XLA Ops:
  0.0 28.9 %copy-start = (s32[512,3]{0,1:T(4,128)S(1)}, s32[512,3]{0,1:T(4,128)}, u32[]{:S(2)}) copy-start(s32[512,3]{0,1:T(4,128)} %param.5) | copy-start | bytes 18436
  1.5 5.8 %copy-start.1 = (bf16[1,3,4,1536]{3,2,1,0:T(4,128)(2,1)S(1)}, bf16[1,3,4,1536]{3,2,1,0:T(4,128)(2,1)}, u32[]{:S(2)}) copy-start(bf16[1,3,4,1536]{3,2,1,0:T(4,128)(2,1)} %param.4) | copy-start | bytes 110596
  1.5 12.7 %all-to-all-start = ((bf16[8,96,128]{2,1,0:T(8,128)(2,1)}), bf16[8,96,128]{2,1,0:T(8,128)(2,1)S(1)}, u32[]{:S(2)}, u32[]{:S(2)}) async-start(bf16[8,96,128]{2,1,0:T(8,128)(2,1)} %broadcast_in_dim.17), calls=%async_computation | async-start | bytes 393216 | tf_op jit(solution)/shard_map/all_to_all | solution.py:240
  14.9 38.2 %all-to-all-start.1 = ((bf16[8,144,128]{2,1,0:T(8,128)(2,1)}), bf16[8,144,128]{2,1,0:T(8,128)(2,1)}, u32[]{:S(2)}, u32[]{:S(2)}) async-start(bf16[8,144,128]{2,1,0:T(8,128)(2,1)} %broadcast_in_dim.18), calls=%async_computation.1 | async-start | bytes 589824 | tf_op jit(solution)/shard_map/all_to_all | solution.py:240
  29.0 13.7 %collective-permute-start = (bf16[12,4,128]{2,1,0:T(4,128)(2,1)S(1)}, bf16[12,4,128]{2,1,0:T(4,128)(2,1)S(1)}, u32[]{:S(2)}, u32[]{:S(2)}) collective-permute-start(bf16[12,4,128]{2,1,0:T(4,128)(2,1)S(1)} %slice.8), channel_id=1, source_target_pairs={{64,0},{72,8},{80,16},{88,24},{96,32},{104,40},{112,48},{120,56},{... | collective-permute-start | bytes 36872 | tf_op jit(solution)/shard_map/ppermute | solution.py:263
  42.8 14.0 %collective-permute-start.3 = (bf16[864,128]{1,0:T(8,128)(2,1)S(1)}, bf16[864,128]{1,0:T(8,128)(2,1)S(1)}, u32[]{:S(2)}, u32[]{:S(2)}) collective-permute-start(bf16[864,128]{1,0:T(8,128)(2,1)S(1)} %bitcast.16), channel_id=1, source_target_pairs={{0,6},{1,7},{2,0},{3,1},{4,2},{5,3},{6,4},{7,5},{8,14},{9,15},{10,... | collective-permute-start | bytes 663560 | tf_op jit(solution)/shard_map/ppermute | solution.py:276
  47.7 10.8 %collective-permute-start.2 = (bf16[864,128]{1,0:T(8,128)(2,1)S(1)}, bf16[864,128]{1,0:T(8,128)(2,1)S(1)}, u32[]{:S(2)}, u32[]{:S(2)}) collective-permute-start(bf16[864,128]{1,0:T(8,128)(2,1)S(1)} %bitcast.17), channel_id=1, source_target_pairs={{0,4},{1,5},{2,6},{3,7},{4,0},{5,1},{6,2},{7,3},{8,12},{9,13},{10,... | collective-permute-start | bytes 663560 | tf_op jit(solution)/shard_map/ppermute | solution.py:276
  50.2 10.5 %collective-permute-start.1 = (bf16[864,128]{1,0:T(8,128)(2,1)S(1)}, bf16[864,128]{1,0:T(8,128)(2,1)S(1)}, u32[]{:S(2)}, u32[]{:S(2)}) collective-permute-start(bf16[864,128]{1,0:T(8,128)(2,1)S(1)} %bitcast.18), channel_id=1, source_target_pairs={{0,2},{1,3},{2,4},{3,5},{4,6},{5,7},{6,0},{7,1},{8,10},{9,11},{10,... | collective-permute-start | bytes 663560 | tf_op jit(solution)/shard_map/ppermute | solution.py:276
  53.1 11.4 %all-to-all-start.2 = ((bf16[8,144,128]{2,1,0:T(8,128)(2,1)}), bf16[8,144,128]{2,1,0:T(8,128)(2,1)S(1)}, u32[]{:S(2)}, u32[]{:S(2)}) async-start(bf16[8,144,128]{2,1,0:T(8,128)(2,1)} %all-to-all-done.1), calls=%async_computation.2 | async-start | bytes 589824 | tf_op jit(solution)/shard_map/all_to_all | solution.py:261
  60.9 12.7 %collective-permute-start.4 = (bf16[4,864,128]{2,1,0:T(8,128)(2,1)S(1)}, bf16[4,864,128]{2,1,0:T(8,128)(2,1)S(1)}, u32[]{:S(2)}, u32[]{:S(2)}) collective-permute-start(bf16[4,864,128]{2,1,0:T(8,128)(2,1)S(1)} %pad_maximum_fusion.refs_3_), channel_id=1, source_target_pairs={{0,1},{1,0},{2,3},{3,2},{4,5},{5,4},{6,7},{7,6},{8,9},{9,8},{10,11... | collective-permute-start | bytes 2654216 | tf_op jit(solution)/shard_map/ppermute | solution.py:279

commit v10 on v9

--- a/solution.py
+++ b/solution.py
@@ -16,7 +16,7 @@
 
 
 def detect_kernel(
-    padded,
+    each,
     factor,
     order_ref,
     groups_ref,
@@ -28,6 +28,7 @@
     home,
     count,
     wide,
+    tails,
     waves,
     norms,
     band,
@@ -43,6 +44,9 @@
     block, spread = groups_ref.shape
     n_group = series_ref.shape[0]
     rows = total.shape[1]
+    padded = rows + 8
+    ahead = tails.shape[0] // templates_ref.shape[0]
+    tail = L // LANES
     parts = 3 * L // LANES
     slots = wide.shape[0] // parts
     stations = slots // (block * spread)
@@ -66,8 +70,9 @@
             count[named] = count[named] + 1
     spare = waves.shape[0] - slots
     for r in range(block):
-        each = slots // block * parts
-        wide[r * each : (r + 1) * each, :] = templates_ref[r, -each:, :].astype(jnp.float32)
+        wide[r * each : (r + 1) * each, :] = templates_ref[r, 0:each, :].astype(jnp.float32)
+    for n in range(templates_ref.shape[0]):
+        tails[n * ahead : (n + 1) * ahead, :] = templates_ref[n, each:, :].astype(jnp.float32)
     for c in range(3):
         for v in range(L // LANES):
             at = c * SPAN + v * LANES
@@ -82,7 +87,7 @@
     band[0:LANES, :] = jnp.where(r >= l, 1.0, 0.0).astype(jnp.bfloat16)
     band[LANES : 2 * LANES, :] = jnp.ones((LANES, LANES), jnp.bfloat16)
     band[2 * LANES :, :] = jnp.where(r < l, 1.0, 0.0).astype(jnp.bfloat16)
-    shifts[:, :, padded:, :] = jnp.zeros((3, 2, 8, LANES), jnp.float32)
+    shifts[:, :, rows:, :] = jnp.zeros((3, 2, 16, LANES), jnp.float32)
     if before_ref is None:
         total[...] = jnp.zeros_like(total)
     else:
@@ -91,10 +96,13 @@
     def prepare(group, station, buffer):
         squares = jnp.zeros((padded, LANES), jnp.float32)
         for c in range(3):
-            at = (c * stations + station) * padded
-            plain = series_ref[group, at : at + padded, :].astype(jnp.float32)
+            line = c * stations + station
+            main = series_ref[group, line * rows : (line + 1) * rows, :]
+            shifts[c, 0, 0:rows, :] = main.astype(jnp.float32)
+            at = order_ref[group] * ahead + line * tail
+            shifts[c, 0, rows : rows + tail, :] = tails[pl.ds(at, tail), :]
+            plain = shifts[c, 0, 0:padded, :]
             squares = squares + plain * plain
-            shifts[c, 0, 0:padded, :] = plain
             after = shifts[c, 0, 1 : padded + 1, :]
             shifts[c, 1, 0:padded, :] = pltpu.roll(jnp.where(low, after, plain), HALF, 1)
         energy[...] = squares
@@ -180,11 +188,13 @@
             out_ref[w, :, i * LANES : (i + 1) * LANES] = turned[w * (samples // LANES) + i]
 
 
-def detect(order, groups, templates, series, before, n_all, padded, parts, factor):
+def detect(order, groups, templates, series, before, each, parts, factor):
+    n_all = templates.shape[0]
     block, spread = groups.shape
     stations = 4
     slots = block * spread * stations
-    rows = padded - 8
+    rows = series.shape[1] // (3 * stations)
+    padded = rows + 8
     samples = rows * LANES // parts
     spare = -(-(slots + stations) // 8) * 8
     if factor is None:
@@ -201,7 +211,7 @@
         refs = list(refs)
         if before is None:
             refs.insert(4, None)
-        detect_kernel(padded, factor, *refs)
+        detect_kernel(each, factor, *refs)
 
     return pl.pallas_call(
         body,
@@ -213,6 +223,7 @@
             pltpu.SMEM((n_all * SLOTS,), jnp.int32),
             pltpu.SMEM((n_all,), jnp.int32),
             pltpu.VMEM((slots * 3 * L // LANES, LANES), jnp.float32),
+            pltpu.VMEM((n_all * (templates.shape[1] - each), LANES), jnp.float32),
             pltpu.VMEM((spare, 3 * SPAN), jnp.float32),
             pltpu.VMEM((spare, LANES), jnp.float32),
             pltpu.VMEM((3 * LANES, LANES), jnp.bfloat16),
@@ -257,15 +268,13 @@
     steps = samples // LANES
     around = copies_to(record.reshape(lines * steps, LANES), "tm", near)
     around, own = lax.optimization_barrier((around, templates.reshape(-1, LANES)))
-    block = copies_to(own, "tm", far)
-    block = lax.all_to_all(block, "sta", 0, 0, tiled=True)
     front = around[0].reshape(lines, steps, LANES)[:, : L // LANES]
     tail = lax.ppermute(front, "tm", [(i + n_b, i) for i in range(n_tm - n_b)])
+    tail = jnp.broadcast_to(tail.reshape(1, -1, LANES), (n_sta, lines * L // LANES, LANES))
+    block = copies_to(own, "tm", far)
+    block = lax.all_to_all(jnp.concatenate([block, tail], axis=1), "sta", 0, 0, tiled=True)
     main = around.reshape(n_b, lines, steps, LANES)
-    main = main.transpose(1, 0, 2, 3).reshape(lines, n_b * steps, LANES)
-    rest = jnp.zeros((lines, 8 - L // LANES, LANES), record.dtype)
-    padded = n_b * steps + 8
-    mine = jnp.concatenate([main, tail, rest], axis=1).reshape(-1, LANES)
+    mine = main.transpose(1, 0, 2, 3).reshape(-1, LANES)
 
     cores = 2
     n_y = n_sta // cores
@@ -279,8 +288,9 @@
     others = lax.ppermute(pieces, "sta", swap)
     rows_of_y = lax.rem(y - jnp.arange(n_y, dtype=jnp.int32) + n_y, n_y) * cores
     factor = math.sqrt(channels * L / (spread * stations))
-    total = detect(rows_of_y + core, groups, block, pieces, None, n_sta, padded, n_b, None)
-    total = detect(rows_of_y + 1 - core, groups, block, others, total, n_sta, padded, n_b, factor)
+    total = detect(rows_of_y + core, groups, block, pieces, None, own.shape[0], n_b, None)
+    other = rows_of_y + 1 - core
+    total = detect(other, groups, block, others, total, own.shape[0], n_b, factor)
 
     found = lax.all_to_all(total, "tm", 0, 0, axis_index_groups=near, tiled=True)
     return found.reshape(n_b * n_a, samples)

time: 93.7 us -> 93.3 us (level)
  the two profiles are of different devices: /device:TPU:64 before, /device:TPU:1 now
where the time goes in v10:
time: 93.3 us; the launch traced here: 92.6 us
  starting transfers between devices  41.1 us (44%)
  waiting for transfers between devices  20.1 us (22%)
  Pallas kernels  18.6 us (20%)
  blocking collectives  8.54 us (9%)
  local copies, waits for them, and re-layouts  3.19 us (3%)
    all_to_all x2, starting transfers between devices, copies_to(): lax.all_to_all(spread, axis, 0, 0, axis_index_groups=groups, tiled=True)  20.3 us
    pallas_call x2, Pallas kernels, detect(): pl.pallas_call(body, out_shape=out_shape, in_specs=[pl.BlockSpec(memory_s...  18.6 us
    all_to_all x2, waiting for transfers between devices, copies_to(): lax.all_to_all(spread, axis, 0, 0, axis_index_groups=groups, tiled=True)  14.2 us
    ppermute x3, starting transfers between devices, on_device(): pieces.append(lax.ppermute(mine, 'sta', pairs))  9.5 us
    all_to_all x1, blocking collectives, on_device(): lax.all_to_all(total, 'tm', 0, 0, axis_index_groups=near, tiled=True)  8.54 us
    all_to_all x1, starting transfers between devices, on_device(): lax.all_to_all(jnp.concatenate([block, tail], axis=1), 'sta', 0, 0, tiled...  8.05 us
    all_to_all x1, waiting for transfers between devices, on_device(): lax.all_to_all(jnp.concatenate([block, tail], axis=1), 'sta', 0, 0, tiled...  5.98 us
    broadcast_in_dim x3, local copies, waits for them, and re-layouts, copies_to(): spread = jnp.broadcast_to(value[None], (count,) + value.shape)  2.23 us
  transfers between devices with their start and end apart: 8, of which 3 were waited for; matrix products, arithmetic and copies ran while one was open for 1% of the time, Pallas kernels for 10%

profile of v10, /device:TPU:1, one launch (start us, length us, event | category | flops | bytes accessed | tf_op | source)
XLA Modules:
  0.0 92.6 jit_solution(14627515910503941391)
XLA Ops:
  0.0 0.0 copy-start
  0.0 0.8 broadcast_in_dim.20
  0.8 0.7 broadcast_in_dim.21
  1.5 0.0 copy-start.1
  1.5 6.3 %all-to-all-start = ((bf16[8,96,128]{2,1,0:T(8,128)(2,1)}), bf16[8,96,128]{2,1,0:T(8,128)(2,1)S(1)}, u32[]{:S(2)}, u32[]{:S(2)}) async-start(bf16[8,96,128]{2,1,0:T(8,128)(2,1)} %broadcast_in_dim.21), calls=%async_computation | async-start | bytes 393216 | tf_op jit(solution)/shard_map/all_to_all | solution.py:251
  7.8 0.0 copy-done.1
  7.8 5.8 %all-to-all-done = bf16[8,96,128]{2,1,0:T(8,128)(2,1)S(1)} async-done(((bf16[8,96,128]{2,1,0:T(8,128)(2,1)}), bf16[8,96,128]{2,1,0:T(8,128)(2,1)S(1)}, u32[]{:S(2)}, u32[]{:S(2)}) %all-to-all-start) | async-done | bytes 196640 | tf_op jit(solution)/shard_map/all_to_all | solution.py:251
  13.6 0.8 broadcast_in_dim.22
  14.4 14.0 %all-to-all-start.1 = ((bf16[8,144,128]{2,1,0:T(8,128)(2,1)}), bf16[8,144,128]{2,1,0:T(8,128)(2,1)S(1)}, u32[]{:S(2)}, u32[]{:S(2)}) async-start(bf16[8,144,128]{2,1,0:T(8,128)(2,1)} %broadcast_in_dim.22), calls=%async_computation.1 | async-start | bytes 589824 | tf_op jit(solution)/shard_map/all_to_all | solution.py:251
  28.4 1.3 %collective-permute-start = (bf16[12,4,128]{2,1,0:T(4,128)(2,1)S(1)}, bf16[12,4,128]{2,1,0:T(4,128)(2,1)S(1)}, u32[]{:S(2)}, u32[]{:S(2)}) collective-permute-start(bf16[12,4,128]{2,1,0:T(4,128)(2,1)S(1)} %slice.8), channel_id=1, source_target_pairs={{64,0},{72,8},{80,16},{88,24},{96,32},{104,40},{112,48},{120,56},{... | collective-permute-start | bytes 36872 | tf_op jit(solution)/shard_map/ppermute | solution.py:272
  29.7 0.0 copy-done
  29.7 0.1 constant_dynamic-slice_fusion
  29.8 0.1 copy.8.refs_1_
  29.9 4.6 %collective-permute-start.3 = (bf16[768,128]{1,0:T(8,128)(2,1)S(1)}, bf16[768,128]{1,0:T(8,128)(2,1)S(1)}, u32[]{:S(2)}, u32[]{:S(2)}) collective-permute-start(bf16[768,128]{1,0:T(8,128)(2,1)S(1)} %bitcast.14), channel_id=1, source_target_pairs={{0,6},{1,7},{2,0},{3,1},{4,2},{5,3},{6,4},{7,5},{8,14},{9,15},{10,... | collective-permute-start | bytes 589832 | tf_op jit(solution)/shard_map/ppermute | solution.py:285
  34.6 2.3 %collective-permute-start.2 = (bf16[768,128]{1,0:T(8,128)(2,1)S(1)}, bf16[768,128]{1,0:T(8,128)(2,1)S(1)}, u32[]{:S(2)}, u32[]{:S(2)}) collective-permute-start(bf16[768,128]{1,0:T(8,128)(2,1)S(1)} %bitcast.15), channel_id=1, source_target_pairs={{0,4},{1,5},{2,6},{3,7},{4,0},{5,1},{6,2},{7,3},{8,12},{9,13},{10,... | collective-permute-start | bytes 589832 | tf_op jit(solution)/shard_map/ppermute | solution.py:285
  36.8 2.6 %collective-permute-start.1 = (bf16[768,128]{1,0:T(8,128)(2,1)S(1)}, bf16[768,128]{1,0:T(8,128)(2,1)S(1)}, u32[]{:S(2)}, u32[]{:S(2)}) collective-permute-start(bf16[768,128]{1,0:T(8,128)(2,1)S(1)} %bitcast.16), channel_id=1, source_target_pairs={{0,2},{1,3},{2,4},{3,5},{4,6},{5,7},{6,0},{7,1},{8,10},{9,11},{10,... | collective-permute-start | bytes 589832 | tf_op jit(solution)/shard_map/ppermute | solution.py:285
  39.4 0.0 collective-permute-done
  39.4 8.4 %all-to-all-done.1 = bf16[8,144,128]{2,1,0:T(8,128)(2,1)S(1)} async-done(((bf16[8,144,128]{2,1,0:T(8,128)(2,1)}), bf16[8,144,128]{2,1,0:T(8,128)(2,1)S(1)}, u32[]{:S(2)}, u32[]{:S(2)}) %all-to-all-start.1) | async-done | bytes 294944 | tf_op jit(solution)/shard_map/all_to_all | solution.py:251
  47.9 0.8 pad_maximum_fusion.1
  48.6 8.0 %all-to-all-start.2 = ((bf16[8,192,128]{2,1,0:T(8,128)(2,1)}), bf16[8,192,128]{2,1,0:T(8,128)(2,1)S(1)}, u32[]{:S(2)}, u32[]{:S(2)}) async-start(bf16[8,192,128]{2,1,0:T(8,128)(2,1)} %pad_maximum_fusion.1), calls=%async_computation.2 | async-start | bytes 786432 | tf_op jit(solution)/shard_map/all_to_all | solution.py:275
  56.7 0.0 collective-permute-done.3
  56.7 0.0 collective-permute-done.2
  56.7 0.0 collective-permute-done.1
  56.7 0.1 pad_maximum_fusion.refs_3_
  56.8 1.9 %collective-permute-start.4 = (bf16[4,768,128]{2,1,0:T(8,128)(2,1)S(1)}, bf16[4,768,128]{2,1,0:T(8,128)(2,1)S(1)}, u32[]{:S(2)}, u32[]{:S(2)}) collective-permute-start(bf16[4,768,128]{2,1,0:T(8,128)(2,1)S(1)} %pad_maximum_fusion.refs_3_), channel_id=1, source_target_pairs={{0,1},{1,0},{2,3},{3,2},{4,5},{5,4},{6,7},{7,6},{8,9},{9,8},{10,11... | collective-permute-start | bytes 2359304 | tf_op jit(solution)/shard_map/ppermute | solution.py:288
  58.8 6.0 %all-to-all-done.2.refs_2_ = bf16[8,192,128]{2,1,0:T(8,128)(2,1)S(1)} async-done(((bf16[8,192,128]{2,1,0:T(8,128)(2,1)}), bf16[8,192,128]{2,1,0:T(8,128)(2,1)S(1)}, u32[]{:S(2)}, u32[]{:S(2)}) %all-to-all-start.2) | async-done | bytes 393248 | tf_op jit(solution)/shard_map/all_to_all | solution.py:275
  64.8 9.2 %shard_map.37.refs_4_ = f32[9,64,128]{2,1,0:T(8,128)S(1)} custom-call(s32[4]{0:T(128)S(1)} %broadcast_add_fusion.refs_0_, s32[8,3]{1,0:T(8,128)S(1)} %copy.8.refs_1_, bf16[8,192,128]{2,1,0:T(8,128)(2,1)S(1)} %all-to-all-done.2.refs_2_, bf16[4,768,128]{2,1,0:T(8,128)(2,1)S(1)} %pad_maximum_fusion.refs_3_), custom_call_target="tpu_custom_call" | custom-call | flops 16106127360 | bytes 655360 | tf_op jit(solution)/shard_map/pallas_call | solution.py:216
  74.0 0.0 collective-permute-done.4.refs_3_
  74.0 9.4 %shard_map.38 = f32[8,8,1024]{2,1,0:T(8,128)S(1)} custom-call(s32[4]{0:T(128)S(1)} %add_subtract_fusion.refs_0_, s32[8,3]{1,0:T(8,128)S(1)} %copy.8.refs_1_, bf16[8,192,128]{2,1,0:T(8,128)(2,1)S(1)} %all-to-all-done.2.refs_2_, bf16[4,768,128]{2,1,0:T(8,128)(2,1)S(1)} %collective-permute-done.4.refs_3_, f32[9,64,128]{2,1,0:T(8,128)S(1)} %shard_map.37.refs_4_), custom_call_target="tpu_custom_call" | custom-call | flops 16106127360 | bytes 655360 | tf_op jit(solution)/shard_map/pallas_call | solution.py:216
  83.4 8.5 %all_to_all.20 = f32[8,8,1024]{2,1,0:T(8,128)S(1)} all-to-all(f32[8,8,1024]{2,1,0:T(8,128)S(1)} %shard_map.38), channel_id=1, replica_groups={{0,8,16,24,32,40,48,56},{64,72,80,88,96,104,112,120},{128,136,144,152,1..., dimensions={0} | all-to-all | bytes 524288 | tf_op jit(solution)/shard_map/all_to_all | solution.py:295
  91.9 0.7 copy.10
  (7 shorter events, 0.1 us)
Async XLA Ops:
  0.0 29.7 %copy-start = (s32[512,3]{0,1:T(4,128)S(1)}, s32[512,3]{0,1:T(4,128)}, u32[]{:S(2)}) copy-start(s32[512,3]{0,1:T(4,128)} %param.5) | copy-start | bytes 18436
  1.5 6.3 %copy-start.1 = (bf16[1,3,4,1536]{3,2,1,0:T(4,128)(2,1)S(1)}, bf16[1,3,4,1536]{3,2,1,0:T(4,128)(2,1)}, u32[]{:S(2)}) copy-start(bf16[1,3,4,1536]{3,2,1,0:T(4,128)(2,1)} %param.4) | copy-start | bytes 110596
  1.5 12.1 %all-to-all-start = ((bf16[8,96,128]{2,1,0:T(8,128)(2,1)}), bf16[8,96,128]{2,1,0:T(8,128)(2,1)S(1)}, u32[]{:S(2)}, u32[]{:S(2)}) async-start(bf16[8,96,128]{2,1,0:T(8,128)(2,1)} %broadcast_in_dim.21), calls=%async_computation | async-start | bytes 393216 | tf_op jit(solution)/shard_map/all_to_all | solution.py:251
  14.4 33.5 %all-to-all-start.1 = ((bf16[8,144,128]{2,1,0:T(8,128)(2,1)}), bf16[8,144,128]{2,1,0:T(8,128)(2,1)S(1)}, u32[]{:S(2)}, u32[]{:S(2)}) async-start(bf16[8,144,128]{2,1,0:T(8,128)(2,1)} %broadcast_in_dim.22), calls=%async_computation.1 | async-start | bytes 589824 | tf_op jit(solution)/shard_map/all_to_all | solution.py:251
  28.4 11.0 %collective-permute-start = (bf16[12,4,128]{2,1,0:T(4,128)(2,1)S(1)}, bf16[12,4,128]{2,1,0:T(4,128)(2,1)S(1)}, u32[]{:S(2)}, u32[]{:S(2)}) collective-permute-start(bf16[12,4,128]{2,1,0:T(4,128)(2,1)S(1)} %slice.8), channel_id=1, source_target_pairs={{64,0},{72,8},{80,16},{88,24},{96,32},{104,40},{112,48},{120,56},{... | collective-permute-start | bytes 36872 | tf_op jit(solution)/shard_map/ppermute | solution.py:272
  29.9 26.8 %collective-permute-start.3 = (bf16[768,128]{1,0:T(8,128)(2,1)S(1)}, bf16[768,128]{1,0:T(8,128)(2,1)S(1)}, u32[]{:S(2)}, u32[]{:S(2)}) collective-permute-start(bf16[768,128]{1,0:T(8,128)(2,1)S(1)} %bitcast.14), channel_id=1, source_target_pairs={{0,6},{1,7},{2,0},{3,1},{4,2},{5,3},{6,4},{7,5},{8,14},{9,15},{10,... | collective-permute-start | bytes 589832 | tf_op jit(solution)/shard_map/ppermute | solution.py:285
  34.6 22.2 %collective-permute-start.2 = (bf16[768,128]{1,0:T(8,128)(2,1)S(1)}, bf16[768,128]{1,0:T(8,128)(2,1)S(1)}, u32[]{:S(2)}, u32[]{:S(2)}) collective-permute-start(bf16[768,128]{1,0:T(8,128)(2,1)S(1)} %bitcast.15), channel_id=1, source_target_pairs={{0,4},{1,5},{2,6},{3,7},{4,0},{5,1},{6,2},{7,3},{8,12},{9,13},{10,... | collective-permute-start | bytes 589832 | tf_op jit(solution)/shard_map/ppermute | solution.py:285
  36.8 19.9 %collective-permute-start.1 = (bf16[768,128]{1,0:T(8,128)(2,1)S(1)}, bf16[768,128]{1,0:T(8,128)(2,1)S(1)}, u32[]{:S(2)}, u32[]{:S(2)}) collective-permute-start(bf16[768,128]{1,0:T(8,128)(2,1)S(1)} %bitcast.16), channel_id=1, source_target_pairs={{0,2},{1,3},{2,4},{3,5},{4,6},{5,7},{6,0},{7,1},{8,10},{9,11},{10,... | collective-permute-start | bytes 589832 | tf_op jit(solution)/shard_map/ppermute | solution.py:285
  48.6 16.1 %all-to-all-start.2 = ((bf16[8,192,128]{2,1,0:T(8,128)(2,1)}), bf16[8,192,128]{2,1,0:T(8,128)(2,1)S(1)}, u32[]{:S(2)}, u32[]{:S(2)}) async-start(bf16[8,192,128]{2,1,0:T(8,128)(2,1)} %pad_maximum_fusion.1), calls=%async_computation.2 | async-start | bytes 786432 | tf_op jit(solution)/shard_map/all_to_all | solution.py:275
  56.8 17.2 %collective-permute-start.4 = (bf16[4,768,128]{2,1,0:T(8,128)(2,1)S(1)}, bf16[4,768,128]{2,1,0:T(8,128)(2,1)S(1)}, u32[]{:S(2)}, u32[]{:S(2)}) collective-permute-start(bf16[4,768,128]{2,1,0:T(8,128)(2,1)S(1)} %pad_maximum_fusion.refs_3_), channel_id=1, source_target_pairs={{0,1},{1,0},{2,3},{3,2},{4,5},{5,4},{6,7},{7,6},{8,9},{9,8},{10,11... | collective-permute-start | bytes 2359304 | tf_op jit(solution)/shard_map/ppermute | solution.py:288

commit v11 on v10

--- a/solution.py
+++ b/solution.py
@@ -10,7 +10,8 @@
 L = 512
 LANES = 128
 HALF = 64
-SPAN = L + LANES
+STEP = L + HALF
+WIDTH = 3 * STEP + HALF
 SLOTS = 4
 epsilon = 1e-06
 
@@ -73,12 +74,11 @@
         wide[r * each : (r + 1) * each, :] = templates_ref[r, 0:each, :].astype(jnp.float32)
     for n in range(templates_ref.shape[0]):
         tails[n * ahead : (n + 1) * ahead, :] = templates_ref[n, each:, :].astype(jnp.float32)
+    waves[...] = jnp.zeros_like(waves)
     for c in range(3):
         for v in range(L // LANES):
-            at = c * SPAN + v * LANES
+            at = c * STEP + v * LANES
             waves[0:slots, at : at + LANES] = wide[pl.ds(c * L // LANES + v, slots, parts), :]
-        waves[0:slots, c * SPAN + L : (c + 1) * SPAN] = jnp.zeros((slots, LANES), jnp.float32)
-    waves[slots:, :] = jnp.zeros((spare, 3 * SPAN), jnp.float32)
     squares = jnp.sum(jnp.square(waves[0:slots, :]), axis=1, keepdims=True)
     norms[0:slots, :] = jnp.broadcast_to(lax.rsqrt(squares + epsilon), (slots, LANES))
     norms[slots:, :] = jnp.zeros((spare, LANES), jnp.float32)
@@ -118,29 +118,25 @@
         scales[buffer, 1] = jnp.where(low, other, scale)
         for j in range(SLOTS):
             row = source[order_ref[group] * SLOTS + j] * stations + station
-            for c in range(3):
-                wave = waves[pl.ds(row, 1), c * SPAN : (c + 1) * SPAN]
-                moved = pltpu.roll(
-                    jnp.broadcast_to(wave, (HALF, SPAN)), 0, 1, stride=1, stride_axis=0
+            wave = jnp.broadcast_to(waves[pl.ds(row, 1), :], (HALF, WIDTH))
+            moved = pltpu.roll(wave, 0, 1, stride=1, stride_axis=0)
+            toeplitz[buffer, j * HALF : (j + 1) * HALF, :] = moved.astype(jnp.bfloat16)
+        for e in range(2):
+            tiles = [shifts[0, e, v : v + rows, :] for v in range(tail)]
+            if e:
+                start = shifts[1, 0, 0:rows, :]
+            else:
+                start = pltpu.roll(shifts[1, 0, 0:rows, :], HALF, 1)
+            tiles.append(jnp.where(low, shifts[0, e, tail : tail + rows, :], start))
+            tiles += [shifts[1, 1 - e, v + e : v + e + rows, :] for v in range(tail)]
+            tiles += [shifts[2, e, v : v + rows, :] for v in range(tail + 1)]
+            for n, tile in enumerate(tiles):
+                at = n * LANES
+                windows[buffer, e * rows : (e + 1) * rows, at : at + LANES] = tile.astype(
+                    jnp.bfloat16
                 )
-                toeplitz[buffer, j * HALF : (j + 1) * HALF, c * SPAN : (c + 1) * SPAN] = (
-                    moved.astype(jnp.bfloat16)
-                )
-        for c in range(3):
-            for e in range(2):
-                for v in range(SPAN // LANES):
-                    at = c * SPAN + v * LANES
-                    windows[buffer, e * rows : (e + 1) * rows, at : at + LANES] = shifts[
-                        c, e, v : v + rows, :
-                    ].astype(jnp.bfloat16)
 
     def combine(group, station, buffer):
-        product = lax.dot_general(
-            windows[buffer],
-            toeplitz[buffer],
-            (((1,), (1,)), ((), ())),
-            preferred_element_type=jnp.float32,
-        )
         weight = []
         for j in range(SLOTS):
             row = source[order_ref[group] * SLOTS + j] * stations + station
@@ -148,9 +144,14 @@
         for p in range(SLOTS // 2):
             both = jnp.where(low, weight[2 * p], weight[2 * p + 1])
             at = p * LANES
+            product = lax.dot_general(
+                windows[buffer],
+                toeplitz[buffer, at : at + LANES, :],
+                (((1,), (1,)), ((), ())),
+                preferred_element_type=jnp.float32,
+            )
             for e in range(2):
-                term = product[e * rows : (e + 1) * rows, at : at + LANES]
-                term = term * (scales[buffer, e] * both)
+                term = product[e * rows : (e + 1) * rows, :] * (scales[buffer, e] * both)
                 if station:
                     term = term + share[e, :, at : at + LANES]
                 share[e, :, at : at + LANES] = term
@@ -158,11 +159,11 @@
     def group_term(group, carry):
         later = lax.min(group + 1, n_group - 1)
         for station in range(stations):
+            combine(group, station, station % 2)
             if station < stations - 1:
                 prepare(group, station + 1, (station + 1) % 2)
             else:
                 prepare(later, 0, (station + 1) % 2)
-            combine(group, station, station % 2)
         for j in range(SLOTS):
             at = (j // 2) * LANES
             first = share[0, :, at : at + LANES]
@@ -224,21 +225,21 @@
             pltpu.SMEM((n_all,), jnp.int32),
             pltpu.VMEM((slots * 3 * L // LANES, LANES), jnp.float32),
             pltpu.VMEM((n_all * (templates.shape[1] - each), LANES), jnp.float32),
-            pltpu.VMEM((spare, 3 * SPAN), jnp.float32),
+            pltpu.VMEM((spare, WIDTH), jnp.float32),
             pltpu.VMEM((spare, LANES), jnp.float32),
             pltpu.VMEM((3 * LANES, LANES), jnp.bfloat16),
             pltpu.VMEM((3, 2, padded + 8, LANES), jnp.float32),
             pltpu.VMEM((padded, LANES), jnp.float32),
             pltpu.VMEM((2, 2, rows, LANES), jnp.float32),
-            pltpu.VMEM((2, 2 * rows, 3 * SPAN), jnp.bfloat16),
-            pltpu.VMEM((2, SLOTS * HALF, 3 * SPAN), jnp.bfloat16),
+            pltpu.VMEM((2, 2 * rows, WIDTH), jnp.bfloat16),
+            pltpu.VMEM((2, SLOTS * HALF, WIDTH), jnp.bfloat16),
             pltpu.VMEM((2, rows, SLOTS * HALF), jnp.float32),
             pltpu.VMEM((block + 1, rows, LANES), jnp.float32),
             pltpu.VMEM((rows, block, LANES), jnp.float32),
         ],
         compiler_params=pltpu.CompilerParams(vmem_limit_bytes=32 * 1024 * 1024),
         cost_estimate=pl.CostEstimate(
-            flops=16 * series.shape[0] * stations * 2 * rows * 3 * SPAN * SLOTS * HALF,
+            flops=16 * series.shape[0] * stations * 2 * rows * WIDTH * SLOTS * HALF,
             bytes_accessed=templates.size * 2 + 4 * block * rows * LANES,
             transcendentals=0,
         ),

time: 93.3 us -> 90.8 us (0.973)
  Pallas kernels: 18.6 us -> 16.1 us
    pallas_call x2, Pallas kernels: 18.6 us -> 16.1 us  [detect(): pl.pallas_call(body, out_shape=out_shape, in_specs=[pl.BlockSpec(memory_s...]
  transfers between devices with their start and end apart: 8 -> 8, of which waited for: 3 -> 3; matrix products, arithmetic and copies ran while one was open for 1% -> 1% of each run, Pallas kernels for 10% -> 9%
where the time goes in v11:
time: 90.8 us; the launch traced here: 90.2 us
  starting transfers between devices  41.1 us (45%)
  waiting for transfers between devices  20.1 us (22%)
  Pallas kernels  16.1 us (18%)
  blocking collectives  8.53 us (9%)
  local copies, waits for them, and re-layouts  3.19 us (4%)
    all_to_all x2, starting transfers between devices, copies_to(): lax.all_to_all(spread, axis, 0, 0, axis_index_groups=groups, tiled=True)  20.3 us
    pallas_call x2, Pallas kernels, detect(): pl.pallas_call(body, out_shape=out_shape, in_specs=[pl.BlockSpec(memory_s...  16.1 us
    all_to_all x2, waiting for transfers between devices, copies_to(): lax.all_to_all(spread, axis, 0, 0, axis_index_groups=groups, tiled=True)  14.2 us
    ppermute x3, starting transfers between devices, on_device(): pieces.append(lax.ppermute(mine, 'sta', pairs))  9.5 us
    all_to_all x1, blocking collectives, on_device(): lax.all_to_all(total, 'tm', 0, 0, axis_index_groups=near, tiled=True)  8.53 us
    all_to_all x1, starting transfers between devices, on_device(): lax.all_to_all(jnp.concatenate([block, tail], axis=1), 'sta', 0, 0, tiled...  8.05 us
    all_to_all x1, waiting for transfers between devices, on_device(): lax.all_to_all(jnp.concatenate([block, tail], axis=1), 'sta', 0, 0, tiled...  5.98 us
    broadcast_in_dim x3, local copies, waits for them, and re-layouts, copies_to(): spread = jnp.broadcast_to(value[None], (count,) + value.shape)  2.23 us
  transfers between devices with their start and end apart: 8, of which 3 were waited for; matrix products, arithmetic and copies ran while one was open for 1% of the time, Pallas kernels for 9%

profile of v11, /device:TPU:1, one launch (start us, length us, event | category | flops | bytes accessed | tf_op | source)
XLA Modules:
  0.0 90.2 jit_solution(10594482884287112011)
XLA Ops:
  0.0 0.0 copy-start
  0.0 0.8 broadcast_in_dim.20
  0.8 0.7 broadcast_in_dim.21
  1.5 0.0 copy-start.1
  1.5 6.3 %all-to-all-start = ((bf16[8,96,128]{2,1,0:T(8,128)(2,1)}), bf16[8,96,128]{2,1,0:T(8,128)(2,1)S(1)}, u32[]{:S(2)}, u32[]{:S(2)}) async-start(bf16[8,96,128]{2,1,0:T(8,128)(2,1)} %broadcast_in_dim.21), calls=%async_computation | async-start | bytes 393216 | tf_op jit(solution)/shard_map/all_to_all | solution.py:252
  7.8 0.0 copy-done.1
  7.8 5.8 %all-to-all-done = bf16[8,96,128]{2,1,0:T(8,128)(2,1)S(1)} async-done(((bf16[8,96,128]{2,1,0:T(8,128)(2,1)}), bf16[8,96,128]{2,1,0:T(8,128)(2,1)S(1)}, u32[]{:S(2)}, u32[]{:S(2)}) %all-to-all-start) | async-done | bytes 196640 | tf_op jit(solution)/shard_map/all_to_all | solution.py:252
  13.6 0.8 broadcast_in_dim.22
  14.4 14.0 %all-to-all-start.1 = ((bf16[8,144,128]{2,1,0:T(8,128)(2,1)}), bf16[8,144,128]{2,1,0:T(8,128)(2,1)S(1)}, u32[]{:S(2)}, u32[]{:S(2)}) async-start(bf16[8,144,128]{2,1,0:T(8,128)(2,1)} %broadcast_in_dim.22), calls=%async_computation.1 | async-start | bytes 589824 | tf_op jit(solution)/shard_map/all_to_all | solution.py:252
  28.4 1.3 %collective-permute-start = (bf16[12,4,128]{2,1,0:T(4,128)(2,1)S(1)}, bf16[12,4,128]{2,1,0:T(4,128)(2,1)S(1)}, u32[]{:S(2)}, u32[]{:S(2)}) collective-permute-start(bf16[12,4,128]{2,1,0:T(4,128)(2,1)S(1)} %slice.8), channel_id=1, source_target_pairs={{64,0},{72,8},{80,16},{88,24},{96,32},{104,40},{112,48},{120,56},{... | collective-permute-start | bytes 36872 | tf_op jit(solution)/shard_map/ppermute | solution.py:273
  29.7 0.0 copy-done
  29.7 0.1 constant_dynamic-slice_fusion
  29.8 0.1 copy.8.refs_1_
  29.9 4.6 %collective-permute-start.3 = (bf16[768,128]{1,0:T(8,128)(2,1)S(1)}, bf16[768,128]{1,0:T(8,128)(2,1)S(1)}, u32[]{:S(2)}, u32[]{:S(2)}) collective-permute-start(bf16[768,128]{1,0:T(8,128)(2,1)S(1)} %bitcast.14), channel_id=1, source_target_pairs={{0,6},{1,7},{2,0},{3,1},{4,2},{5,3},{6,4},{7,5},{8,14},{9,15},{10,... | collective-permute-start | bytes 589832 | tf_op jit(solution)/shard_map/ppermute | solution.py:286
  34.6 2.3 %collective-permute-start.2 = (bf16[768,128]{1,0:T(8,128)(2,1)S(1)}, bf16[768,128]{1,0:T(8,128)(2,1)S(1)}, u32[]{:S(2)}, u32[]{:S(2)}) collective-permute-start(bf16[768,128]{1,0:T(8,128)(2,1)S(1)} %bitcast.15), channel_id=1, source_target_pairs={{0,4},{1,5},{2,6},{3,7},{4,0},{5,1},{6,2},{7,3},{8,12},{9,13},{10,... | collective-permute-start | bytes 589832 | tf_op jit(solution)/shard_map/ppermute | solution.py:286
  36.8 2.6 %collective-permute-start.1 = (bf16[768,128]{1,0:T(8,128)(2,1)S(1)}, bf16[768,128]{1,0:T(8,128)(2,1)S(1)}, u32[]{:S(2)}, u32[]{:S(2)}) collective-permute-start(bf16[768,128]{1,0:T(8,128)(2,1)S(1)} %bitcast.16), channel_id=1, source_target_pairs={{0,2},{1,3},{2,4},{3,5},{4,6},{5,7},{6,0},{7,1},{8,10},{9,11},{10,... | collective-permute-start | bytes 589832 | tf_op jit(solution)/shard_map/ppermute | solution.py:286
  39.4 0.0 collective-permute-done
  39.4 8.4 %all-to-all-done.1 = bf16[8,144,128]{2,1,0:T(8,128)(2,1)S(1)} async-done(((bf16[8,144,128]{2,1,0:T(8,128)(2,1)}), bf16[8,144,128]{2,1,0:T(8,128)(2,1)S(1)}, u32[]{:S(2)}, u32[]{:S(2)}) %all-to-all-start.1) | async-done | bytes 294944 | tf_op jit(solution)/shard_map/all_to_all | solution.py:252
  47.9 0.8 pad_maximum_fusion.1
  48.6 8.0 %all-to-all-start.2 = ((bf16[8,192,128]{2,1,0:T(8,128)(2,1)}), bf16[8,192,128]{2,1,0:T(8,128)(2,1)S(1)}, u32[]{:S(2)}, u32[]{:S(2)}) async-start(bf16[8,192,128]{2,1,0:T(8,128)(2,1)} %pad_maximum_fusion.1), calls=%async_computation.2 | async-start | bytes 786432 | tf_op jit(solution)/shard_map/all_to_all | solution.py:276
  56.7 0.0 collective-permute-done.3
  56.7 0.0 collective-permute-done.2
  56.7 0.0 collective-permute-done.1
  56.7 0.1 pad_maximum_fusion.refs_3_
  56.8 1.9 %collective-permute-start.4 = (bf16[4,768,128]{2,1,0:T(8,128)(2,1)S(1)}, bf16[4,768,128]{2,1,0:T(8,128)(2,1)S(1)}, u32[]{:S(2)}, u32[]{:S(2)}) collective-permute-start(bf16[4,768,128]{2,1,0:T(8,128)(2,1)S(1)} %pad_maximum_fusion.refs_3_), channel_id=1, source_target_pairs={{0,1},{1,0},{2,3},{3,2},{4,5},{5,4},{6,7},{7,6},{8,9},{9,8},{10,11... | collective-permute-start | bytes 2359304 | tf_op jit(solution)/shard_map/ppermute | solution.py:289
  58.8 6.0 %all-to-all-done.2.refs_2_ = bf16[8,192,128]{2,1,0:T(8,128)(2,1)S(1)} async-done(((bf16[8,192,128]{2,1,0:T(8,128)(2,1)}), bf16[8,192,128]{2,1,0:T(8,128)(2,1)S(1)}, u32[]{:S(2)}, u32[]{:S(2)}) %all-to-all-start.2) | async-done | bytes 393248 | tf_op jit(solution)/shard_map/all_to_all | solution.py:276
  64.8 8.0 %shard_map.37.refs_4_ = f32[9,64,128]{2,1,0:T(8,128)S(1)} custom-call(s32[4]{0:T(128)S(1)} %broadcast_add_fusion.refs_0_, s32[8,3]{1,0:T(8,128)S(1)} %copy.8.refs_1_, bf16[8,192,128]{2,1,0:T(8,128)(2,1)S(1)} %all-to-all-done.2.refs_2_, bf16[4,768,128]{2,1,0:T(8,128)(2,1)S(1)} %pad_maximum_fusion.refs_3_), custom_call_target="tpu_custom_call" | custom-call | flops 15032385536 | bytes 655360 | tf_op jit(solution)/shard_map/pallas_call | solution.py:217
  72.8 0.0 collective-permute-done.4.refs_3_
  72.8 8.1 %shard_map.38 = f32[8,8,1024]{2,1,0:T(8,128)S(1)} custom-call(s32[4]{0:T(128)S(1)} %add_subtract_fusion.refs_0_, s32[8,3]{1,0:T(8,128)S(1)} %copy.8.refs_1_, bf16[8,192,128]{2,1,0:T(8,128)(2,1)S(1)} %all-to-all-done.2.refs_2_, bf16[4,768,128]{2,1,0:T(8,128)(2,1)S(1)} %collective-permute-done.4.refs_3_, f32[9,64,128]{2,1,0:T(8,128)S(1)} %shard_map.37.refs_4_), custom_call_target="tpu_custom_call" | custom-call | flops 15032385536 | bytes 655360 | tf_op jit(solution)/shard_map/pallas_call | solution.py:217
  80.9 8.5 %all_to_all.20 = f32[8,8,1024]{2,1,0:T(8,128)S(1)} all-to-all(f32[8,8,1024]{2,1,0:T(8,128)S(1)} %shard_map.38), channel_id=1, replica_groups={{0,8,16,24,32,40,48,56},{64,72,80,88,96,104,112,120},{128,136,144,152,1..., dimensions={0} | all-to-all | bytes 524288 | tf_op jit(solution)/shard_map/all_to_all | solution.py:296
  89.4 0.7 copy.10
  (7 shorter events, 0.1 us)
Async XLA Ops:
  0.0 29.7 %copy-start = (s32[512,3]{0,1:T(4,128)S(1)}, s32[512,3]{0,1:T(4,128)}, u32[]{:S(2)}) copy-start(s32[512,3]{0,1:T(4,128)} %param.5) | copy-start | bytes 18436
  1.5 6.3 %copy-start.1 = (bf16[1,3,4,1536]{3,2,1,0:T(4,128)(2,1)S(1)}, bf16[1,3,4,1536]{3,2,1,0:T(4,128)(2,1)}, u32[]{:S(2)}) copy-start(bf16[1,3,4,1536]{3,2,1,0:T(4,128)(2,1)} %param.4) | copy-start | bytes 110596
  1.5 12.1 %all-to-all-start = ((bf16[8,96,128]{2,1,0:T(8,128)(2,1)}), bf16[8,96,128]{2,1,0:T(8,128)(2,1)S(1)}, u32[]{:S(2)}, u32[]{:S(2)}) async-start(bf16[8,96,128]{2,1,0:T(8,128)(2,1)} %broadcast_in_dim.21), calls=%async_computation | async-start | bytes 393216 | tf_op jit(solution)/shard_map/all_to_all | solution.py:252
  14.4 33.5 %all-to-all-start.1 = ((bf16[8,144,128]{2,1,0:T(8,128)(2,1)}), bf16[8,144,128]{2,1,0:T(8,128)(2,1)S(1)}, u32[]{:S(2)}, u32[]{:S(2)}) async-start(bf16[8,144,128]{2,1,0:T(8,128)(2,1)} %broadcast_in_dim.22), calls=%async_computation.1 | async-start | bytes 589824 | tf_op jit(solution)/shard_map/all_to_all | solution.py:252
  28.4 11.0 %collective-permute-start = (bf16[12,4,128]{2,1,0:T(4,128)(2,1)S(1)}, bf16[12,4,128]{2,1,0:T(4,128)(2,1)S(1)}, u32[]{:S(2)}, u32[]{:S(2)}) collective-permute-start(bf16[12,4,128]{2,1,0:T(4,128)(2,1)S(1)} %slice.8), channel_id=1, source_target_pairs={{64,0},{72,8},{80,16},{88,24},{96,32},{104,40},{112,48},{120,56},{... | collective-permute-start | bytes 36872 | tf_op jit(solution)/shard_map/ppermute | solution.py:273
  29.9 26.8 %collective-permute-start.3 = (bf16[768,128]{1,0:T(8,128)(2,1)S(1)}, bf16[768,128]{1,0:T(8,128)(2,1)S(1)}, u32[]{:S(2)}, u32[]{:S(2)}) collective-permute-start(bf16[768,128]{1,0:T(8,128)(2,1)S(1)} %bitcast.14), channel_id=1, source_target_pairs={{0,6},{1,7},{2,0},{3,1},{4,2},{5,3},{6,4},{7,5},{8,14},{9,15},{10,... | collective-permute-start | bytes 589832 | tf_op jit(solution)/shard_map/ppermute | solution.py:286
  34.6 22.2 %collective-permute-start.2 = (bf16[768,128]{1,0:T(8,128)(2,1)S(1)}, bf16[768,128]{1,0:T(8,128)(2,1)S(1)}, u32[]{:S(2)}, u32[]{:S(2)}) collective-permute-start(bf16[768,128]{1,0:T(8,128)(2,1)S(1)} %bitcast.15), channel_id=1, source_target_pairs={{0,4},{1,5},{2,6},{3,7},{4,0},{5,1},{6,2},{7,3},{8,12},{9,13},{10,... | collective-permute-start | bytes 589832 | tf_op jit(solution)/shard_map/ppermute | solution.py:286
  36.8 19.9 %collective-permute-start.1 = (bf16[768,128]{1,0:T(8,128)(2,1)S(1)}, bf16[768,128]{1,0:T(8,128)(2,1)S(1)}, u32[]{:S(2)}, u32[]{:S(2)}) collective-permute-start(bf16[768,128]{1,0:T(8,128)(2,1)S(1)} %bitcast.16), channel_id=1, source_target_pairs={{0,2},{1,3},{2,4},{3,5},{4,6},{5,7},{6,0},{7,1},{8,10},{9,11},{10,... | collective-permute-start | bytes 589832 | tf_op jit(solution)/shard_map/ppermute | solution.py:286
  48.6 16.1 %all-to-all-start.2 = ((bf16[8,192,128]{2,1,0:T(8,128)(2,1)}), bf16[8,192,128]{2,1,0:T(8,128)(2,1)S(1)}, u32[]{:S(2)}, u32[]{:S(2)}) async-start(bf16[8,192,128]{2,1,0:T(8,128)(2,1)} %pad_maximum_fusion.1), calls=%async_computation.2 | async-start | bytes 786432 | tf_op jit(solution)/shard_map/all_to_all | solution.py:276
  56.8 15.9 %collective-permute-start.4 = (bf16[4,768,128]{2,1,0:T(8,128)(2,1)S(1)}, bf16[4,768,128]{2,1,0:T(8,128)(2,1)S(1)}, u32[]{:S(2)}, u32[]{:S(2)}) collective-permute-start(bf16[4,768,128]{2,1,0:T(8,128)(2,1)S(1)} %pad_maximum_fusion.refs_3_), channel_id=1, source_target_pairs={{0,1},{1,0},{2,3},{3,2},{4,5},{5,4},{6,7},{7,6},{8,9},{9,8},{10,11... | collective-permute-start | bytes 2359304 | tf_op jit(solution)/shard_map/ppermute | solution.py:289

commit v12 on v11

--- a/solution.py
+++ b/solution.py
@@ -267,8 +267,13 @@
 
     lines = channels * stations
     steps = samples // LANES
-    around = copies_to(record.reshape(lines * steps, LANES), "tm", near)
-    around, own = lax.optimization_barrier((around, templates.reshape(-1, LANES)))
+    half = n_b // 2
+    four = [[i + j for j in range(half)] for i in range(0, n_tm, half)]
+    same = lax.all_gather(record.reshape(lines * steps, LANES), "tm", axis_index_groups=four)
+    other = lax.ppermute(same, "tm", [(i, i ^ half) for i in range(n_tm)])
+    upper = lax.rem(m // half, 2) == 1
+    around = jnp.concatenate([jnp.where(upper, other, same), jnp.where(upper, same, other)])
+    own = templates.reshape(-1, LANES)
     front = around[0].reshape(lines, steps, LANES)[:, : L // LANES]
     tail = lax.ppermute(front, "tm", [(i + n_b, i) for i in range(n_tm - n_b)])
     tail = jnp.broadcast_to(tail.reshape(1, -1, LANES), (n_sta, lines * L // LANES, LANES))

time: 90.8 us -> 89.7 us (0.988); the launches traced: 90.2 us -> 88.1 us
  waiting for transfers between devices: 20.1 us -> 8.11 us
  blocking collectives: 8.53 us -> 19.7 us
    all_to_all x2 -> x1, waiting for transfers between devices: 14.2 us -> 0.01 us  [copies_to(): lax.all_to_all(spread, axis, 0, 0, axis_index_groups=groups, tiled=True)]
    all_gather x0 -> x1, blocking collectives: none -> 9.82 us  [on_device(): lax.all_gather(record.reshape(lines * steps, LANES), 'tm', axis_index_gro...]
    all_to_all x2 -> x1, starting transfers between devices: 20.3 us -> 15.8 us  [copies_to(): lax.all_to_all(spread, axis, 0, 0, axis_index_groups=groups, tiled=True)]
    ppermute x0 -> x1, waiting for transfers between devices: none -> 4.17 us  [on_device(): other = lax.ppermute(same, 'tm', [(i, i ^ half) for i in range(n_tm)])]
    ppermute x0 -> x1, starting transfers between devices: none -> 2.79 us  [on_device(): other = lax.ppermute(same, 'tm', [(i, i ^ half) for i in range(n_tm)])]
    all_to_all x1, waiting for transfers between devices: 5.98 us -> 3.93 us  [on_device(): lax.all_to_all(jnp.concatenate([block, tail], axis=1), 'sta', 0, 0, tiled...]
    ppermute x1, starting transfers between devices: 1.92 us -> 3.97 us  [on_device(): others = lax.ppermute(pieces, 'sta', swap)]
    all_to_all x1, blocking collectives: 8.53 us -> 9.92 us  [on_device(): lax.all_to_all(total, 'tm', 0, 0, axis_index_groups=near, tiled=True)]
  transfers between devices with their start and end apart: 8 -> 8, of which waited for: 3 -> 2; matrix products, arithmetic and copies ran while one was open for 1% -> 1% of each run, Pallas kernels for 9% -> 9%
where the time goes in v12:
time: 89.7 us; the launch traced here: 88.1 us
  starting transfers between devices  40.4 us (45%)
  blocking collectives  19.7 us (22%)
  Pallas kernels  16.1 us (18%)
  waiting for transfers between devices  8.11 us (9%)
  local copies, waits for them, and re-layouts  2.52 us (3%)
  other arithmetic  0.93 us (1%)
    pallas_call x2, Pallas kernels, detect(): pl.pallas_call(body, out_shape=out_shape, in_specs=[pl.BlockSpec(memory_s...  16.1 us
    all_to_all x1, starting transfers between devices, copies_to(): lax.all_to_all(spread, axis, 0, 0, axis_index_groups=groups, tiled=True)  15.8 us
    all_to_all x1, blocking collectives, on_device(): lax.all_to_all(total, 'tm', 0, 0, axis_index_groups=near, tiled=True)  9.92 us
    all_gather x1, blocking collectives, on_device(): lax.all_gather(record.reshape(lines * steps, LANES), 'tm', axis_index_gro...  9.82 us
    ppermute x3, starting transfers between devices, on_device(): pieces.append(lax.ppermute(mine, 'sta', pairs))  9.5 us
    all_to_all x1, starting transfers between devices, on_device(): lax.all_to_all(jnp.concatenate([block, tail], axis=1), 'sta', 0, 0, tiled...  7.12 us
    ppermute x1, waiting for transfers between devices, on_device(): other = lax.ppermute(same, 'tm', [(i, i ^ half) for i in range(n_tm)])  4.17 us
    ppermute x1, starting transfers between devices, on_device(): others = lax.ppermute(pieces, 'sta', swap)  3.97 us
  transfers between devices with their start and end apart: 8, of which 2 were waited for; matrix products, arithmetic and copies ran while one was open for 1% of the time, Pallas kernels for 9%

profile of v12, /device:TPU:1, one launch (start us, length us, event | category | flops | bytes accessed | tf_op | source)
XLA Modules:
  0.0 88.1 jit_solution(2627291752767946966)
XLA Ops:
  0.0 0.0 copy-start
  0.0 0.8 broadcast_in_dim.14
  0.8 0.8 broadcast_in_dim.15
  1.6 0.0 copy-start.1
  1.6 15.8 %all-to-all-start = ((bf16[8,144,128]{2,1,0:T(8,128)(2,1)}), bf16[8,144,128]{2,1,0:T(8,128)(2,1)S(1)}, u32[]{:S(2)}, u32[]{:S(2)}) async-start(bf16[8,144,128]{2,1,0:T(8,128)(2,1)} %broadcast_in_dim.15), calls=%async_computation | async-start | bytes 589824 | tf_op jit(solution)/shard_map/all_to_all | solution.py:252
  17.3 0.0 copy-done.1
  17.4 9.8 %all_gather.3 = bf16[4,96,128]{2,1,0:T(8,128)(2,1)S(1)} all-gather(bf16[1,96,128]{2,1,0:T(8,128)(2,1)S(1)} %all_gather_reshape.3), channel_id=1, replica_groups={{0,8,16,24},{32,40,48,56},{64,72,80,88},{96,104,112,120},{128,136,144,1..., dimensions={0}, use_global_device_ids=true | all-gather | bytes 122880 | tf_op jit(solution)/shard_map/all_gather | solution.py:272
  27.2 2.8 %collective-permute-start = (bf16[4,96,128]{2,1,0:T(8,128)(2,1)S(1)}, bf16[4,96,128]{2,1,0:T(8,128)(2,1)S(1)}, u32[]{:S(2)}, u32[]{:S(2)}) collective-permute-start(bf16[4,96,128]{2,1,0:T(8,128)(2,1)S(1)} %all_gather.3), channel_id=1, source_target_pairs={{0,32},{8,40},{16,48},{24,56},{32,0},{40,8},{48,16},{56,24},{64,96... | collective-permute-start | bytes 294920 | tf_op jit(solution)/shard_map/ppermute | solution.py:273
  30.0 0.0 copy-done
  30.0 0.1 constant_dynamic-slice_fusion
  30.1 0.1 copy.11.refs_1_
  30.2 4.2 %collective-permute-done = bf16[4,96,128]{2,1,0:T(8,128)(2,1)S(1)} collective-permute-done((bf16[4,96,128]{2,1,0:T(8,128)(2,1)S(1)}, bf16[4,96,128]{2,1,0:T(8,128)(2,1)S(1)}, u32[]{:S(2)}, u32[]{:S(2)}) %collective-permute-start) | collective-permute-done | bytes 98336 | tf_op jit(solution)/shard_map/ppermute | solution.py:273
  34.4 1.3 %collective-permute-start.1 = (bf16[12,4,128]{2,1,0:T(4,128)(2,1)S(1)}, bf16[12,4,128]{2,1,0:T(4,128)(2,1)S(1)}, u32[]{:S(2)}, u32[]{:S(2)}) collective-permute-start(bf16[12,4,128]{2,1,0:T(4,128)(2,1)S(1)} %slice.9), channel_id=1, source_target_pairs={{64,0},{72,8},{80,16},{88,24},{96,32},{104,40},{112,48},{120,56},{... | collective-permute-start | bytes 36872 | tf_op jit(solution)/shard_map/ppermute | solution.py:278
  35.8 4.6 %collective-permute-start.4 = (bf16[768,128]{1,0:T(8,128)(2,1)S(1)}, bf16[768,128]{1,0:T(8,128)(2,1)S(1)}, u32[]{:S(2)}, u32[]{:S(2)}) collective-permute-start(bf16[768,128]{1,0:T(8,128)(2,1)S(1)} %bitcast.14), channel_id=1, source_target_pairs={{0,6},{1,7},{2,0},{3,1},{4,2},{5,3},{6,4},{7,5},{8,14},{9,15},{10,... | collective-permute-start | bytes 589832 | tf_op jit(solution)/shard_map/ppermute | solution.py:291
  40.4 2.3 %collective-permute-start.3 = (bf16[768,128]{1,0:T(8,128)(2,1)S(1)}, bf16[768,128]{1,0:T(8,128)(2,1)S(1)}, u32[]{:S(2)}, u32[]{:S(2)}) collective-permute-start(bf16[768,128]{1,0:T(8,128)(2,1)S(1)} %bitcast.15), channel_id=1, source_target_pairs={{0,4},{1,5},{2,6},{3,7},{4,0},{5,1},{6,2},{7,3},{8,12},{9,13},{10,... | collective-permute-start | bytes 589832 | tf_op jit(solution)/shard_map/ppermute | solution.py:291
  42.7 2.6 %collective-permute-start.2 = (bf16[768,128]{1,0:T(8,128)(2,1)S(1)}, bf16[768,128]{1,0:T(8,128)(2,1)S(1)}, u32[]{:S(2)}, u32[]{:S(2)}) collective-permute-start(bf16[768,128]{1,0:T(8,128)(2,1)S(1)} %bitcast.16), channel_id=1, source_target_pairs={{0,2},{1,3},{2,4},{3,5},{4,6},{5,7},{6,0},{7,1},{8,10},{9,11},{10,... | collective-permute-start | bytes 589832 | tf_op jit(solution)/shard_map/ppermute | solution.py:291
  45.3 0.0 collective-permute-done.1
  45.3 0.0 all-to-all-done
  45.4 0.8 pad_maximum_fusion.1
  46.1 7.1 %all-to-all-start.1 = ((bf16[8,192,128]{2,1,0:T(8,128)(2,1)}), bf16[8,192,128]{2,1,0:T(8,128)(2,1)S(1)}, u32[]{:S(2)}, u32[]{:S(2)}) async-start(bf16[8,192,128]{2,1,0:T(8,128)(2,1)} %pad_maximum_fusion.1), calls=%async_computation.1 | async-start | bytes 786432 | tf_op jit(solution)/shard_map/all_to_all | solution.py:281
  53.3 0.0 collective-permute-done.4
  53.3 0.0 collective-permute-done.3
  53.3 0.0 collective-permute-done.2
  53.3 0.1 pad_maximum_fusion.refs_3_
  53.4 4.0 %collective-permute-start.5 = (bf16[4,768,128]{2,1,0:T(8,128)(2,1)S(1)}, bf16[4,768,128]{2,1,0:T(8,128)(2,1)S(1)}, u32[]{:S(2)}, u32[]{:S(2)}) collective-permute-start(bf16[4,768,128]{2,1,0:T(8,128)(2,1)S(1)} %pad_maximum_fusion.refs_3_), channel_id=1, source_target_pairs={{0,1},{1,0},{2,3},{3,2},{4,5},{5,4},{6,7},{7,6},{8,9},{9,8},{10,11... | collective-permute-start | bytes 2359304 | tf_op jit(solution)/shard_map/ppermute | solution.py:294
  57.4 3.9 %all-to-all-done.1.refs_2_ = bf16[8,192,128]{2,1,0:T(8,128)(2,1)S(1)} async-done(((bf16[8,192,128]{2,1,0:T(8,128)(2,1)}), bf16[8,192,128]{2,1,0:T(8,128)(2,1)S(1)}, u32[]{:S(2)}, u32[]{:S(2)}) %all-to-all-start.1) | async-done | bytes 393248 | tf_op jit(solution)/shard_map/all_to_all | solution.py:281
  61.3 8.0 %shard_map.37.refs_4_ = f32[9,64,128]{2,1,0:T(8,128)S(1)} custom-call(s32[4]{0:T(128)S(1)} %broadcast_add_fusion.refs_0_, s32[8,3]{1,0:T(8,128)S(1)} %copy.11.refs_1_, bf16[8,192,128]{2,1,0:T(8,128)(2,1)S(1)} %all-to-all-done.1.refs_2_, bf16[4,768,128]{2,1,0:T(8,128)(2,1)S(1)} %pad_maximum_fusion.refs_3_), custom_call_target="tpu_custom_call" | custom-call | flops 15032385536 | bytes 655360 | tf_op jit(solution)/shard_map/pallas_call | solution.py:217
  69.3 0.0 collective-permute-done.5.refs_3_
  69.3 8.1 %shard_map.38 = f32[8,8,1024]{2,1,0:T(8,128)S(1)} custom-call(s32[4]{0:T(128)S(1)} %add_subtract_fusion.refs_0_, s32[8,3]{1,0:T(8,128)S(1)} %copy.11.refs_1_, bf16[8,192,128]{2,1,0:T(8,128)(2,1)S(1)} %all-to-all-done.1.refs_2_, bf16[4,768,128]{2,1,0:T(8,128)(2,1)S(1)} %collective-permute-done.5.refs_3_, f32[9,64,128]{2,1,0:T(8,128)S(1)} %shard_map.37.refs_4_), custom_call_target="tpu_custom_call" | custom-call | flops 15032385536 | bytes 655360 | tf_op jit(solution)/shard_map/pallas_call | solution.py:217
  77.5 9.9 %all_to_all.15 = f32[8,8,1024]{2,1,0:T(8,128)S(1)} all-to-all(f32[8,8,1024]{2,1,0:T(8,128)S(1)} %shard_map.38), channel_id=1, replica_groups={{0,8,16,24,32,40,48,56},{64,72,80,88,96,104,112,120},{128,136,144,152,1..., dimensions={0} | all-to-all | bytes 524288 | tf_op jit(solution)/shard_map/all_to_all | solution.py:301
  87.4 0.7 copy.13
  (9 shorter events, 0.1 us)
Async XLA Ops:
  0.0 30.0 %copy-start = (s32[512,3]{0,1:T(4,128)S(1)}, s32[512,3]{0,1:T(4,128)}, u32[]{:S(2)}) copy-start(s32[512,3]{0,1:T(4,128)} %param.5) | copy-start | bytes 18436
  1.6 15.8 %copy-start.1 = (bf16[3,4,1024]{2,1,0:T(4,128)(2,1)S(1)}, bf16[3,4,1024]{2,1,0:T(4,128)(2,1)}, u32[]{:S(2)}) copy-start(bf16[3,4,1024]{2,1,0:T(4,128)(2,1)} %param.3) | copy-start | bytes 73732
  1.6 43.8 %all-to-all-start = ((bf16[8,144,128]{2,1,0:T(8,128)(2,1)}), bf16[8,144,128]{2,1,0:T(8,128)(2,1)S(1)}, u32[]{:S(2)}, u32[]{:S(2)}) async-start(bf16[8,144,128]{2,1,0:T(8,128)(2,1)} %broadcast_in_dim.15), calls=%async_computation | async-start | bytes 589824 | tf_op jit(solution)/shard_map/all_to_all | solution.py:252
  27.2 7.2 %collective-permute-start = (bf16[4,96,128]{2,1,0:T(8,128)(2,1)S(1)}, bf16[4,96,128]{2,1,0:T(8,128)(2,1)S(1)}, u32[]{:S(2)}, u32[]{:S(2)}) collective-permute-start(bf16[4,96,128]{2,1,0:T(8,128)(2,1)S(1)} %all_gather.3), channel_id=1, source_target_pairs={{0,32},{8,40},{16,48},{24,56},{32,0},{40,8},{48,16},{56,24},{64,96... | collective-permute-start | bytes 294920 | tf_op jit(solution)/shard_map/ppermute | solution.py:273
  34.4 10.9 %collective-permute-start.1 = (bf16[12,4,128]{2,1,0:T(4,128)(2,1)S(1)}, bf16[12,4,128]{2,1,0:T(4,128)(2,1)S(1)}, u32[]{:S(2)}, u32[]{:S(2)}) collective-permute-start(bf16[12,4,128]{2,1,0:T(4,128)(2,1)S(1)} %slice.9), channel_id=1, source_target_pairs={{64,0},{72,8},{80,16},{88,24},{96,32},{104,40},{112,48},{120,56},{... | collective-permute-start | bytes 36872 | tf_op jit(solution)/shard_map/ppermute | solution.py:278
  35.8 17.5 %collective-permute-start.4 = (bf16[768,128]{1,0:T(8,128)(2,1)S(1)}, bf16[768,128]{1,0:T(8,128)(2,1)S(1)}, u32[]{:S(2)}, u32[]{:S(2)}) collective-permute-start(bf16[768,128]{1,0:T(8,128)(2,1)S(1)} %bitcast.14), channel_id=1, source_target_pairs={{0,6},{1,7},{2,0},{3,1},{4,2},{5,3},{6,4},{7,5},{8,14},{9,15},{10,... | collective-permute-start | bytes 589832 | tf_op jit(solution)/shard_map/ppermute | solution.py:291
  40.4 12.8 %collective-permute-start.3 = (bf16[768,128]{1,0:T(8,128)(2,1)S(1)}, bf16[768,128]{1,0:T(8,128)(2,1)S(1)}, u32[]{:S(2)}, u32[]{:S(2)}) collective-permute-start(bf16[768,128]{1,0:T(8,128)(2,1)S(1)} %bitcast.15), channel_id=1, source_target_pairs={{0,4},{1,5},{2,6},{3,7},{4,0},{5,1},{6,2},{7,3},{8,12},{9,13},{10,... | collective-permute-start | bytes 589832 | tf_op jit(solution)/shard_map/ppermute | solution.py:291
  42.7 10.6 %collective-permute-start.2 = (bf16[768,128]{1,0:T(8,128)(2,1)S(1)}, bf16[768,128]{1,0:T(8,128)(2,1)S(1)}, u32[]{:S(2)}, u32[]{:S(2)}) collective-permute-start(bf16[768,128]{1,0:T(8,128)(2,1)S(1)} %bitcast.16), channel_id=1, source_target_pairs={{0,2},{1,3},{2,4},{3,5},{4,6},{5,7},{6,0},{7,1},{8,10},{9,11},{10,... | collective-permute-start | bytes 589832 | tf_op jit(solution)/shard_map/ppermute | solution.py:291
  46.1 15.2 %all-to-all-start.1 = ((bf16[8,192,128]{2,1,0:T(8,128)(2,1)}), bf16[8,192,128]{2,1,0:T(8,128)(2,1)S(1)}, u32[]{:S(2)}, u32[]{:S(2)}) async-start(bf16[8,192,128]{2,1,0:T(8,128)(2,1)} %pad_maximum_fusion.1), calls=%async_computation.1 | async-start | bytes 786432 | tf_op jit(solution)/shard_map/all_to_all | solution.py:281
  53.4 15.9 %collective-permute-start.5 = (bf16[4,768,128]{2,1,0:T(8,128)(2,1)S(1)}, bf16[4,768,128]{2,1,0:T(8,128)(2,1)S(1)}, u32[]{:S(2)}, u32[]{:S(2)}) collective-permute-start(bf16[4,768,128]{2,1,0:T(8,128)(2,1)S(1)} %pad_maximum_fusion.refs_3_), channel_id=1, source_target_pairs={{0,1},{1,0},{2,3},{3,2},{4,5},{5,4},{6,7},{7,6},{8,9},{9,8},{10,11... | collective-permute-start | bytes 2359304 | tf_op jit(solution)/shard_map/ppermute | solution.py:294

commit v13 on v12

--- a/solution.py
+++ b/solution.py
@@ -17,7 +17,6 @@
 
 
 def detect_kernel(
-    each,
     factor,
     order_ref,
     groups_ref,
@@ -46,7 +45,7 @@
     n_group = series_ref.shape[0]
     rows = total.shape[1]
     padded = rows + 8
-    ahead = tails.shape[0] // templates_ref.shape[0]
+    ahead = tails.shape[0] // n_group
     tail = L // LANES
     parts = 3 * L // LANES
     slots = wide.shape[0] // parts
@@ -70,10 +69,11 @@
             home[slot] = r
             count[named] = count[named] + 1
     spare = waves.shape[0] - slots
+    each = slots // block * parts
     for r in range(block):
-        wide[r * each : (r + 1) * each, :] = templates_ref[r, 0:each, :].astype(jnp.float32)
-    for n in range(templates_ref.shape[0]):
-        tails[n * ahead : (n + 1) * ahead, :] = templates_ref[n, each:, :].astype(jnp.float32)
+        wide[r * each : (r + 1) * each, :] = templates_ref[r].astype(jnp.float32)
+    for n in range(n_group):
+        tails[n * ahead : (n + 1) * ahead, :] = series_ref[n, -ahead:, :].astype(jnp.float32)
     waves[...] = jnp.zeros_like(waves)
     for c in range(3):
         for v in range(L // LANES):
@@ -99,7 +99,7 @@
             line = c * stations + station
             main = series_ref[group, line * rows : (line + 1) * rows, :]
             shifts[c, 0, 0:rows, :] = main.astype(jnp.float32)
-            at = order_ref[group] * ahead + line * tail
+            at = group * ahead + line * tail
             shifts[c, 0, rows : rows + tail, :] = tails[pl.ds(at, tail), :]
             plain = shifts[c, 0, 0:padded, :]
             squares = squares + plain * plain
@@ -189,12 +189,13 @@
             out_ref[w, :, i * LANES : (i + 1) * LANES] = turned[w * (samples // LANES) + i]
 
 
-def detect(order, groups, templates, series, before, each, parts, factor):
+def detect(order, groups, templates, series, before, parts, factor):
     n_all = templates.shape[0]
     block, spread = groups.shape
     stations = 4
     slots = block * spread * stations
-    rows = series.shape[1] // (3 * stations)
+    ahead = 3 * stations * L // LANES
+    rows = (series.shape[1] - ahead) // (3 * stations)
     padded = rows + 8
     samples = rows * LANES // parts
     spare = -(-(slots + stations) // 8) * 8
@@ -212,7 +213,7 @@
         refs = list(refs)
         if before is None:
             refs.insert(4, None)
-        detect_kernel(each, factor, *refs)
+        detect_kernel(factor, *refs)
 
     return pl.pallas_call(
         body,
@@ -224,7 +225,7 @@
             pltpu.SMEM((n_all * SLOTS,), jnp.int32),
             pltpu.SMEM((n_all,), jnp.int32),
             pltpu.VMEM((slots * 3 * L // LANES, LANES), jnp.float32),
-            pltpu.VMEM((n_all * (templates.shape[1] - each), LANES), jnp.float32),
+            pltpu.VMEM((series.shape[0] * ahead, LANES), jnp.float32),
             pltpu.VMEM((spare, WIDTH), jnp.float32),
             pltpu.VMEM((spare, LANES), jnp.float32),
             pltpu.VMEM((3 * LANES, LANES), jnp.bfloat16),
@@ -276,11 +277,12 @@
     own = templates.reshape(-1, LANES)
     front = around[0].reshape(lines, steps, LANES)[:, : L // LANES]
     tail = lax.ppermute(front, "tm", [(i + n_b, i) for i in range(n_tm - n_b)])
-    tail = jnp.broadcast_to(tail.reshape(1, -1, LANES), (n_sta, lines * L // LANES, LANES))
     block = copies_to(own, "tm", far)
-    block = lax.all_to_all(jnp.concatenate([block, tail], axis=1), "sta", 0, 0, tiled=True)
+    block = lax.all_to_all(block, "sta", 0, 0, tiled=True)
+    tail, block = lax.optimization_barrier((tail, block))
     main = around.reshape(n_b, lines, steps, LANES)
-    mine = main.transpose(1, 0, 2, 3).reshape(-1, LANES)
+    main = main.transpose(1, 0, 2, 3).reshape(-1, LANES)
+    mine = jnp.concatenate([main, tail.reshape(-1, LANES)])
 
     cores = 2
     n_y = n_sta // cores
@@ -294,9 +296,9 @@
     others = lax.ppermute(pieces, "sta", swap)
     rows_of_y = lax.rem(y - jnp.arange(n_y, dtype=jnp.int32) + n_y, n_y) * cores
     factor = math.sqrt(channels * L / (spread * stations))
-    total = detect(rows_of_y + core, groups, block, pieces, None, own.shape[0], n_b, None)
+    total = detect(rows_of_y + core, groups, block, pieces, None, n_b, None)
     other = rows_of_y + 1 - core
-    total = detect(other, groups, block, others, total, own.shape[0], n_b, factor)
+    total = detect(other, groups, block, others, total, n_b, factor)
 
     found = lax.all_to_all(total, "tm", 0, 0, axis_index_groups=near, tiled=True)
     return found.reshape(n_b * n_a, samples)

time: 89.7 us -> 100 us (1.11); the launches traced: 88.1 us -> 99.6 us
  waiting for transfers between devices: 8.11 us -> 19.5 us
    ppermute x3, waiting for transfers between devices: 0.01 us -> 9.32 us  [on_device(): pieces.append(lax.ppermute(mine, 'sta', pairs))]
    ppermute x1, waiting for transfers between devices: 0.01 us -> 4.26 us  [on_device(): tail = lax.ppermute(front, 'tm', [(i + n_b, i) for i in range(n_tm - n_b)])]
    all_to_all x1, waiting for transfers between devices: 3.93 us -> 1.16 us  [on_device(): block = lax.all_to_all(block, 'sta', 0, 0, tiled=True)]
    all_to_all x1, starting transfers between devices: 7.12 us -> 9.64 us  [on_device(): block = lax.all_to_all(block, 'sta', 0, 0, tiled=True)]
    ppermute x3, starting transfers between devices: 9.5 us -> 8.02 us  [on_device(): pieces.append(lax.ppermute(mine, 'sta', pairs))]
  transfers between devices with their start and end apart: 8 -> 8, of which waited for: 2 -> 6; matrix products, arithmetic and copies ran while one was open for 1% -> 0% of each run, Pallas kernels for 9% -> 8%
where the time goes in v13:
time: 100 us; the launch traced here: 99.6 us
  starting transfers between devices  40.8 us (41%)
  blocking collectives  20.2 us (20%)
  waiting for transfers between devices  19.5 us (20%)
  Pallas kernels  16.2 us (16%)
  local copies, waits for them, and re-layouts  2.49 us (2%)
    pallas_call x2, Pallas kernels, detect(): pl.pallas_call(body, out_shape=out_shape, in_specs=[pl.BlockSpec(memory_s...  16.2 us
    all_to_all x1, starting transfers between devices, copies_to(): lax.all_to_all(spread, axis, 0, 0, axis_index_groups=groups, tiled=True)  15.8 us
    all_to_all x1, blocking collectives, on_device(): lax.all_to_all(total, 'tm', 0, 0, axis_index_groups=near, tiled=True)  10.3 us
    all_gather x1, blocking collectives, on_device(): lax.all_gather(record.reshape(lines * steps, LANES), 'tm', axis_index_gro...  9.93 us
    all_to_all x1, starting transfers between devices, on_device(): block = lax.all_to_all(block, 'sta', 0, 0, tiled=True)  9.64 us
    ppermute x3, waiting for transfers between devices, on_device(): pieces.append(lax.ppermute(mine, 'sta', pairs))  9.32 us
    ppermute x3, starting transfers between devices, on_device(): pieces.append(lax.ppermute(mine, 'sta', pairs))  8.02 us
    ppermute x1, waiting for transfers between devices, on_device(): tail = lax.ppermute(front, 'tm', [(i + n_b, i) for i in range(n_tm - n_b)])  4.26 us
  transfers between devices with their start and end apart: 8, of which 6 were waited for; matrix products, arithmetic and copies ran while one was open for 0% of the time, Pallas kernels for 8%

profile of v13, /device:TPU:1, one launch (start us, length us, event | category | flops | bytes accessed | tf_op | source)
XLA Modules:
  0.0 99.6 jit_solution(13108942548513494026)
XLA Ops:
  0.0 0.0 copy-start
  0.0 0.8 broadcast_in_dim.7
  0.8 0.7 broadcast_in_dim.8
  1.6 0.0 copy-start.1
  1.6 15.8 %all-to-all-start = ((bf16[8,144,128]{2,1,0:T(8,128)(2,1)}), bf16[8,144,128]{2,1,0:T(8,128)(2,1)}, u32[]{:S(2)}, u32[]{:S(2)}) async-start(bf16[8,144,128]{2,1,0:T(8,128)(2,1)} %broadcast_in_dim.8), calls=%async_computation | async-start | bytes 589824 | tf_op jit(solution)/shard_map/all_to_all | solution.py:253
  17.3 0.0 copy-done.1
  17.4 9.9 %all_gather.3 = bf16[4,96,128]{2,1,0:T(8,128)(2,1)S(1)} all-gather(bf16[1,96,128]{2,1,0:T(8,128)(2,1)S(1)} %all_gather_reshape.3), channel_id=1, replica_groups={{0,8,16,24},{32,40,48,56},{64,72,80,88},{96,104,112,120},{128,136,144,1..., dimensions={0}, use_global_device_ids=true | all-gather | bytes 122880 | tf_op jit(solution)/shard_map/all_gather | solution.py:273
  27.3 2.8 %collective-permute-start = (bf16[4,96,128]{2,1,0:T(8,128)(2,1)S(1)}, bf16[4,96,128]{2,1,0:T(8,128)(2,1)S(1)}, u32[]{:S(2)}, u32[]{:S(2)}) collective-permute-start(bf16[4,96,128]{2,1,0:T(8,128)(2,1)S(1)} %all_gather.3), channel_id=1, source_target_pairs={{0,32},{8,40},{16,48},{24,56},{32,0},{40,8},{48,16},{56,24},{64,96... | collective-permute-start | bytes 294920 | tf_op jit(solution)/shard_map/ppermute | solution.py:274
  30.1 0.0 copy-done
  30.1 0.1 constant_dynamic-slice_fusion
  30.2 0.1 copy.9.refs_1_
  30.3 4.1 %collective-permute-done = bf16[4,96,128]{2,1,0:T(8,128)(2,1)S(1)} collective-permute-done((bf16[4,96,128]{2,1,0:T(8,128)(2,1)S(1)}, bf16[4,96,128]{2,1,0:T(8,128)(2,1)S(1)}, u32[]{:S(2)}, u32[]{:S(2)}) %collective-permute-start) | collective-permute-done | bytes 98336 | tf_op jit(solution)/shard_map/ppermute | solution.py:274
  34.4 0.7 all-to-all-done
  35.1 9.6 %all-to-all-start.1 = ((bf16[8,144,128]{2,1,0:T(8,128)(2,1)}), bf16[8,144,128]{2,1,0:T(8,128)(2,1)S(1)}, u32[]{:S(2)}, u32[]{:S(2)}) async-start(bf16[8,144,128]{2,1,0:T(8,128)(2,1)} %all-to-all-done), calls=%async_computation.1 | async-start | bytes 589824 | tf_op jit(solution)/shard_map/all_to_all | solution.py:281
  44.7 1.3 %collective-permute-start.1 = (bf16[12,4,128]{2,1,0:T(4,128)(2,1)S(1)}, bf16[12,4,128]{2,1,0:T(4,128)(2,1)S(1)}, u32[]{:S(2)}, u32[]{:S(2)}) collective-permute-start(bf16[12,4,128]{2,1,0:T(4,128)(2,1)S(1)} %slice.9), channel_id=1, source_target_pairs={{64,0},{72,8},{80,16},{88,24},{96,32},{104,40},{112,48},{120,56},{... | collective-permute-start | bytes 36872 | tf_op jit(solution)/shard_map/ppermute | solution.py:279
  46.1 4.3 %collective-permute-done.1 = bf16[12,4,128]{2,1,0:T(4,128)(2,1)S(1)} collective-permute-done((bf16[12,4,128]{2,1,0:T(4,128)(2,1)S(1)}, bf16[12,4,128]{2,1,0:T(4,128)(2,1)S(1)}, u32[]{:S(2)}, u32[]{:S(2)}) %collective-permute-start.1) | collective-permute-done | bytes 12320 | tf_op jit(solution)/shard_map/ppermute | solution.py:279
  50.4 1.2 %all-to-all-done.1.refs_2_ = bf16[8,144,128]{2,1,0:T(8,128)(2,1)S(1)} async-done(((bf16[8,144,128]{2,1,0:T(8,128)(2,1)}), bf16[8,144,128]{2,1,0:T(8,128)(2,1)S(1)}, u32[]{:S(2)}, u32[]{:S(2)}) %all-to-all-start.1) | async-done | bytes 294944 | tf_op jit(solution)/shard_map/all_to_all | solution.py:281
  51.6 3.3 %collective-permute-start.4 = (bf16[816,128]{1,0:T(8,128)(2,1)S(1)}, bf16[816,128]{1,0:T(8,128)(2,1)S(1)}, u32[]{:S(2)}, u32[]{:S(2)}) collective-permute-start(bf16[816,128]{1,0:T(8,128)(2,1)S(1)} %get-tuple-element.10), channel_id=1, source_target_pairs={{0,6},{1,7},{2,0},{3,1},{4,2},{5,3},{6,4},{7,5},{8,14},{9,15},{10,... | collective-permute-start | bytes 626696 | tf_op jit(solution)/shard_map/ppermute | solution.py:293
  54.9 2.5 %collective-permute-start.3 = (bf16[816,128]{1,0:T(8,128)(2,1)S(1)}, bf16[816,128]{1,0:T(8,128)(2,1)S(1)}, u32[]{:S(2)}, u32[]{:S(2)}) collective-permute-start(bf16[816,128]{1,0:T(8,128)(2,1)S(1)} %get-tuple-element.10), channel_id=1, source_target_pairs={{0,4},{1,5},{2,6},{3,7},{4,0},{5,1},{6,2},{7,3},{8,12},{9,13},{10,... | collective-permute-start | bytes 626696 | tf_op jit(solution)/shard_map/ppermute | solution.py:293
  57.5 2.1 %collective-permute-start.2 = (bf16[816,128]{1,0:T(8,128)(2,1)S(1)}, bf16[816,128]{1,0:T(8,128)(2,1)S(1)}, u32[]{:S(2)}, u32[]{:S(2)}) collective-permute-start(bf16[816,128]{1,0:T(8,128)(2,1)S(1)} %get-tuple-element.10), channel_id=1, source_target_pairs={{0,2},{1,3},{2,4},{3,5},{4,6},{5,7},{6,0},{7,1},{8,10},{9,11},{10,... | collective-permute-start | bytes 626696 | tf_op jit(solution)/shard_map/ppermute | solution.py:293
  59.6 0.0 collective-permute-done.4
  59.7 3.8 %collective-permute-done.3 = bf16[816,128]{1,0:T(8,128)(2,1)S(1)} collective-permute-done((bf16[816,128]{1,0:T(8,128)(2,1)S(1)}, bf16[816,128]{1,0:T(8,128)(2,1)S(1)}, u32[]{:S(2)}, u32[]{:S(2)}) %collective-permute-start.3) | collective-permute-done | bytes 208928 | tf_op jit(solution)/shard_map/ppermute | solution.py:293
  63.5 5.5 %collective-permute-done.2 = bf16[816,128]{1,0:T(8,128)(2,1)S(1)} collective-permute-done((bf16[816,128]{1,0:T(8,128)(2,1)S(1)}, bf16[816,128]{1,0:T(8,128)(2,1)S(1)}, u32[]{:S(2)}, u32[]{:S(2)}) %collective-permute-start.2) | collective-permute-done | bytes 208928 | tf_op jit(solution)/shard_map/ppermute | solution.py:293
  69.0 0.1 pad_maximum_fusion.refs_3_
  69.1 3.3 %collective-permute-start.5 = (bf16[4,816,128]{2,1,0:T(8,128)(2,1)S(1)}, bf16[4,816,128]{2,1,0:T(8,128)(2,1)S(1)}, u32[]{:S(2)}, u32[]{:S(2)}) collective-permute-start(bf16[4,816,128]{2,1,0:T(8,128)(2,1)S(1)} %pad_maximum_fusion.refs_3_), channel_id=1, source_target_pairs={{0,1},{1,0},{2,3},{3,2},{4,5},{5,4},{6,7},{7,6},{8,9},{9,8},{10,11... | collective-permute-start | bytes 2506760 | tf_op jit(solution)/shard_map/ppermute | solution.py:296
  72.4 8.0 %shard_map.37.refs_4_ = f32[9,64,128]{2,1,0:T(8,128)S(1)} custom-call(s32[4]{0:T(128)S(1)} %broadcast_add_fusion.refs_0_, s32[8,3]{1,0:T(8,128)S(1)} %copy.9.refs_1_, bf16[8,144,128]{2,1,0:T(8,128)(2,1)S(1)} %all-to-all-done.1.refs_2_, bf16[4,816,128]{2,1,0:T(8,128)(2,1)S(1)} %pad_maximum_fusion.refs_3_), custom_call_target="tpu_custom_call" | custom-call | flops 15032385536 | bytes 557056 | tf_op jit(solution)/shard_map/pallas_call | solution.py:218
  80.4 0.0 collective-permute-done.5.refs_3_
  80.5 8.2 %shard_map.38 = f32[8,8,1024]{2,1,0:T(8,128)S(1)} custom-call(s32[4]{0:T(128)S(1)} %add_subtract_fusion.refs_0_, s32[8,3]{1,0:T(8,128)S(1)} %copy.9.refs_1_, bf16[8,144,128]{2,1,0:T(8,128)(2,1)S(1)} %all-to-all-done.1.refs_2_, bf16[4,816,128]{2,1,0:T(8,128)(2,1)S(1)} %collective-permute-done.5.refs_3_, f32[9,64,128]{2,1,0:T(8,128)S(1)} %shard_map.37.refs_4_), custom_call_target="tpu_custom_call" | custom-call | flops 15032385536 | bytes 557056 | tf_op jit(solution)/shard_map/pallas_call | solution.py:218
  88.6 10.3 %all_to_all.15 = f32[8,8,1024]{2,1,0:T(8,128)S(1)} all-to-all(f32[8,8,1024]{2,1,0:T(8,128)S(1)} %shard_map.38), channel_id=1, replica_groups={{0,8,16,24,32,40,48,56},{64,72,80,88,96,104,112,120},{128,136,144,152,1..., dimensions={0} | all-to-all | bytes 524288 | tf_op jit(solution)/shard_map/all_to_all | solution.py:303
  98.9 0.7 copy.11
  (9 shorter events, 0.2 us)
Async XLA Ops:
  0.0 30.1 %copy-start = (s32[512,3]{0,1:T(4,128)S(1)}, s32[512,3]{0,1:T(4,128)}, u32[]{:S(2)}) copy-start(s32[512,3]{0,1:T(4,128)} %param.5) | copy-start | bytes 18436
  1.6 15.8 %copy-start.1 = (bf16[3,4,1024]{2,1,0:T(4,128)(2,1)S(1)}, bf16[3,4,1024]{2,1,0:T(4,128)(2,1)}, u32[]{:S(2)}) copy-start(bf16[3,4,1024]{2,1,0:T(4,128)(2,1)} %param.3) | copy-start | bytes 73732
  1.6 33.5 %all-to-all-start = ((bf16[8,144,128]{2,1,0:T(8,128)(2,1)}), bf16[8,144,128]{2,1,0:T(8,128)(2,1)}, u32[]{:S(2)}, u32[]{:S(2)}) async-start(bf16[8,144,128]{2,1,0:T(8,128)(2,1)} %broadcast_in_dim.8), calls=%async_computation | async-start | bytes 589824 | tf_op jit(solution)/shard_map/all_to_all | solution.py:253
  27.3 7.1 %collective-permute-start = (bf16[4,96,128]{2,1,0:T(8,128)(2,1)S(1)}, bf16[4,96,128]{2,1,0:T(8,128)(2,1)S(1)}, u32[]{:S(2)}, u32[]{:S(2)}) collective-permute-start(bf16[4,96,128]{2,1,0:T(8,128)(2,1)S(1)} %all_gather.3), channel_id=1, source_target_pairs={{0,32},{8,40},{16,48},{24,56},{32,0},{40,8},{48,16},{56,24},{64,96... | collective-permute-start | bytes 294920 | tf_op jit(solution)/shard_map/ppermute | solution.py:274
  35.1 16.5 %all-to-all-start.1 = ((bf16[8,144,128]{2,1,0:T(8,128)(2,1)}), bf16[8,144,128]{2,1,0:T(8,128)(2,1)S(1)}, u32[]{:S(2)}, u32[]{:S(2)}) async-start(bf16[8,144,128]{2,1,0:T(8,128)(2,1)} %all-to-all-done), calls=%async_computation.1 | async-start | bytes 589824 | tf_op jit(solution)/shard_map/all_to_all | solution.py:281
  44.7 5.6 %collective-permute-start.1 = (bf16[12,4,128]{2,1,0:T(4,128)(2,1)S(1)}, bf16[12,4,128]{2,1,0:T(4,128)(2,1)S(1)}, u32[]{:S(2)}, u32[]{:S(2)}) collective-permute-start(bf16[12,4,128]{2,1,0:T(4,128)(2,1)S(1)} %slice.9), channel_id=1, source_target_pairs={{64,0},{72,8},{80,16},{88,24},{96,32},{104,40},{112,48},{120,56},{... | collective-permute-start | bytes 36872 | tf_op jit(solution)/shard_map/ppermute | solution.py:279
  51.6 8.1 %collective-permute-start.4 = (bf16[816,128]{1,0:T(8,128)(2,1)S(1)}, bf16[816,128]{1,0:T(8,128)(2,1)S(1)}, u32[]{:S(2)}, u32[]{:S(2)}) collective-permute-start(bf16[816,128]{1,0:T(8,128)(2,1)S(1)} %get-tuple-element.10), channel_id=1, source_target_pairs={{0,6},{1,7},{2,0},{3,1},{4,2},{5,3},{6,4},{7,5},{8,14},{9,15},{10,... | collective-permute-start | bytes 626696 | tf_op jit(solution)/shard_map/ppermute | solution.py:293
  54.9 8.6 %collective-permute-start.3 = (bf16[816,128]{1,0:T(8,128)(2,1)S(1)}, bf16[816,128]{1,0:T(8,128)(2,1)S(1)}, u32[]{:S(2)}, u32[]{:S(2)}) collective-permute-start(bf16[816,128]{1,0:T(8,128)(2,1)S(1)} %get-tuple-element.10), channel_id=1, source_target_pairs={{0,4},{1,5},{2,6},{3,7},{4,0},{5,1},{6,2},{7,3},{8,12},{9,13},{10,... | collective-permute-start | bytes 626696 | tf_op jit(solution)/shard_map/ppermute | solution.py:293
  57.5 11.5 %collective-permute-start.2 = (bf16[816,128]{1,0:T(8,128)(2,1)S(1)}, bf16[816,128]{1,0:T(8,128)(2,1)S(1)}, u32[]{:S(2)}, u32[]{:S(2)}) collective-permute-start(bf16[816,128]{1,0:T(8,128)(2,1)S(1)} %get-tuple-element.10), channel_id=1, source_target_pairs={{0,2},{1,3},{2,4},{3,5},{4,6},{5,7},{6,0},{7,1},{8,10},{9,11},{10,... | collective-permute-start | bytes 626696 | tf_op jit(solution)/shard_map/ppermute | solution.py:293
  69.1 11.4 %collective-permute-start.5 = (bf16[4,816,128]{2,1,0:T(8,128)(2,1)S(1)}, bf16[4,816,128]{2,1,0:T(8,128)(2,1)S(1)}, u32[]{:S(2)}, u32[]{:S(2)}) collective-permute-start(bf16[4,816,128]{2,1,0:T(8,128)(2,1)S(1)} %pad_maximum_fusion.refs_3_), channel_id=1, source_target_pairs={{0,1},{1,0},{2,3},{3,2},{4,5},{5,4},{6,7},{7,6},{8,9},{9,8},{10,11... | collective-permute-start | bytes 2506760 | tf_op jit(solution)/shard_map/ppermute | solution.py:296

commit v14 on v13

--- a/solution.py
+++ b/solution.py
@@ -270,19 +270,23 @@
     steps = samples // LANES
     half = n_b // 2
     four = [[i + j for j in range(half)] for i in range(0, n_tm, half)]
-    same = lax.all_gather(record.reshape(lines * steps, LANES), "tm", axis_index_groups=four)
-    other = lax.ppermute(same, "tm", [(i, i ^ half) for i in range(n_tm)])
+    head = lax.ppermute(record[:, :, :L], "tm", [(i + half, i) for i in range(n_tm - half)])
+    piece = [record.reshape(lines * steps, LANES), head.reshape(-1, LANES)]
+    four_pieces = lax.all_gather(jnp.concatenate(piece), "tm", axis_index_groups=four)
+    same = four_pieces[:, : lines * steps].reshape(-1, LANES)
+    next_head = four_pieces[0, lines * steps :]
+    sent = jnp.concatenate([same, next_head])
+    other = lax.ppermute(sent, "tm", [(i, i ^ half) for i in range(n_tm)])
+    other, other_head = other[: same.shape[0]], other[same.shape[0] :]
     upper = lax.rem(m // half, 2) == 1
     around = jnp.concatenate([jnp.where(upper, other, same), jnp.where(upper, same, other)])
+    tail = jnp.where(upper, next_head, other_head)
     own = templates.reshape(-1, LANES)
-    front = around[0].reshape(lines, steps, LANES)[:, : L // LANES]
-    tail = lax.ppermute(front, "tm", [(i + n_b, i) for i in range(n_tm - n_b)])
     block = copies_to(own, "tm", far)
     block = lax.all_to_all(block, "sta", 0, 0, tiled=True)
-    tail, block = lax.optimization_barrier((tail, block))
     main = around.reshape(n_b, lines, steps, LANES)
     main = main.transpose(1, 0, 2, 3).reshape(-1, LANES)
-    mine = jnp.concatenate([main, tail.reshape(-1, LANES)])
+    mine = jnp.concatenate([main, tail])
 
     cores = 2
     n_y = n_sta // cores

time: 100 us -> 90.5 us (0.905)
  waiting for transfers between devices: 19.5 us -> 5.12 us
  starting transfers between devices: 40.8 us -> 42.5 us
  local copies, waits for them, and re-layouts: 2.49 us -> 3.93 us
    ppermute x3, waiting for transfers between devices: 9.32 us -> 0.01 us  [on_device(): pieces.append(lax.ppermute(mine, 'sta', pairs))]
    ppermute x2, waiting for transfers between devices: 8.36 us -> 3.83 us  [the longest x1 3.83 us: on_device(): other = lax.ppermute(sent, 'tm', [(i, i ^ half) for i in range(n_tm)])]
    all_to_all x1, starting transfers between devices: 9.64 us -> 7.06 us  [on_device(): block = lax.all_to_all(block, 'sta', 0, 0, tiled=True)]
    ppermute x1, starting transfers between devices: 3.31 us -> 5.29 us  [on_device(): others = lax.ppermute(pieces, 'sta', swap)]
    ppermute x3, starting transfers between devices: 8.02 us -> 9.5 us  [on_device(): pieces.append(lax.ppermute(mine, 'sta', pairs))]
  transfers between devices with their start and end apart: 8 -> 8, of which waited for: 6 -> 2; matrix products, arithmetic and copies ran while one was open for 0% -> 2% of each run, Pallas kernels for 8% -> 9%
where the time goes in v14:
time: 90.5 us; the launch traced here: 89.4 us
  starting transfers between devices  42.5 us (47%)
  blocking collectives  21.1 us (23%)
  Pallas kernels  16.2 us (18%)
  waiting for transfers between devices  5.12 us (6%)
  local copies, waits for them, and re-layouts  3.93 us (4%)
    all_to_all x1, starting transfers between devices, copies_to(): lax.all_to_all(spread, axis, 0, 0, axis_index_groups=groups, tiled=True)  16.3 us
    pallas_call x2, Pallas kernels, detect(): pl.pallas_call(body, out_shape=out_shape, in_specs=[pl.BlockSpec(memory_s...  16.2 us
    all_to_all x1, blocking collectives, on_device(): lax.all_to_all(total, 'tm', 0, 0, axis_index_groups=near, tiled=True)  10.8 us
    all_gather x1, blocking collectives, on_device(): lax.all_gather(jnp.concatenate(piece), 'tm', axis_index_groups=four)  10.4 us
    ppermute x3, starting transfers between devices, on_device(): pieces.append(lax.ppermute(mine, 'sta', pairs))  9.5 us
    all_to_all x1, starting transfers between devices, on_device(): block = lax.all_to_all(block, 'sta', 0, 0, tiled=True)  7.06 us
    ppermute x1, starting transfers between devices, on_device(): others = lax.ppermute(pieces, 'sta', swap)  5.29 us
    ppermute x1, waiting for transfers between devices, on_device(): other = lax.ppermute(sent, 'tm', [(i, i ^ half) for i in range(n_tm)])  3.83 us
  transfers between devices with their start and end apart: 8, of which 2 were waited for; matrix products, arithmetic and copies ran while one was open for 2% of the time, Pallas kernels for 9%

profile of v14, /device:TPU:1, one launch (start us, length us, event | category | flops | bytes accessed | tf_op | source)
XLA Modules:
  0.0 89.4 jit_solution(229292443563707764)
XLA Ops:
  0.0 0.0 copy-start
  0.0 0.7 slice.15
  0.7 1.3 %collective-permute-start = (bf16[3,4,512]{2,1,0:T(4,128)(2,1)S(1)}, bf16[3,4,512]{2,1,0:T(4,128)(2,1)S(1)}, u32[]{:S(2)}, u32[]{:S(2)}) collective-permute-start(bf16[3,4,512]{2,1,0:T(4,128)(2,1)S(1)} %slice.15), channel_id=1, source_target_pairs={{32,0},{40,8},{48,16},{56,24},{64,32},{72,40},{80,48},{88,56},{96,... | collective-permute-start | bytes 36872 | tf_op jit(solution)/shard_map/ppermute | solution.py:273
  2.0 0.8 broadcast_in_dim.7
  2.8 0.7 broadcast_in_dim.8
  3.6 16.3 %all-to-all-start = ((bf16[8,144,128]{2,1,0:T(8,128)(2,1)}), bf16[8,144,128]{2,1,0:T(8,128)(2,1)}, u32[]{:S(2)}, u32[]{:S(2)}) async-start(bf16[8,144,128]{2,1,0:T(8,128)(2,1)} %broadcast_in_dim.8), calls=%async_computation | async-start | bytes 589824 | tf_op jit(solution)/shard_map/all_to_all | solution.py:253
  19.8 0.0 copy-start.1
  19.8 0.7 copy-done.1
  20.6 0.0 collective-permute-done
  20.7 10.4 %all-gather = bf16[576,128]{1,0:T(8,128)(2,1)S(1)} all-gather(bf16[144,128]{1,0:T(8,128)(2,1)S(1)} %pad_maximum_fusion.4), channel_id=2, replica_groups={{0,8,16,24},{32,40,48,56},{64,72,80,88},{96,104,112,120},{128,136,144,1..., dimensions={0}, use_global_device_ids=true | all-gather | bytes 184320 | tf_op jit(solution)/shard_map/all_gather | solution.py:275
  31.1 3.1 %collective-permute-start.1 = (bf16[432,128]{1,0:T(8,128)(2,1)S(1)}, bf16[432,128]{1,0:T(8,128)(2,1)S(1)}, u32[]{:S(2)}, u32[]{:S(2)}) collective-permute-start(bf16[432,128]{1,0:T(8,128)(2,1)S(1)} %pad_maximum_fusion.3), channel_id=1, source_target_pairs={{0,32},{8,40},{16,48},{24,56},{32,0},{40,8},{48,16},{56,24},{64,96... | collective-permute-start | bytes 331784 | tf_op jit(solution)/shard_map/ppermute | solution.py:279
  34.2 0.0 copy-done
  34.2 0.1 constant_dynamic-slice_fusion
  34.3 3.8 %collective-permute-done.1 = bf16[432,128]{1,0:T(8,128)(2,1)S(1)} collective-permute-done((bf16[432,128]{1,0:T(8,128)(2,1)S(1)}, bf16[432,128]{1,0:T(8,128)(2,1)S(1)}, u32[]{:S(2)}, u32[]{:S(2)}) %collective-permute-start.1) | collective-permute-done | bytes 110624 | tf_op jit(solution)/shard_map/ppermute | solution.py:279
  38.3 4.6 %collective-permute-start.4 = (bf16[816,128]{1,0:T(8,128)(2,1)S(1)}, bf16[816,128]{1,0:T(8,128)(2,1)S(1)}, u32[]{:S(2)}, u32[]{:S(2)}) collective-permute-start(bf16[816,128]{1,0:T(8,128)(2,1)S(1)} %get-tuple-element.6), channel_id=1, source_target_pairs={{0,6},{1,7},{2,0},{3,1},{4,2},{5,3},{6,4},{7,5},{8,14},{9,15},{10,... | collective-permute-start | bytes 626696 | tf_op jit(solution)/shard_map/ppermute | solution.py:297
  42.9 2.3 %collective-permute-start.3 = (bf16[816,128]{1,0:T(8,128)(2,1)S(1)}, bf16[816,128]{1,0:T(8,128)(2,1)S(1)}, u32[]{:S(2)}, u32[]{:S(2)}) collective-permute-start(bf16[816,128]{1,0:T(8,128)(2,1)S(1)} %get-tuple-element.6), channel_id=1, source_target_pairs={{0,4},{1,5},{2,6},{3,7},{4,0},{5,1},{6,2},{7,3},{8,12},{9,13},{10,... | collective-permute-start | bytes 626696 | tf_op jit(solution)/shard_map/ppermute | solution.py:297
  45.2 2.6 %collective-permute-start.2 = (bf16[816,128]{1,0:T(8,128)(2,1)S(1)}, bf16[816,128]{1,0:T(8,128)(2,1)S(1)}, u32[]{:S(2)}, u32[]{:S(2)}) collective-permute-start(bf16[816,128]{1,0:T(8,128)(2,1)S(1)} %get-tuple-element.6), channel_id=1, source_target_pairs={{0,2},{1,3},{2,4},{3,5},{4,6},{5,7},{6,0},{7,1},{8,10},{9,11},{10,... | collective-permute-start | bytes 626696 | tf_op jit(solution)/shard_map/ppermute | solution.py:297
  47.8 0.0 all-to-all-done
  47.8 7.1 %all-to-all-start.1 = ((bf16[8,144,128]{2,1,0:T(8,128)(2,1)}), bf16[8,144,128]{2,1,0:T(8,128)(2,1)S(1)}, u32[]{:S(2)}, u32[]{:S(2)}) async-start(bf16[8,144,128]{2,1,0:T(8,128)(2,1)} %all-to-all-done), calls=%async_computation.1 | async-start | bytes 589824 | tf_op jit(solution)/shard_map/all_to_all | solution.py:286
  54.9 0.1 copy.6.refs_1_
  55.0 0.0 collective-permute-done.4
  55.0 0.0 collective-permute-done.3
  55.0 0.0 collective-permute-done.2
  55.0 0.1 pad_maximum_fusion.refs_3_
  55.1 5.3 %collective-permute-start.5 = (bf16[4,816,128]{2,1,0:T(8,128)(2,1)S(1)}, bf16[4,816,128]{2,1,0:T(8,128)(2,1)S(1)}, u32[]{:S(2)}, u32[]{:S(2)}) collective-permute-start(bf16[4,816,128]{2,1,0:T(8,128)(2,1)S(1)} %pad_maximum_fusion.refs_3_), channel_id=1, source_target_pairs={{0,1},{1,0},{2,3},{3,2},{4,5},{5,4},{6,7},{7,6},{8,9},{9,8},{10,11... | collective-permute-start | bytes 2506760 | tf_op jit(solution)/shard_map/ppermute | solution.py:300
  60.4 1.3 %all-to-all-done.1.refs_2_ = bf16[8,144,128]{2,1,0:T(8,128)(2,1)S(1)} async-done(((bf16[8,144,128]{2,1,0:T(8,128)(2,1)}), bf16[8,144,128]{2,1,0:T(8,128)(2,1)S(1)}, u32[]{:S(2)}, u32[]{:S(2)}) %all-to-all-start.1) | async-done | bytes 294944 | tf_op jit(solution)/shard_map/all_to_all | solution.py:286
  61.7 8.0 %shard_map.37.refs_4_ = f32[9,64,128]{2,1,0:T(8,128)S(1)} custom-call(s32[4]{0:T(128)S(1)} %broadcast_add_fusion.refs_0_, s32[8,3]{1,0:T(8,128)S(1)} %copy.6.refs_1_, bf16[8,144,128]{2,1,0:T(8,128)(2,1)S(1)} %all-to-all-done.1.refs_2_, bf16[4,816,128]{2,1,0:T(8,128)(2,1)S(1)} %pad_maximum_fusion.refs_3_), custom_call_target="tpu_custom_call" | custom-call | flops 15032385536 | bytes 557056 | tf_op jit(solution)/shard_map/pallas_call | solution.py:218
  69.7 0.0 collective-permute-done.5.refs_3_
  69.7 8.2 %shard_map.38 = f32[8,8,1024]{2,1,0:T(8,128)S(1)} custom-call(s32[4]{0:T(128)S(1)} %add_subtract_fusion.refs_0_, s32[8,3]{1,0:T(8,128)S(1)} %copy.6.refs_1_, bf16[8,144,128]{2,1,0:T(8,128)(2,1)S(1)} %all-to-all-done.1.refs_2_, bf16[4,816,128]{2,1,0:T(8,128)(2,1)S(1)} %collective-permute-done.5.refs_3_, f32[9,64,128]{2,1,0:T(8,128)S(1)} %shard_map.37.refs_4_), custom_call_target="tpu_custom_call" | custom-call | flops 15032385536 | bytes 557056 | tf_op jit(solution)/shard_map/pallas_call | solution.py:218
  77.9 10.8 %all_to_all.15 = f32[8,8,1024]{2,1,0:T(8,128)S(1)} all-to-all(f32[8,8,1024]{2,1,0:T(8,128)S(1)} %shard_map.38), channel_id=1, replica_groups={{0,8,16,24,32,40,48,56},{64,72,80,88,96,104,112,120},{128,136,144,152,1..., dimensions={0} | all-to-all | bytes 524288 | tf_op jit(solution)/shard_map/all_to_all | solution.py:307
  88.7 0.7 copy.8
  (13 shorter events, 0.2 us)
Async XLA Ops:
  0.0 34.2 %copy-start = (s32[512,3]{0,1:T(4,128)S(1)}, s32[512,3]{0,1:T(4,128)}, u32[]{:S(2)}) copy-start(s32[512,3]{0,1:T(4,128)} %param.5) | copy-start | bytes 18436
  0.7 19.9 %collective-permute-start = (bf16[3,4,512]{2,1,0:T(4,128)(2,1)S(1)}, bf16[3,4,512]{2,1,0:T(4,128)(2,1)S(1)}, u32[]{:S(2)}, u32[]{:S(2)}) collective-permute-start(bf16[3,4,512]{2,1,0:T(4,128)(2,1)S(1)} %slice.15), channel_id=1, source_target_pairs={{32,0},{40,8},{48,16},{56,24},{64,32},{72,40},{80,48},{88,56},{96,... | collective-permute-start | bytes 36872 | tf_op jit(solution)/shard_map/ppermute | solution.py:273
  3.6 44.2 %all-to-all-start = ((bf16[8,144,128]{2,1,0:T(8,128)(2,1)}), bf16[8,144,128]{2,1,0:T(8,128)(2,1)}, u32[]{:S(2)}, u32[]{:S(2)}) async-start(bf16[8,144,128]{2,1,0:T(8,128)(2,1)} %broadcast_in_dim.8), calls=%async_computation | async-start | bytes 589824 | tf_op jit(solution)/shard_map/all_to_all | solution.py:253
  19.8 0.7 copy-start.1
  31.1 7.0 %collective-permute-start.1 = (bf16[432,128]{1,0:T(8,128)(2,1)S(1)}, bf16[432,128]{1,0:T(8,128)(2,1)S(1)}, u32[]{:S(2)}, u32[]{:S(2)}) collective-permute-start(bf16[432,128]{1,0:T(8,128)(2,1)S(1)} %pad_maximum_fusion.3), channel_id=1, source_target_pairs={{0,32},{8,40},{16,48},{24,56},{32,0},{40,8},{48,16},{56,24},{64,96... | collective-permute-start | bytes 331784 | tf_op jit(solution)/shard_map/ppermute | solution.py:279
  38.3 16.7 %collective-permute-start.4 = (bf16[816,128]{1,0:T(8,128)(2,1)S(1)}, bf16[816,128]{1,0:T(8,128)(2,1)S(1)}, u32[]{:S(2)}, u32[]{:S(2)}) collective-permute-start(bf16[816,128]{1,0:T(8,128)(2,1)S(1)} %get-tuple-element.6), channel_id=1, source_target_pairs={{0,6},{1,7},{2,0},{3,1},{4,2},{5,3},{6,4},{7,5},{8,14},{9,15},{10,... | collective-permute-start | bytes 626696 | tf_op jit(solution)/shard_map/ppermute | solution.py:297
  42.9 12.1 %collective-permute-start.3 = (bf16[816,128]{1,0:T(8,128)(2,1)S(1)}, bf16[816,128]{1,0:T(8,128)(2,1)S(1)}, u32[]{:S(2)}, u32[]{:S(2)}) collective-permute-start(bf16[816,128]{1,0:T(8,128)(2,1)S(1)} %get-tuple-element.6), channel_id=1, source_target_pairs={{0,4},{1,5},{2,6},{3,7},{4,0},{5,1},{6,2},{7,3},{8,12},{9,13},{10,... | collective-permute-start | bytes 626696 | tf_op jit(solution)/shard_map/ppermute | solution.py:297
  45.2 9.8 %collective-permute-start.2 = (bf16[816,128]{1,0:T(8,128)(2,1)S(1)}, bf16[816,128]{1,0:T(8,128)(2,1)S(1)}, u32[]{:S(2)}, u32[]{:S(2)}) collective-permute-start(bf16[816,128]{1,0:T(8,128)(2,1)S(1)} %get-tuple-element.6), channel_id=1, source_target_pairs={{0,2},{1,3},{2,4},{3,5},{4,6},{5,7},{6,0},{7,1},{8,10},{9,11},{10,... | collective-permute-start | bytes 626696 | tf_op jit(solution)/shard_map/ppermute | solution.py:297
  47.8 13.9 %all-to-all-start.1 = ((bf16[8,144,128]{2,1,0:T(8,128)(2,1)}), bf16[8,144,128]{2,1,0:T(8,128)(2,1)S(1)}, u32[]{:S(2)}, u32[]{:S(2)}) async-start(bf16[8,144,128]{2,1,0:T(8,128)(2,1)} %all-to-all-done), calls=%async_computation.1 | async-start | bytes 589824 | tf_op jit(solution)/shard_map/all_to_all | solution.py:286
  55.1 14.6 %collective-permute-start.5 = (bf16[4,816,128]{2,1,0:T(8,128)(2,1)S(1)}, bf16[4,816,128]{2,1,0:T(8,128)(2,1)S(1)}, u32[]{:S(2)}, u32[]{:S(2)}) collective-permute-start(bf16[4,816,128]{2,1,0:T(8,128)(2,1)S(1)} %pad_maximum_fusion.refs_3_), channel_id=1, source_target_pairs={{0,1},{1,0},{2,3},{3,2},{4,5},{5,4},{6,7},{7,6},{8,9},{9,8},{10,11... | collective-permute-start | bytes 2506760 | tf_op jit(solution)/shard_map/ppermute | solution.py:300

commit v15 on v14

--- a/solution.py
+++ b/solution.py
@@ -27,7 +27,6 @@
     source,
     home,
     count,
-    wide,
     tails,
     waves,
     norms,
@@ -47,9 +46,8 @@
     padded = rows + 8
     ahead = tails.shape[0] // n_group
     tail = L // LANES
-    parts = 3 * L // LANES
-    slots = wide.shape[0] // parts
-    stations = slots // (block * spread)
+    stations = templates_ref.shape[2]
+    slots = block * spread * stations
     lane = lax.broadcasted_iota(jnp.int32, (1, LANES), 1)
     low = lane < HALF
 
@@ -69,16 +67,14 @@
             home[slot] = r
             count[named] = count[named] + 1
     spare = waves.shape[0] - slots
-    each = slots // block * parts
-    for r in range(block):
-        wide[r * each : (r + 1) * each, :] = templates_ref[r].astype(jnp.float32)
     for n in range(n_group):
         tails[n * ahead : (n + 1) * ahead, :] = series_ref[n, -ahead:, :].astype(jnp.float32)
     waves[...] = jnp.zeros_like(waves)
-    for c in range(3):
-        for v in range(L // LANES):
-            at = c * STEP + v * LANES
-            waves[0:slots, at : at + LANES] = wide[pl.ds(c * L // LANES + v, slots, parts), :]
+    for n in range(block * spread):
+        for c in range(3):
+            part = templates_ref[n // spread, n % spread, :, c * L : (c + 1) * L]
+            at = c * STEP
+            waves[n * stations : (n + 1) * stations, at : at + L] = part.astype(jnp.float32)
     squares = jnp.sum(jnp.square(waves[0:slots, :]), axis=1, keepdims=True)
     norms[0:slots, :] = jnp.broadcast_to(lax.rsqrt(squares + epsilon), (slots, LANES))
     norms[slots:, :] = jnp.zeros((spare, LANES), jnp.float32)
@@ -224,7 +220,6 @@
             pltpu.SMEM((n_all * SLOTS,), jnp.int32),
             pltpu.SMEM((n_all * SLOTS,), jnp.int32),
             pltpu.SMEM((n_all,), jnp.int32),
-            pltpu.VMEM((slots * 3 * L // LANES, LANES), jnp.float32),
             pltpu.VMEM((series.shape[0] * ahead, LANES), jnp.float32),
             pltpu.VMEM((spare, WIDTH), jnp.float32),
             pltpu.VMEM((spare, LANES), jnp.float32),
@@ -270,8 +265,8 @@
     steps = samples // LANES
     half = n_b // 2
     four = [[i + j for j in range(half)] for i in range(0, n_tm, half)]
-    head = lax.ppermute(record[:, :, :L], "tm", [(i + half, i) for i in range(n_tm - half)])
-    piece = [record.reshape(lines * steps, LANES), head.reshape(-1, LANES)]
+    head = lax.ppermute(record, "tm", [(i + half, i) for i in range(n_tm - half)])
+    piece = [record.reshape(lines * steps, LANES), head[:, :, :L].reshape(-1, LANES)]
     four_pieces = lax.all_gather(jnp.concatenate(piece), "tm", axis_index_groups=four)
     same = four_pieces[:, : lines * steps].reshape(-1, LANES)
     next_head = four_pieces[0, lines * steps :]
@@ -281,7 +276,7 @@
     upper = lax.rem(m // half, 2) == 1
     around = jnp.concatenate([jnp.where(upper, other, same), jnp.where(upper, same, other)])
     tail = jnp.where(upper, next_head, other_head)
-    own = templates.reshape(-1, LANES)
+    own = templates[0]
     block = copies_to(own, "tm", far)
     block = lax.all_to_all(block, "sta", 0, 0, tiled=True)
     main = around.reshape(n_b, lines, steps, LANES)

time: 90.5 us -> 90.1 us (level)
  no operation moved by 1% of the time
where the time goes in v15:
time: 90.1 us; the launch traced here: 88.9 us
  starting transfers between devices  42.6 us (47%)
  blocking collectives  21.1 us (23%)
  Pallas kernels  16.3 us (18%)
  waiting for transfers between devices  5.12 us (6%)
  local copies, waits for them, and re-layouts  3.23 us (4%)
    pallas_call x2, Pallas kernels, detect(): pl.pallas_call(body, out_shape=out_shape, in_specs=[pl.BlockSpec(memory_s...  16.3 us
    all_to_all x1, starting transfers between devices, copies_to(): lax.all_to_all(spread, axis, 0, 0, axis_index_groups=groups, tiled=True)  16.3 us
    all_to_all x1, blocking collectives, on_device(): lax.all_to_all(total, 'tm', 0, 0, axis_index_groups=near, tiled=True)  10.8 us
    all_gather x1, blocking collectives, on_device(): lax.all_gather(jnp.concatenate(piece), 'tm', axis_index_groups=four)  10.4 us
    ppermute x3, starting transfers between devices, on_device(): pieces.append(lax.ppermute(mine, 'sta', pairs))  9.5 us
    all_to_all x1, starting transfers between devices, on_device(): block = lax.all_to_all(block, 'sta', 0, 0, tiled=True)  7.07 us
    ppermute x1, starting transfers between devices, on_device(): others = lax.ppermute(pieces, 'sta', swap)  5.27 us
    ppermute x1, waiting for transfers between devices, on_device(): other = lax.ppermute(sent, 'tm', [(i, i ^ half) for i in range(n_tm)])  3.81 us
  transfers between devices with their start and end apart: 8, of which 2 were waited for; matrix products, arithmetic and copies ran while one was open for 2% of the time, Pallas kernels for 9%

profile of v15, /device:TPU:1, one launch (start us, length us, event | category | flops | bytes accessed | tf_op | source)
XLA Modules:
  0.0 88.9 jit_solution(9176164901190921079)
XLA Ops:
  0.0 0.0 copy-start
  0.0 1.4 %collective-permute-start = (bf16[3,4,1024]{2,1,0:T(4,128)(2,1)}, bf16[3,4,1024]{2,1,0:T(4,128)(2,1)S(1)}, u32[]{:S(2)}, u32[]{:S(2)}) collective-permute-start(bf16[3,4,1024]{2,1,0:T(4,128)(2,1)} %param.3), channel_id=1, source_target_pairs={{32,0},{40,8},{48,16},{56,24},{64,32},{72,40},{80,48},{88,56},{96,... | collective-permute-start | bytes 73736 | tf_op jit(solution)/shard_map/ppermute | solution.py:268
  1.4 1.6 %broadcast_in_dim.8 = bf16[8,3,4,1536]{3,2,1,0:T(4,128)(2,1)} broadcast(bf16[3,4,1536]{2,1,0:T(4,128)(2,1)} %bitcast.29), dimensions={1,2,3} | broadcast | bytes 331776 | tf_op jit(solution)/shard_map/broadcast_in_dim | solution.py:247
  3.0 16.3 %all-to-all-start = ((bf16[8,3,4,1536]{3,2,1,0:T(4,128)(2,1)}), bf16[8,3,4,1536]{3,2,1,0:T(4,128)(2,1)}, u32[]{:S(2)}, u32[]{:S(2)}) async-start(bf16[8,3,4,1536]{3,2,1,0:T(4,128)(2,1)} %broadcast_in_dim.8), calls=%async_computation | async-start | bytes 589824 | tf_op jit(solution)/shard_map/all_to_all | solution.py:248
  19.2 0.0 copy-start.1
  19.3 0.7 copy-done.1
  20.0 0.0 collective-permute-done
  20.1 10.4 %all-gather = bf16[576,128]{1,0:T(8,128)(2,1)S(1)} all-gather(bf16[144,128]{1,0:T(8,128)(2,1)S(1)} %pad_maximum_fusion.4), channel_id=2, replica_groups={{0,8,16,24},{32,40,48,56},{64,72,80,88},{96,104,112,120},{128,136,144,1..., dimensions={0}, use_global_device_ids=true | all-gather | bytes 184320 | tf_op jit(solution)/shard_map/all_gather | solution.py:270
  30.5 3.1 %collective-permute-start.1 = (bf16[432,128]{1,0:T(8,128)(2,1)S(1)}, bf16[432,128]{1,0:T(8,128)(2,1)S(1)}, u32[]{:S(2)}, u32[]{:S(2)}) collective-permute-start(bf16[432,128]{1,0:T(8,128)(2,1)S(1)} %pad_maximum_fusion.3), channel_id=1, source_target_pairs={{0,32},{8,40},{16,48},{24,56},{32,0},{40,8},{48,16},{56,24},{64,96... | collective-permute-start | bytes 331784 | tf_op jit(solution)/shard_map/ppermute | solution.py:274
  33.6 0.0 copy-done
  33.6 0.1 constant_dynamic-slice_fusion
  33.7 3.8 %collective-permute-done.1 = bf16[432,128]{1,0:T(8,128)(2,1)S(1)} collective-permute-done((bf16[432,128]{1,0:T(8,128)(2,1)S(1)}, bf16[432,128]{1,0:T(8,128)(2,1)S(1)}, u32[]{:S(2)}, u32[]{:S(2)}) %collective-permute-start.1) | collective-permute-done | bytes 110624 | tf_op jit(solution)/shard_map/ppermute | solution.py:274
  37.7 4.6 %collective-permute-start.4 = (bf16[816,128]{1,0:T(8,128)(2,1)S(1)}, bf16[816,128]{1,0:T(8,128)(2,1)S(1)}, u32[]{:S(2)}, u32[]{:S(2)}) collective-permute-start(bf16[816,128]{1,0:T(8,128)(2,1)S(1)} %get-tuple-element.6), channel_id=1, source_target_pairs={{0,6},{1,7},{2,0},{3,1},{4,2},{5,3},{6,4},{7,5},{8,14},{9,15},{10,... | collective-permute-start | bytes 626696 | tf_op jit(solution)/shard_map/ppermute | solution.py:292
  42.3 2.3 %collective-permute-start.3 = (bf16[816,128]{1,0:T(8,128)(2,1)S(1)}, bf16[816,128]{1,0:T(8,128)(2,1)S(1)}, u32[]{:S(2)}, u32[]{:S(2)}) collective-permute-start(bf16[816,128]{1,0:T(8,128)(2,1)S(1)} %get-tuple-element.6), channel_id=1, source_target_pairs={{0,4},{1,5},{2,6},{3,7},{4,0},{5,1},{6,2},{7,3},{8,12},{9,13},{10,... | collective-permute-start | bytes 626696 | tf_op jit(solution)/shard_map/ppermute | solution.py:292
  44.6 2.6 %collective-permute-start.2 = (bf16[816,128]{1,0:T(8,128)(2,1)S(1)}, bf16[816,128]{1,0:T(8,128)(2,1)S(1)}, u32[]{:S(2)}, u32[]{:S(2)}) collective-permute-start(bf16[816,128]{1,0:T(8,128)(2,1)S(1)} %get-tuple-element.6), channel_id=1, source_target_pairs={{0,2},{1,3},{2,4},{3,5},{4,6},{5,7},{6,0},{7,1},{8,10},{9,11},{10,... | collective-permute-start | bytes 626696 | tf_op jit(solution)/shard_map/ppermute | solution.py:292
  47.2 0.0 all-to-all-done
  47.2 7.1 %all-to-all-start.1 = ((bf16[8,3,4,1536]{3,2,1,0:T(4,128)(2,1)}), bf16[8,3,4,1536]{3,2,1,0:T(4,128)(2,1)S(1)}, u32[]{:S(2)}, u32[]{:S(2)}) async-start(bf16[8,3,4,1536]{3,2,1,0:T(4,128)(2,1)} %all-to-all-done), calls=%async_computation.1 | async-start | bytes 589824 | tf_op jit(solution)/shard_map/all_to_all | solution.py:281
  54.3 0.1 copy.6.refs_1_
  54.4 0.0 collective-permute-done.4
  54.4 0.0 collective-permute-done.3
  54.4 0.0 collective-permute-done.2
  54.4 0.1 pad_maximum_fusion.refs_3_
  54.5 5.3 %collective-permute-start.5 = (bf16[4,816,128]{2,1,0:T(8,128)(2,1)S(1)}, bf16[4,816,128]{2,1,0:T(8,128)(2,1)S(1)}, u32[]{:S(2)}, u32[]{:S(2)}) collective-permute-start(bf16[4,816,128]{2,1,0:T(8,128)(2,1)S(1)} %pad_maximum_fusion.refs_3_), channel_id=1, source_target_pairs={{0,1},{1,0},{2,3},{3,2},{4,5},{5,4},{6,7},{7,6},{8,9},{9,8},{10,11... | collective-permute-start | bytes 2506760 | tf_op jit(solution)/shard_map/ppermute | solution.py:295
  59.8 1.3 %all-to-all-done.1.refs_2_ = bf16[8,3,4,1536]{3,2,1,0:T(4,128)(2,1)S(1)} async-done(((bf16[8,3,4,1536]{3,2,1,0:T(4,128)(2,1)}), bf16[8,3,4,1536]{3,2,1,0:T(4,128)(2,1)S(1)}, u32[]{:S(2)}, u32[]{:S(2)}) %all-to-all-start.1) | async-done | bytes 294944 | tf_op jit(solution)/shard_map/all_to_all | solution.py:281
  61.1 8.1 %shard_map.37.refs_4_ = f32[9,64,128]{2,1,0:T(8,128)S(1)} custom-call(s32[4]{0:T(128)S(1)} %broadcast_add_fusion.refs_0_, s32[8,3]{1,0:T(8,128)S(1)} %copy.6.refs_1_, bf16[8,3,4,1536]{3,2,1,0:T(4,128)(2,1)S(1)} %all-to-all-done.1.refs_2_, bf16[4,816,128]{2,1,0:T(8,128)(2,1)S(1)} %pad_maximum_fusion.refs_3_), custom_call_target="tpu_custom_call" | custom-call | flops 15032385536 | bytes 557056 | tf_op jit(solution)/shard_map/pallas_call | solution.py:214
  69.2 0.0 collective-permute-done.5.refs_3_
  69.2 8.2 %shard_map.38 = f32[8,8,1024]{2,1,0:T(8,128)S(1)} custom-call(s32[4]{0:T(128)S(1)} %add_subtract_fusion.refs_0_, s32[8,3]{1,0:T(8,128)S(1)} %copy.6.refs_1_, bf16[8,3,4,1536]{3,2,1,0:T(4,128)(2,1)S(1)} %all-to-all-done.1.refs_2_, bf16[4,816,128]{2,1,0:T(8,128)(2,1)S(1)} %collective-permute-done.5.refs_3_, f32[9,64,128]{2,1,0:T(8,128)S(1)} %shard_map.37.refs_4_), custom_call_target="tpu_custom_call" | custom-call | flops 15032385536 | bytes 557056 | tf_op jit(solution)/shard_map/pallas_call | solution.py:214
  77.4 10.8 %all_to_all.15 = f32[8,8,1024]{2,1,0:T(8,128)S(1)} all-to-all(f32[8,8,1024]{2,1,0:T(8,128)S(1)} %shard_map.38), channel_id=1, replica_groups={{0,8,16,24,32,40,48,56},{64,72,80,88,96,104,112,120},{128,136,144,152,1..., dimensions={0} | all-to-all | bytes 524288 | tf_op jit(solution)/shard_map/all_to_all | solution.py:302
  88.2 0.7 copy.8
  (14 shorter events, 0.2 us)
Async XLA Ops:
  0.0 33.6 %copy-start = (s32[512,3]{0,1:T(4,128)S(1)}, s32[512,3]{0,1:T(4,128)}, u32[]{:S(2)}) copy-start(s32[512,3]{0,1:T(4,128)} %param.5) | copy-start | bytes 18436
  0.0 20.0 %collective-permute-start = (bf16[3,4,1024]{2,1,0:T(4,128)(2,1)}, bf16[3,4,1024]{2,1,0:T(4,128)(2,1)S(1)}, u32[]{:S(2)}, u32[]{:S(2)}) collective-permute-start(bf16[3,4,1024]{2,1,0:T(4,128)(2,1)} %param.3), channel_id=1, source_target_pairs={{32,0},{40,8},{48,16},{56,24},{64,32},{72,40},{80,48},{88,56},{96,... | collective-permute-start | bytes 73736 | tf_op jit(solution)/shard_map/ppermute | solution.py:268
  3.0 44.2 %all-to-all-start = ((bf16[8,3,4,1536]{3,2,1,0:T(4,128)(2,1)}), bf16[8,3,4,1536]{3,2,1,0:T(4,128)(2,1)}, u32[]{:S(2)}, u32[]{:S(2)}) async-start(bf16[8,3,4,1536]{3,2,1,0:T(4,128)(2,1)} %broadcast_in_dim.8), calls=%async_computation | async-start | bytes 589824 | tf_op jit(solution)/shard_map/all_to_all | solution.py:248
  19.2 0.7 copy-start.1
  30.5 7.0 %collective-permute-start.1 = (bf16[432,128]{1,0:T(8,128)(2,1)S(1)}, bf16[432,128]{1,0:T(8,128)(2,1)S(1)}, u32[]{:S(2)}, u32[]{:S(2)}) collective-permute-start(bf16[432,128]{1,0:T(8,128)(2,1)S(1)} %pad_maximum_fusion.3), channel_id=1, source_target_pairs={{0,32},{8,40},{16,48},{24,56},{32,0},{40,8},{48,16},{56,24},{64,96... | collective-permute-start | bytes 331784 | tf_op jit(solution)/shard_map/ppermute | solution.py:274
  37.7 16.7 %collective-permute-start.4 = (bf16[816,128]{1,0:T(8,128)(2,1)S(1)}, bf16[816,128]{1,0:T(8,128)(2,1)S(1)}, u32[]{:S(2)}, u32[]{:S(2)}) collective-permute-start(bf16[816,128]{1,0:T(8,128)(2,1)S(1)} %get-tuple-element.6), channel_id=1, source_target_pairs={{0,6},{1,7},{2,0},{3,1},{4,2},{5,3},{6,4},{7,5},{8,14},{9,15},{10,... | collective-permute-start | bytes 626696 | tf_op jit(solution)/shard_map/ppermute | solution.py:292
  42.3 12.1 %collective-permute-start.3 = (bf16[816,128]{1,0:T(8,128)(2,1)S(1)}, bf16[816,128]{1,0:T(8,128)(2,1)S(1)}, u32[]{:S(2)}, u32[]{:S(2)}) collective-permute-start(bf16[816,128]{1,0:T(8,128)(2,1)S(1)} %get-tuple-element.6), channel_id=1, source_target_pairs={{0,4},{1,5},{2,6},{3,7},{4,0},{5,1},{6,2},{7,3},{8,12},{9,13},{10,... | collective-permute-start | bytes 626696 | tf_op jit(solution)/shard_map/ppermute | solution.py:292
  44.6 9.8 %collective-permute-start.2 = (bf16[816,128]{1,0:T(8,128)(2,1)S(1)}, bf16[816,128]{1,0:T(8,128)(2,1)S(1)}, u32[]{:S(2)}, u32[]{:S(2)}) collective-permute-start(bf16[816,128]{1,0:T(8,128)(2,1)S(1)} %get-tuple-element.6), channel_id=1, source_target_pairs={{0,2},{1,3},{2,4},{3,5},{4,6},{5,7},{6,0},{7,1},{8,10},{9,11},{10,... | collective-permute-start | bytes 626696 | tf_op jit(solution)/shard_map/ppermute | solution.py:292
  47.2 13.9 %all-to-all-start.1 = ((bf16[8,3,4,1536]{3,2,1,0:T(4,128)(2,1)}), bf16[8,3,4,1536]{3,2,1,0:T(4,128)(2,1)S(1)}, u32[]{:S(2)}, u32[]{:S(2)}) async-start(bf16[8,3,4,1536]{3,2,1,0:T(4,128)(2,1)} %all-to-all-done), calls=%async_computation.1 | async-start | bytes 589824 | tf_op jit(solution)/shard_map/all_to_all | solution.py:281
  54.5 14.7 %collective-permute-start.5 = (bf16[4,816,128]{2,1,0:T(8,128)(2,1)S(1)}, bf16[4,816,128]{2,1,0:T(8,128)(2,1)S(1)}, u32[]{:S(2)}, u32[]{:S(2)}) collective-permute-start(bf16[4,816,128]{2,1,0:T(8,128)(2,1)S(1)} %pad_maximum_fusion.refs_3_), channel_id=1, source_target_pairs={{0,1},{1,0},{2,3},{3,2},{4,5},{5,4},{6,7},{7,6},{8,9},{9,8},{10,11... | collective-permute-start | bytes 2506760 | tf_op jit(solution)/shard_map/ppermute | solution.py:295

commit v16 on v12

--- a/solution.py
+++ b/solution.py
@@ -286,13 +286,14 @@
     n_y = n_sta // cores
     y, core = s // cores, lax.rem(s, cores)
     pieces = [mine]
-    for k in range(1, n_y):
+    turns = [0, 1, 3, 2]
+    for k in turns[1:]:
         pairs = [(t, (t + k * cores) % n_sta) for t in range(n_sta)]
         pieces.append(lax.ppermute(mine, "sta", pairs))
     swap = [(t, t ^ 1) for t in range(n_sta)]
     pieces = jnp.stack(pieces)
     others = lax.ppermute(pieces, "sta", swap)
-    rows_of_y = lax.rem(y - jnp.arange(n_y, dtype=jnp.int32) + n_y, n_y) * cores
+    rows_of_y = lax.rem(y - jnp.array(turns, jnp.int32) + n_y, n_y) * cores
     factor = math.sqrt(channels * L / (spread * stations))
     total = detect(rows_of_y + core, groups, block, pieces, None, own.shape[0], n_b, None)
     other = rows_of_y + 1 - core

time: 89.7 us -> 90.3 us (level)
  no operation moved by 1% of the time
where the time goes in v16:
time: 90.3 us; the launch traced here: 88.6 us
  starting transfers between devices  40.5 us (45%)
  blocking collectives  19.7 us (22%)
  Pallas kernels  16.1 us (18%)
  waiting for transfers between devices  8.04 us (9%)
  local copies, waits for them, and re-layouts  3.15 us (3%)
  other arithmetic  0.92 us (1%)
    pallas_call x2, Pallas kernels, detect(): pl.pallas_call(body, out_shape=out_shape, in_specs=[pl.BlockSpec(memory_s...  16.1 us
    all_to_all x1, starting transfers between devices, copies_to(): lax.all_to_all(spread, axis, 0, 0, axis_index_groups=groups, tiled=True)  15.8 us
    ppermute x3, starting transfers between devices, on_device(): pieces.append(lax.ppermute(mine, 'sta', pairs))  10.1 us
    all_to_all x1, blocking collectives, on_device(): lax.all_to_all(total, 'tm', 0, 0, axis_index_groups=near, tiled=True)  9.91 us
    all_gather x1, blocking collectives, on_device(): lax.all_gather(record.reshape(lines * steps, LANES), 'tm', axis_index_gro...  9.82 us
    all_to_all x1, starting transfers between devices, on_device(): lax.all_to_all(jnp.concatenate([block, tail], axis=1), 'sta', 0, 0, tiled...  7.12 us
    all_to_all x1, waiting for transfers between devices, on_device(): lax.all_to_all(jnp.concatenate([block, tail], axis=1), 'sta', 0, 0, tiled...  4.52 us
    ppermute x1, waiting for transfers between devices, on_device(): other = lax.ppermute(same, 'tm', [(i, i ^ half) for i in range(n_tm)])  3.5 us
  transfers between devices with their start and end apart: 8, of which 2 were waited for; matrix products, arithmetic and copies ran while one was open for 1% of the time, Pallas kernels for 9%

profile of v16, /device:TPU:1, one launch (start us, length us, event | category | flops | bytes accessed | tf_op | source)
XLA Modules:
  0.0 88.6 jit_solution(10446646361190369501)
XLA Ops:
  0.0 0.0 copy-start
  0.0 0.8 broadcast_in_dim.14
  0.8 0.7 broadcast_in_dim.15
  1.5 0.0 copy-start.1
  1.6 15.8 %all-to-all-start = ((bf16[8,144,128]{2,1,0:T(8,128)(2,1)}), bf16[8,144,128]{2,1,0:T(8,128)(2,1)S(1)}, u32[]{:S(2)}, u32[]{:S(2)}) async-start(bf16[8,144,128]{2,1,0:T(8,128)(2,1)} %broadcast_in_dim.15), calls=%async_computation | async-start | bytes 589824 | tf_op jit(solution)/shard_map/all_to_all | solution.py:252
  17.3 0.0 copy-done.1
  17.4 9.8 %all_gather.3 = bf16[4,96,128]{2,1,0:T(8,128)(2,1)S(1)} all-gather(bf16[1,96,128]{2,1,0:T(8,128)(2,1)S(1)} %all_gather_reshape.3), channel_id=1, replica_groups={{0,8,16,24},{32,40,48,56},{64,72,80,88},{96,104,112,120},{128,136,144,1..., dimensions={0}, use_global_device_ids=true | all-gather | bytes 122880 | tf_op jit(solution)/shard_map/all_gather | solution.py:272
  27.2 2.8 %collective-permute-start = (bf16[4,96,128]{2,1,0:T(8,128)(2,1)S(1)}, bf16[4,96,128]{2,1,0:T(8,128)(2,1)S(1)}, u32[]{:S(2)}, u32[]{:S(2)}) collective-permute-start(bf16[4,96,128]{2,1,0:T(8,128)(2,1)S(1)} %all_gather.3), channel_id=1, source_target_pairs={{0,32},{8,40},{16,48},{24,56},{32,0},{40,8},{48,16},{56,24},{64,96... | collective-permute-start | bytes 294920 | tf_op jit(solution)/shard_map/ppermute | solution.py:273
  30.0 0.0 copy-start.2
  30.0 0.6 copy-done.2
  30.7 0.0 copy-done
  30.7 0.1 constant_dynamic-slice_fusion
  30.8 0.1 copy.12.refs_1_
  30.8 3.5 %collective-permute-done = bf16[4,96,128]{2,1,0:T(8,128)(2,1)S(1)} collective-permute-done((bf16[4,96,128]{2,1,0:T(8,128)(2,1)S(1)}, bf16[4,96,128]{2,1,0:T(8,128)(2,1)S(1)}, u32[]{:S(2)}, u32[]{:S(2)}) %collective-permute-start) | collective-permute-done | bytes 98336 | tf_op jit(solution)/shard_map/ppermute | solution.py:273
  34.4 1.3 %collective-permute-start.1 = (bf16[12,4,128]{2,1,0:T(4,128)(2,1)S(1)}, bf16[12,4,128]{2,1,0:T(4,128)(2,1)S(1)}, u32[]{:S(2)}, u32[]{:S(2)}) collective-permute-start(bf16[12,4,128]{2,1,0:T(4,128)(2,1)S(1)} %slice.9), channel_id=1, source_target_pairs={{64,0},{72,8},{80,16},{88,24},{96,32},{104,40},{112,48},{120,56},{... | collective-permute-start | bytes 36872 | tf_op jit(solution)/shard_map/ppermute | solution.py:278
  35.8 4.8 %collective-permute-start.4 = (bf16[768,128]{1,0:T(8,128)(2,1)S(1)}, bf16[768,128]{1,0:T(8,128)(2,1)S(1)}, u32[]{:S(2)}, u32[]{:S(2)}) collective-permute-start(bf16[768,128]{1,0:T(8,128)(2,1)S(1)} %bitcast.14), channel_id=1, source_target_pairs={{0,4},{1,5},{2,6},{3,7},{4,0},{5,1},{6,2},{7,3},{8,12},{9,13},{10,... | collective-permute-start | bytes 589832 | tf_op jit(solution)/shard_map/ppermute | solution.py:292
  40.6 2.7 %collective-permute-start.3 = (bf16[768,128]{1,0:T(8,128)(2,1)S(1)}, bf16[768,128]{1,0:T(8,128)(2,1)S(1)}, u32[]{:S(2)}, u32[]{:S(2)}) collective-permute-start(bf16[768,128]{1,0:T(8,128)(2,1)S(1)} %bitcast.15), channel_id=1, source_target_pairs={{0,6},{1,7},{2,0},{3,1},{4,2},{5,3},{6,4},{7,5},{8,14},{9,15},{10,... | collective-permute-start | bytes 589832 | tf_op jit(solution)/shard_map/ppermute | solution.py:292
  43.3 2.6 %collective-permute-start.2 = (bf16[768,128]{1,0:T(8,128)(2,1)S(1)}, bf16[768,128]{1,0:T(8,128)(2,1)S(1)}, u32[]{:S(2)}, u32[]{:S(2)}) collective-permute-start(bf16[768,128]{1,0:T(8,128)(2,1)S(1)} %bitcast.16), channel_id=1, source_target_pairs={{0,2},{1,3},{2,4},{3,5},{4,6},{5,7},{6,0},{7,1},{8,10},{9,11},{10,... | collective-permute-start | bytes 589832 | tf_op jit(solution)/shard_map/ppermute | solution.py:292
  45.9 0.0 collective-permute-done.1
  45.9 0.0 all-to-all-done
  45.9 0.8 pad_maximum_fusion.1
  46.7 7.1 %all-to-all-start.1 = ((bf16[8,192,128]{2,1,0:T(8,128)(2,1)}), bf16[8,192,128]{2,1,0:T(8,128)(2,1)S(1)}, u32[]{:S(2)}, u32[]{:S(2)}) async-start(bf16[8,192,128]{2,1,0:T(8,128)(2,1)} %pad_maximum_fusion.1), calls=%async_computation.1 | async-start | bytes 786432 | tf_op jit(solution)/shard_map/all_to_all | solution.py:281
  53.8 0.0 collective-permute-done.4
  53.8 0.0 collective-permute-done.3
  53.8 0.0 collective-permute-done.2
  53.9 0.1 pad_maximum_fusion.refs_3_
  54.0 3.4 %collective-permute-start.5 = (bf16[4,768,128]{2,1,0:T(8,128)(2,1)S(1)}, bf16[4,768,128]{2,1,0:T(8,128)(2,1)S(1)}, u32[]{:S(2)}, u32[]{:S(2)}) collective-permute-start(bf16[4,768,128]{2,1,0:T(8,128)(2,1)S(1)} %pad_maximum_fusion.refs_3_), channel_id=1, source_target_pairs={{0,1},{1,0},{2,3},{3,2},{4,5},{5,4},{6,7},{7,6},{8,9},{9,8},{10,11... | collective-permute-start | bytes 2359304 | tf_op jit(solution)/shard_map/ppermute | solution.py:295
  57.4 4.5 %all-to-all-done.1.refs_2_ = bf16[8,192,128]{2,1,0:T(8,128)(2,1)S(1)} async-done(((bf16[8,192,128]{2,1,0:T(8,128)(2,1)}), bf16[8,192,128]{2,1,0:T(8,128)(2,1)S(1)}, u32[]{:S(2)}, u32[]{:S(2)}) %all-to-all-start.1) | async-done | bytes 393248 | tf_op jit(solution)/shard_map/all_to_all | solution.py:281
  61.9 8.0 %shard_map.46.refs_4_ = f32[9,64,128]{2,1,0:T(8,128)S(1)} custom-call(s32[4]{0:T(128)S(1)} %get-tuple-element.5.refs_0_, s32[8,3]{1,0:T(8,128)S(1)} %copy.12.refs_1_, bf16[8,192,128]{2,1,0:T(8,128)(2,1)S(1)} %all-to-all-done.1.refs_2_, bf16[4,768,128]{2,1,0:T(8,128)(2,1)S(1)} %pad_maximum_fusion.refs_3_), custom_call_target="tpu_custom_call" | custom-call | flops 15032385536 | bytes 655360 | tf_op jit(solution)/shard_map/pallas_call | solution.py:217
  69.9 0.0 collective-permute-done.5.refs_3_
  69.9 8.1 %shard_map.47 = f32[8,8,1024]{2,1,0:T(8,128)S(1)} custom-call(s32[4]{0:T(128)S(1)} %add_subtract_fusion.refs_0_, s32[8,3]{1,0:T(8,128)S(1)} %copy.12.refs_1_, bf16[8,192,128]{2,1,0:T(8,128)(2,1)S(1)} %all-to-all-done.1.refs_2_, bf16[4,768,128]{2,1,0:T(8,128)(2,1)S(1)} %collective-permute-done.5.refs_3_, f32[9,64,128]{2,1,0:T(8,128)S(1)} %shard_map.46.refs_4_), custom_call_target="tpu_custom_call" | custom-call | flops 15032385536 | bytes 655360 | tf_op jit(solution)/shard_map/pallas_call | solution.py:217
  78.0 9.9 %all_to_all.15 = f32[8,8,1024]{2,1,0:T(8,128)S(1)} all-to-all(f32[8,8,1024]{2,1,0:T(8,128)S(1)} %shard_map.47), channel_id=1, replica_groups={{0,8,16,24,32,40,48,56},{64,72,80,88,96,104,112,120},{128,136,144,152,1..., dimensions={0} | all-to-all | bytes 524288 | tf_op jit(solution)/shard_map/all_to_all | solution.py:302
  87.9 0.7 copy.14
  (9 shorter events, 0.1 us)
Async XLA Ops:
  0.0 30.7 %copy-start = (s32[512,3]{0,1:T(4,128)S(1)}, s32[512,3]{0,1:T(4,128)}, u32[]{:S(2)}) copy-start(s32[512,3]{0,1:T(4,128)} %param.6) | copy-start | bytes 18436
  1.5 15.8 %copy-start.1 = (bf16[3,4,1024]{2,1,0:T(4,128)(2,1)S(1)}, bf16[3,4,1024]{2,1,0:T(4,128)(2,1)}, u32[]{:S(2)}) copy-start(bf16[3,4,1024]{2,1,0:T(4,128)(2,1)} %param.4) | copy-start | bytes 73732
  1.6 44.4 %all-to-all-start = ((bf16[8,144,128]{2,1,0:T(8,128)(2,1)}), bf16[8,144,128]{2,1,0:T(8,128)(2,1)S(1)}, u32[]{:S(2)}, u32[]{:S(2)}) async-start(bf16[8,144,128]{2,1,0:T(8,128)(2,1)} %broadcast_in_dim.15), calls=%async_computation | async-start | bytes 589824 | tf_op jit(solution)/shard_map/all_to_all | solution.py:252
  27.2 7.2 %collective-permute-start = (bf16[4,96,128]{2,1,0:T(8,128)(2,1)S(1)}, bf16[4,96,128]{2,1,0:T(8,128)(2,1)S(1)}, u32[]{:S(2)}, u32[]{:S(2)}) collective-permute-start(bf16[4,96,128]{2,1,0:T(8,128)(2,1)S(1)} %all_gather.3), channel_id=1, source_target_pairs={{0,32},{8,40},{16,48},{24,56},{32,0},{40,8},{48,16},{56,24},{64,96... | collective-permute-start | bytes 294920 | tf_op jit(solution)/shard_map/ppermute | solution.py:273
  30.0 0.7 copy-start.2
  34.4 11.5 %collective-permute-start.1 = (bf16[12,4,128]{2,1,0:T(4,128)(2,1)S(1)}, bf16[12,4,128]{2,1,0:T(4,128)(2,1)S(1)}, u32[]{:S(2)}, u32[]{:S(2)}) collective-permute-start(bf16[12,4,128]{2,1,0:T(4,128)(2,1)S(1)} %slice.9), channel_id=1, source_target_pairs={{64,0},{72,8},{80,16},{88,24},{96,32},{104,40},{112,48},{120,56},{... | collective-permute-start | bytes 36872 | tf_op jit(solution)/shard_map/ppermute | solution.py:278
  35.8 18.1 %collective-permute-start.4 = (bf16[768,128]{1,0:T(8,128)(2,1)S(1)}, bf16[768,128]{1,0:T(8,128)(2,1)S(1)}, u32[]{:S(2)}, u32[]{:S(2)}) collective-permute-start(bf16[768,128]{1,0:T(8,128)(2,1)S(1)} %bitcast.14), channel_id=1, source_target_pairs={{0,4},{1,5},{2,6},{3,7},{4,0},{5,1},{6,2},{7,3},{8,12},{9,13},{10,... | collective-permute-start | bytes 589832 | tf_op jit(solution)/shard_map/ppermute | solution.py:292
  40.6 13.2 %collective-permute-start.3 = (bf16[768,128]{1,0:T(8,128)(2,1)S(1)}, bf16[768,128]{1,0:T(8,128)(2,1)S(1)}, u32[]{:S(2)}, u32[]{:S(2)}) collective-permute-start(bf16[768,128]{1,0:T(8,128)(2,1)S(1)} %bitcast.15), channel_id=1, source_target_pairs={{0,6},{1,7},{2,0},{3,1},{4,2},{5,3},{6,4},{7,5},{8,14},{9,15},{10,... | collective-permute-start | bytes 589832 | tf_op jit(solution)/shard_map/ppermute | solution.py:292
  43.3 10.6 %collective-permute-start.2 = (bf16[768,128]{1,0:T(8,128)(2,1)S(1)}, bf16[768,128]{1,0:T(8,128)(2,1)S(1)}, u32[]{:S(2)}, u32[]{:S(2)}) collective-permute-start(bf16[768,128]{1,0:T(8,128)(2,1)S(1)} %bitcast.16), channel_id=1, source_target_pairs={{0,2},{1,3},{2,4},{3,5},{4,6},{5,7},{6,0},{7,1},{8,10},{9,11},{10,... | collective-permute-start | bytes 589832 | tf_op jit(solution)/shard_map/ppermute | solution.py:292
  46.7 15.2 %all-to-all-start.1 = ((bf16[8,192,128]{2,1,0:T(8,128)(2,1)}), bf16[8,192,128]{2,1,0:T(8,128)(2,1)S(1)}, u32[]{:S(2)}, u32[]{:S(2)}) async-start(bf16[8,192,128]{2,1,0:T(8,128)(2,1)} %pad_maximum_fusion.1), calls=%async_computation.1 | async-start | bytes 786432 | tf_op jit(solution)/shard_map/all_to_all | solution.py:281
  54.0 16.0 %collective-permute-start.5 = (bf16[4,768,128]{2,1,0:T(8,128)(2,1)S(1)}, bf16[4,768,128]{2,1,0:T(8,128)(2,1)S(1)}, u32[]{:S(2)}, u32[]{:S(2)}) collective-permute-start(bf16[4,768,128]{2,1,0:T(8,128)(2,1)S(1)} %pad_maximum_fusion.refs_3_), channel_id=1, source_target_pairs={{0,1},{1,0},{2,3},{3,2},{4,5},{5,4},{6,7},{7,6},{8,9},{9,8},{10,11... | collective-permute-start | bytes 2359304 | tf_op jit(solution)/shard_map/ppermute | solution.py:295
